TPU v7x, 32 devices: a whole 2x2x4 slice. The times are simulated.
32 devices in a mesh: dp: 8 (over y, x, core), tensor: 4 (over z).
Axes of the slice: x: 2, y: 2, z: 4, core: 2. Of those that a mesh axis runs over, the one named last changes fastest.
Arguments:
- images: bfloat16 [24, 729, 1152], P('dp'), may hold values from -6 to 6
- counts: int32 [8], P('dp'), may hold values from 2 to 3, as said below
- cotangent: bfloat16 [24, 729, 1152], P('dp'), may hold values from -6 to 6
- query_w: bfloat16 [1152, 1152], P(None, 'tensor'), may hold values from -0.1875 to 0.1875
- query_b: float32 [1152], P('tensor'), may hold values from -3 to 3
- key_w: bfloat16 [1152, 1152], P(None, 'tensor'), may hold values from -0.1875 to 0.1875
- value_w: bfloat16 [1152, 1152], P(None, 'tensor'), may hold values from -0.1875 to 0.1875
- value_b: float32 [1152], P('tensor'), may hold values from -0.3 to 0.3
- out_w: bfloat16 [1152, 1152], P('tensor'), may hold values from -3 to 3
- out_b: float32 [1152], replicated, may hold values from -3 to 3
- norm1_gain: float32 [1152], replicated, may hold values from 0.25 to 1.75
- norm1_shift: float32 [1152], replicated, may hold values from -0.3 to 0.3
- norm2_gain: float32 [1152], replicated, may hold values from 0.25 to 1.75
- norm2_shift: float32 [1152], replicated, may hold values from -2 to 2
- expand_w: bfloat16 [1152, 4304], P(None, 'tensor'), may hold values from -0.1875 to 0.1875
- expand_b: float32 [4304], P('tensor'), may hold values from -3 to 3
- shrink_w: bfloat16 [4304, 1152], P('tensor'), may hold values from -0.09375 to 0.09375
- shrink_b: float32 [1152], replicated, may hold values from -3 to 3
Outputs:
- output: bfloat16 [24, 729, 1152], P('dp')
- input_grad: float32 [24, 729, 1152], P('dp')
- grad_query_w: float32 [1152, 1152], P('dp', 'tensor')
- grad_query_b: float32 [1152], P('tensor')
- grad_key_w: float32 [1152, 1152], P('dp', 'tensor')
- grad_value_w: float32 [1152, 1152], P('dp', 'tensor')
- grad_value_b: float32 [1152], P('tensor')
- grad_out_w: float32 [1152, 1152], P('tensor', 'dp')
- grad_out_b: float32 [1152], replicated
- grad_norm1_gain: float32 [1152], replicated
- grad_norm1_shift: float32 [1152], replicated
- grad_norm2_gain: float32 [1152], replicated
- grad_norm2_shift: float32 [1152], replicated
- grad_expand_w: float32 [1152, 4304], P('dp', 'tensor')
- grad_expand_b: float32 [4304], P('tensor')
- grad_shrink_w: float32 [4304, 1152], P('tensor', 'dp')
- grad_shrink_b: float32 [1152], replicated
- clipped_query_w: bfloat16 [1152, 1152], P(None, 'tensor')
- clipped_key_w: bfloat16 [1152, 1152], P(None, 'tensor')
Inputs may be any that keep to these rules, and one draw needn't show every extreme that they name: Each dp index holds 3 image slots, the first counts of them live; in every draw some index has 3 live slots and another 3 - 1.
All inputs are finite; a program needn't handle non-finite values.
Results may differ from a plain program's by a relative error of at most 0.02.
Values may be sent and summed in bfloat16 or wider, within the bound.
A program may use at most 192 MiB of HBM per device.

v0:
```python
import math

import jax
import jax.numpy as jnp
from jax import lax
from jax.sharding import PartitionSpec as P

HD = 72


norm_eps = 1e-06
clip_limit = 3.0
tanh_coef = 0.7978845608028654
cube_coef = 0.044715


def matmul(left_side, right_side):
    return jnp.dot(left_side, right_side, preferred_element_type=jnp.float32)


def matmul_nt(left_side, right_side):
    return lax.dot_general(
        left_side, right_side, (((1,), (1,)), ((), ())), preferred_element_type=jnp.float32
    )


def matmul_tn(left_side, right_side):
    return lax.dot_general(
        left_side, right_side, (((0,), (0,)), ((), ())), preferred_element_type=jnp.float32
    )


def normalize(values):
    centre = jnp.mean(values, axis=-1, keepdims=True)
    centred = values - centre
    spread = jnp.mean(centred * centred, axis=-1, keepdims=True)
    inverse = lax.rsqrt(spread + norm_eps)
    return (centred * inverse, inverse)


def norm_back(grad_norm, normed, inverse, gain):
    scaled = grad_norm * gain
    first_mean = jnp.mean(scaled, axis=-1, keepdims=True)
    second_mean = jnp.mean(scaled * normed, axis=-1, keepdims=True)
    grad_input = inverse * (scaled - first_mean - normed * second_mean)
    return (grad_input, jnp.sum(grad_norm * normed, axis=0), jnp.sum(grad_norm, axis=0))


def gelu_value(pre_act):
    return (
        0.5
        * pre_act
        * (1.0 + jnp.tanh(tanh_coef * (pre_act + cube_coef * pre_act * pre_act * pre_act)))
    )


def gelu_slope(pre_act):
    tangent = jnp.tanh(tanh_coef * (pre_act + cube_coef * pre_act * pre_act * pre_act))
    return 0.5 * (1.0 + tangent) + 0.5 * pre_act * (1.0 - tangent * tangent) * tanh_coef * (
        1.0 + 3.0 * cube_coef * pre_act * pre_act
    )


def shards(
    images,
    counts,
    cotangent,
    query_w,
    query_b,
    key_w,
    value_w,
    value_b,
    out_w,
    out_b,
    norm1_gain,
    norm1_shift,
    norm2_gain,
    norm2_shift,
    expand_w,
    expand_b,
    shrink_w,
    shrink_b,
):
    slot_count, length, model_width = images.shape
    tokens = slot_count * length
    local_width = query_w.shape[1]
    head_count = local_width // HD
    score_scale = 1.0 / math.sqrt(HD)
    live_slots = (jnp.arange(slot_count, dtype=jnp.int32) < counts[0]).astype(jnp.float32)
    live_rows = jnp.repeat(live_slots, length)[:, None]
    residual = images.reshape(tokens, model_width).astype(jnp.float32)
    grad_out = cotangent.reshape(tokens, model_width).astype(jnp.float32) * live_rows
    normed1, inverse1 = normalize(residual)
    first_part = (normed1 * norm1_gain + norm1_shift).astype(jnp.bfloat16)
    queries = (matmul(first_part, query_w) + query_b).astype(jnp.bfloat16)
    key_rows = matmul(first_part, key_w).astype(jnp.bfloat16)
    value_rows = (matmul(first_part, value_w) + value_b).astype(jnp.bfloat16)
    per_head = (slot_count, length, head_count, HD)
    query_heads = queries.reshape(per_head)
    key_heads = key_rows.reshape(per_head)
    value_heads = value_rows.reshape(per_head)

    def attend(slot_block):
        query_blk, key_blk, value_blk = slot_block
        scores = (
            jnp.einsum("qhc,khc->hqk", query_blk, key_blk, preferred_element_type=jnp.float32)
            * score_scale
        )
        row_top = jnp.max(scores, axis=-1, keepdims=True)
        exponent = jnp.exp(scores - row_top)
        row_total = jnp.sum(exponent, axis=-1, keepdims=True)
        attn_prob = (exponent / row_total).astype(jnp.bfloat16)
        mixture = jnp.einsum(
            "hqk,khc->qhc", attn_prob, value_blk, preferred_element_type=jnp.float32
        )
        log_total = (row_top + jnp.log(row_total))[..., 0]
        return (mixture.astype(jnp.bfloat16), log_total, jnp.max(row_top, axis=(1, 2)))

    attended, log_totals, head_tops = lax.map(attend, (query_heads, key_heads, value_heads))
    masked_tops = jnp.where(live_slots[:, None] > 0.0, head_tops, -1e30)
    logit_top = lax.pmax(jnp.max(masked_tops, axis=0), "dp")
    attended_flat = attended.reshape(tokens, local_width)
    attn_term = matmul(attended_flat, out_w)
    attn_part = lax.psum(attn_term.astype(jnp.bfloat16), "tensor").astype(jnp.float32)
    midway = residual + attn_part + out_b
    normed2, inverse2 = normalize(midway)
    second_part = (normed2 * norm2_gain + norm2_shift).astype(jnp.bfloat16)
    pre_act = matmul(second_part, expand_w) + expand_b
    activated = gelu_value(pre_act).astype(jnp.bfloat16)
    mlp_term = matmul(activated, shrink_w)
    mlp_part = lax.psum(mlp_term.astype(jnp.bfloat16), "tensor").astype(jnp.float32)
    output_part = ((midway + mlp_part + shrink_b) * live_rows).astype(jnp.bfloat16)
    grad_out_low = grad_out.astype(jnp.bfloat16)
    grad_shrink_b = jnp.sum(grad_out, axis=0)
    grad_shrink_w = matmul_tn(activated, grad_out_low)
    grad_pre = matmul_nt(grad_out_low, shrink_w) * gelu_slope(pre_act)
    grad_expand_b = jnp.sum(grad_pre, axis=0)
    grad_pre_low = grad_pre.astype(jnp.bfloat16)
    grad_expand_w = matmul_tn(second_part, grad_pre_low)
    second_term = matmul_nt(grad_pre_low, expand_w)
    grad_second = lax.psum(second_term.astype(jnp.bfloat16), "tensor").astype(jnp.float32)
    back_second, grad_norm2_gain, grad_norm2_shift = norm_back(
        grad_second, normed2, inverse2, norm2_gain
    )
    grad_mid = grad_out + back_second
    grad_out_b = jnp.sum(grad_mid, axis=0)
    grad_mid_part = grad_mid.astype(jnp.bfloat16)
    output = output_part.reshape(images.shape)
    grad_out_w = matmul_tn(attended_flat, grad_mid_part)
    grad_attended = matmul_nt(grad_mid_part, out_w).astype(jnp.bfloat16).reshape(per_head)

    def attend_back(slot_block):
        query_blk, key_blk, value_blk, grad_blk, log_blk = slot_block
        scores = (
            jnp.einsum("qhc,khc->hqk", query_blk, key_blk, preferred_element_type=jnp.float32)
            * score_scale
        )
        attn_prob = jnp.exp(scores - log_blk[..., None])
        grad_prob = jnp.einsum(
            "qhc,khc->hqk", grad_blk, value_blk, preferred_element_type=jnp.float32
        )
        row_dot = jnp.sum(grad_prob * attn_prob, axis=-1, keepdims=True)
        grad_scores = (attn_prob * (grad_prob - row_dot)).astype(jnp.bfloat16)
        grad_value = jnp.einsum(
            "hqk,qhc->khc",
            attn_prob.astype(jnp.bfloat16),
            grad_blk,
            preferred_element_type=jnp.float32,
        )
        grad_query = (
            jnp.einsum("hqk,khc->qhc", grad_scores, key_blk, preferred_element_type=jnp.float32)
            * score_scale
        )
        grad_key = (
            jnp.einsum("hqk,qhc->khc", grad_scores, query_blk, preferred_element_type=jnp.float32)
            * score_scale
        )
        return (grad_query, grad_key, grad_value)

    grad_queries, grad_keys, grad_values = lax.map(
        attend_back, (query_heads, key_heads, value_heads, grad_attended, log_totals)
    )
    grad_queries = grad_queries.reshape(tokens, local_width)
    grad_keys = grad_keys.reshape(tokens, local_width)
    grad_values = grad_values.reshape(tokens, local_width)
    grad_query_b = jnp.sum(grad_queries, axis=0)
    grad_value_b = jnp.sum(grad_values, axis=0)
    query_low = grad_queries.astype(jnp.bfloat16)
    key_low = grad_keys.astype(jnp.bfloat16)
    value_low = grad_values.astype(jnp.bfloat16)
    grad_query_w = matmul_tn(first_part, query_low)
    grad_key_w = matmul_tn(first_part, key_low)
    grad_value_w = matmul_tn(first_part, value_low)
    first_term = (
        matmul_nt(query_low, query_w) + matmul_nt(key_low, key_w) + matmul_nt(value_low, value_w)
    )
    grad_first = lax.psum(first_term.astype(jnp.bfloat16), "tensor").astype(jnp.float32)
    back_first, grad_norm1_gain, grad_norm1_shift = norm_back(
        grad_first, normed1, inverse1, norm1_gain
    )
    input_part = (grad_mid + back_first) * live_rows
    input_grad = input_part.reshape(images.shape)
    summed = lax.psum(
        (
            grad_query_b,
            grad_value_b,
            grad_expand_b,
            grad_out_b,
            grad_shrink_b,
            grad_norm1_gain,
            grad_norm1_shift,
            grad_norm2_gain,
            grad_norm2_shift,
        ),
        "dp",
    )
    grad_query_w, grad_key_w, grad_value_w, grad_expand_w = (
        lax.psum_scatter(
            grad_query_w.astype(jnp.bfloat16), "dp", scatter_dimension=0, tiled=True
        ).astype(jnp.float32),
        lax.psum_scatter(
            grad_key_w.astype(jnp.bfloat16), "dp", scatter_dimension=0, tiled=True
        ).astype(jnp.float32),
        lax.psum_scatter(
            grad_value_w.astype(jnp.bfloat16), "dp", scatter_dimension=0, tiled=True
        ).astype(jnp.float32),
        lax.psum_scatter(
            grad_expand_w.astype(jnp.bfloat16), "dp", scatter_dimension=0, tiled=True
        ).astype(jnp.float32),
    )
    grad_out_w, grad_shrink_w = (
        lax.psum_scatter(
            grad_out_w.astype(jnp.bfloat16), "dp", scatter_dimension=1, tiled=True
        ).astype(jnp.float32),
        lax.psum_scatter(
            grad_shrink_w.astype(jnp.bfloat16), "dp", scatter_dimension=1, tiled=True
        ).astype(jnp.float32),
    )
    factor = jnp.sqrt(clip_limit / jnp.maximum(logit_top, clip_limit))
    column_factor = jnp.repeat(factor, HD)
    clipped_query = (query_w.astype(jnp.float32) * column_factor).astype(jnp.bfloat16)
    clipped_key = (key_w.astype(jnp.float32) * column_factor).astype(jnp.bfloat16)
    return (
        output,
        input_grad,
        grad_query_w,
        summed[0],
        grad_key_w,
        grad_value_w,
        summed[1],
        grad_out_w,
        summed[3],
        summed[5],
        summed[6],
        summed[7],
        summed[8],
        grad_expand_w,
        summed[2],
        grad_shrink_w,
        summed[4],
        clipped_query,
        clipped_key,
    )


def solution(mesh):
    placed = (
        P("dp", None, None),
        P("dp"),
        P("dp", None, None),
        P(None, "tensor"),
        P("tensor"),
        P(None, "tensor"),
        P(None, "tensor"),
        P("tensor"),
        P("tensor", None),
        P(),
        P(),
        P(),
        P(),
        P(),
        P(None, "tensor"),
        P("tensor"),
        P("tensor", None),
        P(),
    )
    return jax.shard_map(
        shards,
        mesh=mesh,
        in_specs=placed,
        out_specs=(
            P("dp", None, None),
            P("dp", None, None),
            P("dp", "tensor"),
            P("tensor"),
            P("dp", "tensor"),
            P("dp", "tensor"),
            P("tensor"),
            P("tensor", "dp"),
            P(),
            P(),
            P(),
            P(),
            P(),
            P("dp", "tensor"),
            P("tensor"),
            P("tensor", "dp"),
            P(),
            P(None, "tensor"),
            P(None, "tensor"),
        ),
        check_vma=False,
    )
```

profile of v0, /device:TPU:1, one launch (start us, length us, event | category | flops | bytes accessed | tf_op | source)
XLA Modules:
  0.0 1249.7 jit_solution(17047455783183330821)
XLA Ops:
  14.7 7.5 reshape.249
  22.3 5.4 add_convert_fusion.2
  33.1 5.3 reshape.244
  41.1 5.7 fusion.75
  46.8 5.3 reshape.242
  54.8 5.4 fusion.76
  60.2 5.3 reshape.243
  68.2 33.1 %while.28 = (s32[]{:T(128)}, bf16[3,729,4,72]{1,3,2,0:T(8,128)(2,1)}, f32[3,4,729]{2,1,0:T(4,128)}, f32[3,4]{1,0:T(4,128)}, bf16[3,729,4,72]{1,3,2,0:T(8,128)(2,...) while((s32[]{:T(128)}, ...), condition=%wide.region_6.7_spmd, body=%wide.region_2.6_spmd.sunk | while | flops 633684736 | bytes 27374780 | solution.py:119
  109.7 6.7 convolution_convert_fusion.2
  117.6 7.7 reshape.250
  125.3 176.4 %all-reduce.6.cloned.1.call-done = bf16[2187,1152]{1,0:T(8,128)(2,1)} async-done(((bf16[2187,1152]{1,0:T(8,128)(2,1)}), bf16[2187,1152]{1,0:T(8,128)(2,1)}) %all-reduce.6.cloned.1.call-update) | async-done | bytes 5038864 | tf_op jit(solution)/shard_map/psum | solution.py:124
  301.7 10.5 fusion.83
  312.2 5.2 multiply_reduce_fusion.5
  319.0 11.7 convolution_add_fusion.2
  330.7 15.3 %fusion.86 = (f32[1076]{0:T(1024)}, bf16[2187,1076]{0,1:T(8,128)(2,1)}) fusion(f32[2187,1076]{0,1:T(8,128)} %convolution_add_fusion.2, bf16[1076,1152]{1,0:T(8,128)(2,1)S(1)} %copy-done, f32[2187,1152]{1,0:T(8,128)S(1)} %bitcast.152, f32[2187]{0:T(1024)S(1)} %mul.238), kind=kOutput, calls=%fused_computation.143 | convolution fusion | flops 5473901568 | bytes 26689124 | tf_op jit(solution)/shard_map/dot_general | solution.py:22
  346.1 11.1 convolution_convert_fusion
  357.7 16.7 %convolution_convert_fusion.3 = bf16[1076,1152]{0,1:T(8,128)(2,1)} fusion(f32[2187,1152]{1,0:T(8,128)} %reshape.250, f32[2187]{0:T(1024)S(1)} %mul.238, f32[2187,1076]{0,1:T(8,128)} %convolution_add_fusion.2), kind=kOutput, calls=%fused_computation.109 | convolution fusion | flops 5449257984 | bytes 21978396 | tf_op jit(solution)/shard_map/dot_general | solution.py:28
  374.8 6.7 add_convert_fusion
  381.5 5.8 convert_element_type.209
  387.3 14.8 %convolution_convert_fusion.4 = bf16[1152,1076]{1,0:T(8,128)(2,1)} fusion(bf16[2187,1076]{0,1:T(8,128)(2,1)} %get-tuple-element.215, f32[2187,1152]{1,0:T(8,128)} %get-tuple-element.201, f32[1152]{0:T(1024)S(1)} %copy-done.42, f32[1152]{0:T(1024)S(1)} %copy-done.32, f32[2187]{0:T(1024)S(1)} %add_rsqrt_fusion, f32[2187]{0:T(1024)S(1)} %broadcast_multiply_fusion.4), kind=kOutput, calls=%fused_computation.110 | convolution fusion | flops 5435637248 | bytes 17289936 | tf_op jit(solution)/shard_map/dot_general | solution.py:28
  402.2 137.2 %all-reduce.8.cloned.1.call-done = bf16[2187,1152]{1,0:T(8,128)(2,1)} async-done(((bf16[2187,1152]{1,0:T(8,128)(2,1)}), bf16[2187,1152]{1,0:T(8,128)(2,1)}) %all-reduce.8.cloned.1.call-update) | async-done | bytes 5038864 | tf_op jit(solution)/shard_map/psum | solution.py:141
  539.4 9.2 fusion.68
  548.6 10.3 fusion.81
  565.7 5.3 reshape.247
  573.7 95.7 %while.29 = (s32[]{:T(128)}, f32[3,729,4,72]{1,3,2,0:T(8,128)}, bf16[3,729,4,72]{1,3,2,0:T(8,128)(2,1)}, f32[3,729,4,72]{1,3,2,0:T(8,128)}, bf16[3,729,4,72]{1,3...) while((s32[]{:T(128)}, f32[3,729,4,72]{1,3,2,0:T(8,128)}, ...), condition=%wide.region_16.17_spmd, body=%wide.region_14.16_spmd.sunk | while | flops 1556476160 | bytes 110285696 | solution.py:180
  580.6 6.1 multiply_reduce_fusion.11
  586.7 10.2 multiply_convert_fusion.11
  612.7 6.1 multiply_reduce_fusion.11
  618.7 10.3 multiply_convert_fusion.11
  644.4 5.9 multiply_reduce_fusion.11
  650.3 10.2 multiply_convert_fusion.11
  669.4 8.2 convolution_convert_fusion.7
  677.9 5.7 fusion.84
  690.7 6.8 convolution_convert_fusion.8
  697.6 12.6 %convolution_convert_fusion.1 = bf16[2187,1152]{1,0:T(8,128)(2,1)} fusion(bf16[1076,1152]{1,0:T(8,128)(2,1)S(1)} %copy-done, f32[2187,1076]{0,1:T(8,128)} %convolution_add_fusion.2), kind=kOutput, calls=%fused_computation.78 | convolution fusion | flops 5445498880 | bytes 16930800 | tf_op jit(solution)/shard_map/dot_general | solution.py:18
  725.9 6.8 convolution_convert_fusion.10
  733.3 8.4 fusion.87
  741.6 6.3 convolution_convert_fusion.9
  748.1 8.0 convolution_add_fusion.1
  756.1 5.5 fusion.58
  762.4 11.9 pmax.7
  790.3 37.1 %reduce-scatter.9.cloned.1.call-done = bf16[144,288]{1,0:T(8,128)(2,1)} async-done(((bf16[1152,288]{1,0:T(8,128)(2,1)}), bf16[144,288]{1,0:T(8,128)(2,1)}) %reduce-scatter.9.cloned.1.call-update) | async-done | bytes 82960 | tf_op jit(solution)/shard_map/reduce_scatter | solution.py:221
  829.0 349.1 %all-reduce.10.cloned.1.call-done = (bf16[2187,1152]{1,0:T(8,128)(2,1)}, bf16[2187,1152]{1,0:T(8,128)(2,1)}) async-done(((bf16[2187,1152]{1,0:T(8,128)(2,1)}, bf16[2187,1152]{1,0:T(8,128)(2,1)}), (bf16[2187,1152]{1,0:T(8,128)(2,1)}, bf16[2187,1152]{1,0:T(8,128)(2,1)})) %all-reduce.10.cloned.1.call-update) | async-done | bytes 10077712 | tf_op jit(solution)/shard_map/psum | solution.py:131
  1178.2 9.2 fusion.69
  1187.5 17.9 %fusion.62 = (f32[2187,1152]{1,0:T(8,128)}, bf16[2187,1152]{1,0:T(8,128)(2,1)}) fusion(f32[2187,1152]{1,0:T(8,128)} %copy-done.3, bf16[2187,1152]{1,0:T(8,128)(2,1)S(1)} %bitcast.154, f32[2187,1152]{1,0:T(8,128)} %reshape.249, f32[2187]{0:T(1024)S(1)} %broadcast_multiply_fusion, f32[2187]{0:T(1024)S(1)} %broadcast_multiply_fusion.1, f32[2187]{0:T(1024)S(1)} %copy-done.25, ...), kind=kLoop, calls=%fused_computation.86 | loop fusion | flops 37791360 | bytes 55480284 | tf_op jit(solution)/shard_map/mul | solution.py:201
  1205.4 8.9 reshape.248
  1214.3 6.0 reshape.246
  1220.3 22.7 %all-reduce = (f32[288]{0:T(512)}, f32[288]{0:T(512)}, f32[1152]{0:T(1024)}, f32[1152]{0:T(1024)}, f32[1152]{0:T(1024)}, /*index=5*/f32[1152]{0:T(1024)}, f32[1152]{0:T(1024)}, f32[1076]{0:T(1024)}, f32[1152]{0:T(1024)}) all-reduce(f32[288]{0:T(512)S(1)} %reduce_sum.184, ...), channel_id=1, replica_groups=mesh['dp'=8,'tensor'=4] {'dp'}, use_global_device_ids=true, to_apply=%region_22.23 | all-reduce | flops 8564 | bytes 68512 | tf_op jit(solution)/shard_map/psum | solution.py:203
  (218 shorter events, 163.4 us)
Async XLA Ops:
  7.2 323.5 %copy-start = (bf16[1076,1152]{1,0:T(8,128)(2,1)S(1)}, bf16[1076,1152]{1,0:T(8,128)(2,1)}, u32[]{:S(2)}) copy-start(bf16[1076,1152]{1,0:T(8,128)(2,1)} %param.38) | copy-start | bytes 7437316
  7.2 294.5 %all-reduce.6.cloned.1.call-start = ((), (), s32[]{:S(2)}) async-start(), calls=%async_computation.6 | async-start | bytes 10100736 | tf_op jit(solution)/shard_map/psum | solution.py:124
  10.7 11.6 copy-start.15
  10.7 11.6 copy-start.21
  10.7 11.6 copy-start.30
  22.2 10.9 copy-start.26
  22.3 10.8 copy-start.17
  30.0 11.1 copy-start.43
  41.1 13.7 %copy-start.10 = (bf16[1152,288]{0,1:T(8,128)(2,1)S(1)}, bf16[1152,288]{0,1:T(8,128)(2,1)}, u32[]{:S(2)}) copy-start(bf16[1152,288]{0,1:T(8,128)(2,1)} %param.25) | copy-start | bytes 1990660
  41.1 13.7 %copy-start.44 = (f32[288]{0:T(512)S(1)}, f32[288]{0:T(512)}, u32[]{:S(2)}) copy-start(f32[288]{0:T(512)} %param.26) | copy-start | bytes 3460
  68.2 41.5 %copy-start.13 = (bf16[288,1152]{1,0:T(8,128)(2,1)S(1)}, bf16[288,1152]{1,0:T(8,128)(2,1)}, u32[]{:S(2)}) copy-start(bf16[288,1152]{1,0:T(8,128)(2,1)} %param.30) | copy-start | bytes 1990660
  116.5 185.3 %copy-start.34 = (f32[1152]{0:T(1024)S(1)}, f32[1152]{0:T(1024)}, u32[]{:S(2)}) copy-start(f32[1152]{0:T(1024)} %param.31) | copy-start | bytes 13828
  116.5 422.8 %all-reduce.8.cloned.1.call-start = ((), (), s32[]{:S(2)}) async-start(), calls=%async_computation.7 | async-start | bytes 10100736 | tf_op jit(solution)/shard_map/psum | solution.py:141
  117.6 431.0 %copy-start.24 = (f32[2187]{0:T(1024)}, f32[2187]{0:T(1024)S(1)}, u32[]{:S(2)}) copy-start(f32[2187]{0:T(1024)S(1)} %mul.238) | copy-start | bytes 26248
  312.2 18.5 %slice-start = ((s8[10100736]{0:T(1024)(128)(4,1)}), s8[4194304]{0:T(1024)(128)(4,1)S(1)}, s32[]{:S(2)}) async-start(s8[10100736]{0:T(1024)(128)(4,1)} %bitcast.151), calls=%async_computation.15 | async-start | bytes 8388608
  318.9 11.8 slice-start.1
  318.9 11.8 slice-start.2
  330.7 15.3 %copy-start.40 = (bf16[1152,1076]{0,1:T(8,128)(2,1)S(1)}, bf16[1152,1076]{0,1:T(8,128)(2,1)}, u32[]{:S(2)}) copy-start(bf16[1152,1076]{0,1:T(8,128)(2,1)} %param.36) | copy-start | bytes 7437316
  357.2 17.5 %copy-start.20 = (f32[3,729]{1,0:T(4,128)S(1)}, f32[3,729]{1,0:T(4,128)}, u32[]{:S(2)}) copy-start(f32[3,729]{1,0:T(4,128)} %copy-done.19) | copy-start | bytes 26248
  357.2 17.5 %copy-start.22 = (f32[1152]{0:T(1024)S(1)}, f32[1152]{0:T(1024)}, u32[]{:S(2)}) copy-start(f32[1152]{0:T(1024)} %param.32) | copy-start | bytes 13828
  357.2 17.5 %copy-start.27 = (f32[3,729]{1,0:T(4,128)S(1)}, f32[3,729]{1,0:T(4,128)}, u32[]{:S(2)}) copy-start(f32[3,729]{1,0:T(4,128)} %copy-done.26) | copy-start | bytes 26248
  357.2 17.5 %copy-start.31 = (f32[1152]{0:T(1024)S(1)}, f32[1152]{0:T(1024)}, u32[]{:S(2)}) copy-start(f32[1152]{0:T(1024)} %param.33) | copy-start | bytes 13828
  357.3 423.4 %reduce-scatter.17.cloned.1.call-start = ((), (), s32[]{:S(2)}) async-start(), calls=%async_computation.13 | async-start | bytes 2985984 | tf_op jit(solution)/shard_map/reduce_scatter | solution.py:235
  374.5 408.1 %reduce-scatter.15.cloned.1.call-start = ((), (), s32[]{:S(2)}) async-start(), calls=%async_computation.12 | async-start | bytes 2985984 | tf_op jit(solution)/shard_map/reduce_scatter | solution.py:227
  402.1 382.5 %reduce-scatter.13.cloned.1.call-start = ((), (), s32[]{:S(2)}) async-start(), calls=%async_computation.11 | async-start | bytes 995328 | tf_op jit(solution)/shard_map/reduce_scatter | solution.py:232
  539.3 9.2 copy-start.5
  577.5 9.2 copy-start.1
  609.5 9.2 copy-start.1
  641.3 9.0 copy-start.1
  677.6 108.6 %reduce-scatter.11.cloned.1.call-start = ((), (), s32[]{:S(2)}) async-start(), calls=%async_computation.10 | async-start | bytes 995328 | tf_op jit(solution)/shard_map/reduce_scatter | solution.py:224
  697.5 91.2 %reduce-scatter.7.cloned.1.call-start = ((), (), s32[]{:S(2)}) async-start(), calls=%async_computation.8 | async-start | bytes 995328 | tf_op jit(solution)/shard_map/reduce_scatter | solution.py:218
  697.6 12.6 %copy-start.7 = (bf16[3,729,4,72]{1,3,2,0:T(8,128)(2,1)S(1)}, bf16[3,729,4,72]{1,3,2,0:T(8,128)(2,1)}, u32[]{:S(2)}) copy-start(bf16[3,729,4,72]{1,3,2,0:T(8,128)(2,1)} %get-tuple-element.216) | copy-start | bytes 3779140
  721.1 12.2 copy-start.11
  732.8 94.6 %reduce-scatter.9.cloned.1.call-start = ((), (), s32[]{:S(2)}) async-start(), calls=%async_computation.9 | async-start | bytes 995328 | tf_op jit(solution)/shard_map/reduce_scatter | solution.py:221
  733.2 8.4 copy-start.6
  748.0 430.1 %all-reduce.10.cloned.1.call-start = ((), (), s32[]{:S(2)}) async-start(), calls=%async_computation.14 | async-start | bytes 20201472 | tf_op jit(solution)/shard_map/psum | solution.py:131
  748.1 8.0 copy-start.8
  748.1 8.0 copy-start.14
  761.6 12.8 %copy-start.39 = (f32[3]{0:T(128)S(1)}, f32[3]{0:T(128)}, u32[]{:S(2)}) copy-start(f32[3]{0:T(128)} %copy-done.38) | copy-start | bytes 40
  761.6 416.5 %copy-start.16 = (f32[2187]{0:T(1024)S(1)}, f32[2187]{0:T(1024)}, u32[]{:S(2)}) copy-start(f32[2187]{0:T(1024)} %copy-done.15) | copy-start | bytes 26248
  761.6 416.5 %copy-start.18 = (f32[2187]{0:T(1024)S(1)}, f32[2187]{0:T(1024)}, u32[]{:S(2)}) copy-start(f32[2187]{0:T(1024)} %copy-done.17) | copy-start | bytes 26248
  761.6 416.5 %copy-start.23 = (f32[1152]{0:T(1024)S(1)}, f32[1152]{0:T(1024)}, u32[]{:S(2)}) copy-start(f32[1152]{0:T(1024)} %param.32) | copy-start | bytes 13828
  782.5 404.9 %copy-start.25 = (f32[2187]{0:T(1024)S(1)}, f32[2187]{0:T(1024)}, u32[]{:S(2)}) copy-start(f32[2187]{0:T(1024)} %copy-done.24) | copy-start | bytes 26248
  782.5 404.9 %copy-start.35 = (f32[1152]{0:T(1024)S(1)}, f32[1152]{0:T(1024)}, u32[]{:S(2)}) copy-start(f32[1152]{0:T(1024)} %param.39) | copy-start | bytes 13828
  1178.1 9.3 slice-start.3
  1178.1 9.3 slice-start.5
  1178.1 9.3 slice-start.4
  1178.1 9.3 slice-start.6
  (17 other events, 87.7 us)
Sparse Core Ops, SparseCore 0:
  116.6 185.0 all-reduce.5
  357.3 181.9 all-reduce.7
  542.8 42.7 reduce-scatter.16
  589.4 43.7 reduce-scatter.14
  677.8 34.0 reduce-scatter.12
  715.3 35.0 reduce-scatter.10
  753.6 35.0 reduce-scatter.6
  792.3 35.0 reduce-scatter.8
  830.6 347.4 all-reduce.9
where the time goes:
time: 1260 us; the launch traced here: 1250 us
  waiting for transfers between devices  701 us (56%)
  matrix products  238 us (19%)
  other arithmetic  144 us (11%)
  local copies, waits for them, and re-layouts  115 us (9%)
  blocking collectives  34.6 us (3%)
  between operations  15.3 us (1%)
    psum x1, waiting for transfers between devices, shards(): lax.psum(mlp_term.astype(jnp.bfloat16), 'tensor').astype(jnp.float32)  349 us
    psum x1, waiting for transfers between devices, shards(): lax.psum(attn_term.astype(jnp.bfloat16), 'tensor').astype(jnp.float32)  176 us
    psum x1, waiting for transfers between devices, shards(): lax.psum(second_term.astype(jnp.bfloat16), 'tensor').astype(jnp.float32)  137 us
    dot_general x6, matrix products, matmul_tn(): lax.dot_general(left_side, right_side, (((0,), (0,)), ((), ())), preferre...  59.7 us
    dot_general x6, matrix products, matmul_nt(): lax.dot_general(left_side, right_side, (((1,), (1,)), ((), ())), preferre...  51.3 us
    dot_general x6, matrix products, matmul(): return jnp.dot(left_side, right_side, preferred_element_type=jnp.float32)  45.2 us
    reduce_scatter x1, waiting for transfers between devices, shards(): lax.psum_scatter(grad_key_w.astype(jnp.bfloat16), 'dp', scatter_dimension...  37.1 us
    convert_element_type x3, other arithmetic, attend_back(): grad_scores = (attn_prob * (grad_prob - row_dot)).astype(jnp.bfloat16)  30.6 us
  transfers between devices with their start and end apart: 9, of which 5 were waited for; matrix products, arithmetic and copies ran while one was open for 23% of the time, Pallas kernels for 0%

commit v1 on v0

v1 whole, which is shorter than its diff:
```python
import functools, math
import jax, jax.numpy as jnp
from jax import lax
from jax.experimental import pallas as pl
from jax.experimental.pallas import tpu as pltpu
from jax.sharding import PartitionSpec as P

HD=72; TOK=768
norm_eps=1e-06; clip_limit=3.0
SC=1/math.sqrt(HD); LOG2E=1.4426950408889634
RT=256
F32=jnp.float32; BF=jnp.bfloat16
tanh_coef=0.7978845608028654; cube_coef=0.044715
def nn(a,b): return jnp.dot(a,b,preferred_element_type=F32)
def nt(a,b): return lax.dot_general(a,b,(((1,),(1,)),((),())),preferred_element_type=F32)
def tn(a,b): return lax.dot_general(a,b,(((0,),(0,)),((),())),preferred_element_type=F32)
VM=pl.BlockSpec(memory_space=pltpu.VMEM)

def attn_fwd_kernel(length, first, W, qb, vb, acc_in, qkv, att, lse, tops, acc, *, heads):
    cw=heads*HD
    @pl.loop(0, TOK//RT)
    def _(i):
        rows=pl.ds(pl.multiple_of(i*RT,RT),RT)
        t=nn(first[rows,:], W[:, :3*cw])
        q=(t[:, :cw]+qb[...]).astype(BF); k=t[:, cw:2*cw].astype(BF); v=(t[:,2*cw:]+vb[...]).astype(BF)
        for h in range(heads):
            qkv[h,rows,:]=q[:,h*HD:(h+1)*HD]
            qkv[heads+h,rows,:]=k[:,h*HD:(h+1)*HD]
            qkv[2*heads+h,rows,:]=v[:,h*HD:(h+1)*HD]
    tops[...]=jnp.full(tops.shape,-1e30,F32)
    @pl.loop(0, TOK//RT)
    def _(i):
        rows=pl.ds(pl.multiple_of(i*RT,RT),RT)
        rid=lax.broadcasted_iota(jnp.int32,(RT,1),0)+i*RT
        cid=lax.broadcasted_iota(jnp.int32,(1,TOK),1)
        outs=[]
        for h in range(heads):
            s=nt(qkv[h,rows,:], qkv[heads+h])
            s=jnp.where(cid<length, s, -1e30)
            m=jnp.max(s,axis=1,keepdims=True)
            e=jnp.exp2((s-m)*(SC*LOG2E))
            l=jnp.sum(e,axis=1,keepdims=True)
            o=nn(e.astype(BF), qkv[2*heads+h])*(1.0/l)
            outs.append(o.astype(BF))
            lse[h,rows,:]=m*(SC*LOG2E)+jnp.log2(l)
            tops[h:h+1,:]=jnp.maximum(tops[h:h+1,:], jnp.max(jnp.where(rid<length,m,-1e30))*SC)
        a=jnp.concatenate(outs,axis=1)
        att[rows,:]=a
        acc[rows,:]=acc_in[rows,:]+nt(a, W[:,3*cw:])

def attn_fwd(first, W, qb, vb, acc, length):
    D=first.shape[1]; cw=W.shape[1]//4; heads=cw//HD
    return pl.pallas_call(functools.partial(attn_fwd_kernel,length,heads=heads),
        out_shape=(jax.ShapeDtypeStruct((3*heads,TOK,HD),BF),jax.ShapeDtypeStruct((TOK,cw),BF),
                   jax.ShapeDtypeStruct((heads,TOK,1),F32),jax.ShapeDtypeStruct((heads,128),F32),jax.ShapeDtypeStruct((TOK,D),F32)),
        in_specs=[VM]*5,out_specs=(VM,)*5,
        input_output_aliases={4:4},
        compiler_params=pltpu.CompilerParams(vmem_limit_bytes=48*2**20),
        cost_estimate=pl.CostEstimate(flops=2*TOK*(D*cw*4+heads*2*TOK*HD*3),bytes_accessed=20*2**20,transcendentals=heads*TOK*TOK),
        name="attn_fwd")(first,W,qb,vb,acc)

def mlp_kernel(second, secondT, gout, goutT, E, ST, eb, mlp_in, sec_in, gE, gST, geb, mlp, sec, act_s, gpre_s):
    geb[...]=jnp.zeros_like(geb)
    @pl.loop(0, TOK//RT)
    def _(i):
        rows=pl.ds(pl.multiple_of(i*RT,RT),RT)
        u=nn(second[rows,:],E[...])+eb[...]
        ga=nn(gout[rows,:],ST[...])
        u2=u*u
        t=jnp.tanh(u*(tanh_coef+(tanh_coef*cube_coef)*u2))
        hu=0.5*(1.0+t)
        act=(u*hu).astype(BF)
        act_s[rows,:]=act
        slope=hu+u*(0.5*tanh_coef)*(1.0-t*t)*(1.0+(3.0*cube_coef)*u2)
        gp=ga*slope
        geb[...]+=jnp.sum(gp,axis=0,keepdims=True)
        gpl=gp.astype(BF)
        gpre_s[rows,:]=gpl
        mlp[rows,:]=mlp_in[rows,:]+nt(act,ST[...])
        sec[rows,:]=sec_in[rows,:]+nt(gpl,E[...])
    @pl.loop(0, secondT.shape[0]//384)
    def _(i):
        rows=pl.ds(pl.multiple_of(i*384,128),384)
        gE[rows,:]=nn(secondT[rows,:],gpre_s[...]).astype(BF)
        gST[rows,:]=nn(goutT[rows,:],act_s[...]).astype(BF)

def mlp_call(second,secondT,gout,goutT,E,ST,eb,mlp,sec):
    D=second.shape[1]; F=E.shape[1]
    return pl.pallas_call(mlp_kernel,
        out_shape=(jax.ShapeDtypeStruct((D,F),BF),jax.ShapeDtypeStruct((D,F),BF),jax.ShapeDtypeStruct((1,F),F32),
                   jax.ShapeDtypeStruct((TOK,D),F32),jax.ShapeDtypeStruct((TOK,D),F32)),
        in_specs=[VM]*9,out_specs=(VM,)*5,
        input_output_aliases={7:3,8:4},
        scratch_shapes=[pltpu.VMEM((TOK,F),BF),pltpu.VMEM((TOK,F),BF)],
        compiler_params=pltpu.CompilerParams(vmem_limit_bytes=56*2**20),
        cost_estimate=pl.CostEstimate(flops=2*6*TOK*D*F,bytes_accessed=30*2**20,transcendentals=TOK*F),
        name="mlp")(second,secondT,gout,goutT,E,ST,eb,mlp,sec)

def attn_bwd_kernel(length, gmid, gmidT, firstT, W, qkv, att, lse, acc_in, gW, gqb, gvb, acc, ga_s, d_s, dk_s, dv_s, *, heads):
    cw=heads*HD
    @pl.loop(0, TOK//RT)
    def _(i):
        rows=pl.ds(pl.multiple_of(i*RT,RT),RT)
        g=nn(gmid[rows,:], W[:,3*cw:]).astype(BF)
        for h in range(heads):
            ga_s[h,rows,:]=g[:,h*HD:(h+1)*HD]
    gqb[...]=jnp.zeros_like(gqb)
    dk_s[...]=jnp.zeros_like(dk_s); dv_s[...]=jnp.zeros_like(dv_s)
    @pl.loop(0, TOK//RT)
    def _(i):
        rows=pl.ds(pl.multiple_of(i*RT,RT),RT)
        cid=lax.broadcasted_iota(jnp.int32,(1,TOK),1)
        dqs=[]
        for h in range(heads):
            q=qkv[h,rows,:]; k=qkv[heads+h]; v=qkv[2*heads+h]; g=ga_s[h,rows,:]
            s=nt(q,k)
            p=jnp.exp2(s*(SC*LOG2E)-lse[h,rows,:])
            p=jnp.where(cid<length,p,0.0)
            dp=nt(g,v)
            dd=jnp.sum(g.astype(F32)*att[rows,h*HD:(h+1)*HD].astype(F32),axis=1,keepdims=True)
            ds=(p*(dp-dd)).astype(BF)
            dqs.append(nn(ds,k)*SC)
            dk_s[h]+=tn(ds,q)
            dv_s[h]+=tn(p.astype(BF),g)
        dq=jnp.concatenate(dqs,axis=1)
        gqb[...]+=jnp.sum(dq,axis=0,keepdims=True)
        d_s[rows,:cw]=dq.astype(BF)
    dk=jnp.concatenate([dk_s[h]*SC for h in range(heads)],axis=1)
    d_s[:,cw:2*cw]=dk.astype(BF)
    dv=jnp.concatenate([dv_s[h] for h in range(heads)],axis=1)
    gvb[...]=jnp.sum(dv,axis=0,keepdims=True)
    d_s[:,2*cw:]=dv.astype(BF)
    @pl.loop(0, TOK//RT)
    def _(i):
        rows=pl.ds(pl.multiple_of(i*RT,RT),RT)
        acc[rows,:]=acc_in[rows,:]+nt(d_s[rows,:],W[:,:3*cw])
    @pl.loop(0, firstT.shape[0]//384)
    def _(i):
        rows=pl.ds(pl.multiple_of(i*384,128),384)
        gW[rows,:3*cw]=nn(firstT[rows,:],d_s[...]).astype(BF)
        gW[rows,3*cw:]=nn(gmidT[rows,:],att[...]).astype(BF)

def attn_bwd(gmid,gmidT,firstT,W,qkv,att,lse,acc,length):
    D=gmid.shape[1]; cw=W.shape[1]//4; heads=cw//HD
    return pl.pallas_call(functools.partial(attn_bwd_kernel,length,heads=heads),
        out_shape=(jax.ShapeDtypeStruct((D,4*cw),BF),jax.ShapeDtypeStruct((1,cw),F32),jax.ShapeDtypeStruct((1,cw),F32),jax.ShapeDtypeStruct((TOK,D),F32)),
        in_specs=[VM]*8,out_specs=(VM,)*4,
        input_output_aliases={7:3},
        scratch_shapes=[pltpu.VMEM((heads,TOK,HD),BF),pltpu.VMEM((TOK,3*cw),BF),pltpu.VMEM((heads,TOK,HD),F32),pltpu.VMEM((heads,TOK,HD),F32)],
        compiler_params=pltpu.CompilerParams(vmem_limit_bytes=56*2**20),
        cost_estimate=pl.CostEstimate(flops=2*TOK*(D*cw*8+heads*5*TOK*HD*3),bytes_accessed=25*2**20,transcendentals=heads*TOK*TOK),
        name="attn_bwd")(gmid,gmidT,firstT,W,qkv,att,lse,acc)


def normalize(values):
    centre = jnp.mean(values, axis=-1, keepdims=True)
    centred = values - centre
    spread = jnp.mean(centred * centred, axis=-1, keepdims=True)
    inverse = lax.rsqrt(spread + norm_eps)
    return centred * inverse, inverse


def norm_back(grad_norm, normed, inverse, gain):
    scaled = grad_norm * gain
    first_mean = jnp.mean(scaled, axis=-1, keepdims=True)
    second_mean = jnp.mean(scaled * normed, axis=-1, keepdims=True)
    grad_input = inverse * (scaled - first_mean - normed * second_mean)
    return grad_input, jnp.sum(grad_norm * normed, axis=0), jnp.sum(grad_norm, axis=0)


def slot_table(d, groups):
    z = lax.axis_index("tensor")
    middle = 1 + d % 2
    return jnp.where(z == 0, 0, jnp.where(z == groups - 1, 1, 2)), (z == 0) | (z == groups - 1) | (z == middle)


def spread_general(own, groups):
    d, count = lax.axis_index("dp"), lax.axis_size("dp")
    rows = own.shape[0] // count
    piece = lax.dynamic_slice_in_dim(own, d * rows, rows, 0)
    piece = lax.all_gather(piece, "tensor")
    whole = lax.all_gather(piece, "dp", axis=1, tiled=True)
    return [whole[i] for i in range(groups)]


def collect_general(parts):
    part = lax.psum_scatter(jnp.stack(parts), "dp", scatter_dimension=1, tiled=True)
    return lax.psum_scatter(part, "tensor", scatter_dimension=0, tiled=True)[0].astype(F32)


def share_general(mine, d, groups):
    every = lax.all_gather(mine, "tensor")
    return jnp.stack([every[0], every[groups - 1], lax.dynamic_index_in_dim(every, 1 + d % 2, 0, keepdims=False)])


def shards(images, counts, cotangent, query_w, query_b, key_w, value_w, value_b, out_w, out_b, norm1_gain, norm1_shift,
           norm2_gain, norm2_shift, expand_w, expand_b, shrink_w, shrink_b):
    slots, length, width = images.shape
    groups = lax.axis_size("tensor")
    d, z = lax.axis_index("dp"), lax.axis_index("tensor")
    cw, fw = query_w.shape[1], expand_w.shape[1]
    heads = cw // HD
    slot, used = slot_table(d, groups)
    live = jnp.where(used & (slot < counts[0]), 1.0, 0.0).astype(F32)
    pad = lambda a: jnp.pad(a, ((0, TOK - length), (0, 0)))
    x = pad(lax.dynamic_index_in_dim(images, slot, 0, keepdims=False)).astype(F32)
    gout = pad(lax.dynamic_index_in_dim(cotangent, slot, 0, keepdims=False)) * live.astype(BF)
    gout_t = gout.T

    attn_own = jnp.concatenate([query_w, key_w, value_w, out_w.T], axis=1)
    mlp_own = jnp.concatenate([expand_w, shrink_w.T], axis=1)
    attn_ws = spread_general(attn_own, groups)
    mlp_ws = spread_general(mlp_own, groups)
    biases = lax.all_gather(jnp.concatenate([query_b, value_b, expand_b]), "tensor")
    shard_of = list(range(groups))

    normed1, inverse1 = normalize(x)
    first = (normed1 * norm1_gain + norm1_shift).astype(BF)
    first_t = first.T
    acc = x + out_b
    kept, tops = [], []
    for k in range(groups):
        b = biases[k]
        qkv, att, lse, top, acc = attn_fwd(first, attn_ws[k], b[None, :cw], b[None, cw:2 * cw], acc, length)
        kept.append((qkv, att, lse))
        tops.append(top[:, 0])
    midway = acc
    normed2, inverse2 = normalize(midway)
    second = (normed2 * norm2_gain + norm2_shift).astype(BF)
    second_t = second.T
    mlp = midway + shrink_b
    sec = jnp.zeros((TOK, width), F32)
    grad_mlp, geb = [], []
    for k in range(groups):
        w = mlp_ws[k]
        g_e, g_s, g_b, mlp, sec = mlp_call(second, second_t, gout, gout_t, w[:, :fw], w[:, fw:], biases[k][None, 2 * cw:], mlp, sec)
        grad_mlp.append(jnp.concatenate([g_e, g_s], axis=1))
        geb.append(g_b[0])
    output = (mlp[:length] * live).astype(BF)
    back2, gn2g, gn2s = norm_back(sec, normed2, inverse2, norm2_gain)
    gout32 = gout.astype(F32)
    gmid = gout32 + back2
    gmid_low = gmid.astype(BF)
    gmid_t = gmid_low.T
    acc = jnp.zeros((TOK, width), F32)
    grad_attn, gqb, gvb = [], [], []
    for k in range(groups):
        g_w, g_q, g_v, acc = attn_bwd(gmid_low, gmid_t, first_t, attn_ws[k], *kept[k], acc, length)
        grad_attn.append(g_w)
        gqb.append(g_q[0])
        gvb.append(g_v[0])
    back1, gn1g, gn1s = norm_back(acc, normed1, inverse1, norm1_gain)
    input_grad = ((gmid + back1) * live)[:length].astype(BF)

    outputs = share_general(output, d, groups)
    input_grads = share_general(input_grad, d, groups).astype(F32)
    sum_attn = collect_general(grad_attn)
    sum_mlp = collect_general(grad_mlp)
    vector = jnp.concatenate([jnp.stack(gqb + gvb, 0).reshape(-1), jnp.stack(geb).reshape(-1), jnp.sum(gmid, axis=0), jnp.sum(gout32, axis=0), gn1g, gn1s, gn2g, gn2s])
    vector = lax.psum(vector, ("dp", "tensor"))
    part = lambda start, size: lax.dynamic_slice_in_dim(vector, start, size, 0)
    whole, hidden = cw * groups, fw * groups
    tail = [vector[2 * whole + hidden + i * width:][:width] for i in range(6)]
    logit_top = lax.pmax(jnp.where(live > 0.0, jnp.stack(tops), -1e30), ("dp", "tensor"))
    logit_top = lax.dynamic_index_in_dim(logit_top, z, 0, keepdims=False)
    factor = jnp.sqrt(clip_limit / jnp.maximum(logit_top, clip_limit))
    column_factor = jnp.repeat(factor, HD)
    clipped_query = (query_w.astype(F32) * column_factor).astype(BF)
    clipped_key = (key_w.astype(F32) * column_factor).astype(BF)
    return (outputs, input_grads, sum_attn[:, :cw], part(z * cw, cw), sum_attn[:, cw:2 * cw], sum_attn[:, 2 * cw:3 * cw], part(whole + z * cw, cw),
            sum_attn[:, 3 * cw:].T, tail[0], tail[2], tail[3], tail[4], tail[5], sum_mlp[:, :fw], part(2 * whole + z * fw, fw), sum_mlp[:, fw:].T,
            tail[1], clipped_query, clipped_key)


def solution(mesh):
    columns, rows, vector = P(None, "tensor"), P("tensor", None), P("tensor")
    whole = P("dp", None, None)
    return jax.shard_map(
        shards, mesh=mesh,
        in_specs=(whole, P("dp"), whole, columns, vector, columns, columns, vector, rows, P(), P(), P(), P(), P(), columns, vector, rows, P()),
        out_specs=(whole, whole, P("dp", "tensor"), vector, P("dp", "tensor"), P("dp", "tensor"), vector, P("tensor", "dp"), P(), P(), P(), P(), P(),
                   P("dp", "tensor"), vector, P("tensor", "dp"), P(), columns, columns),
        check_vma=False)
```

time: 1260 us -> 1100 us (0.87)
  Pallas kernels: 0 us -> 271 us
  matrix products: 238 us -> 0 us
  waiting for transfers between devices: 701 us -> 489 us
  blocking collectives: 34.6 us -> 105 us
  other arithmetic: 144 us -> 88.4 us
    psum x3 -> x0, waiting for transfers between devices: 663 us -> none  [the longest x1 349 us: shards(): lax.psum(mlp_term.astype(jnp.bfloat16), 'tensor').astype(jnp.float32)]
    pallas_call x0 -> x12, Pallas kernels: none -> 271 us  [the longest x4 106 us: mlp_call(): pl.pallas_call(mlp_kernel, out_shape=(jax.ShapeDtypeStruct((D, F), BF), j...]
    all_gather x0 -> x6, waiting for transfers between devices: none -> 246 us  [the longest x2 139 us: share_general(): every = lax.all_gather(mine, 'tensor')]
    dot_general x39 -> x0, matrix products: 238 us -> none  [the longest x6 59.7 us: matmul_tn(): lax.dot_general(left_side, right_side, (((0,), (0,)), ((), ())), preferre...]
    reduce_scatter x6 -> x4, waiting for transfers between devices: 38 us -> 243 us  [the longest x2 169 us: collect_general(): lax.psum_scatter(jnp.stack(parts), 'dp', scatter_dimension=1, tiled=True)]
    convert_element_type x13 -> x7, other arithmetic: 55.3 us -> 12.2 us  [the longest x1 4.78 us: shards(): input_grads = share_general(input_grad, d, groups).astype(F32)]
    another operation x4 -> x8, other arithmetic: 0.01 us -> 39.6 us  [the longest x6 35.3 us: collect_general(): jnp.stack(parts)]
    reshape x7 -> x2, local copies, waits for them, and re-layouts: 40.9 us -> 2.19 us  [the longest x1 1.41 us: shards(): jnp.stack(geb).reshape(-1)]
  transfers between devices with their start and end apart: 9 -> 10, of which waited for: 5 -> 10; matrix products, arithmetic and copies ran while one was open for 23% -> 13% of each run, Pallas kernels for 0% -> 6%
where the time goes in v1:
time: 1100 us; the launch traced here: 1090 us
  waiting for transfers between devices  489 us (44%)
  Pallas kernels  271 us (25%)
  local copies, waits for them, and re-layouts  122 us (11%)
  blocking collectives  105 us (10%)
  other arithmetic  88.4 us (8%)
  between operations  16.2 us (1%)
    reduce_scatter x2, waiting for transfers between devices, collect_general(): lax.psum_scatter(jnp.stack(parts), 'dp', scatter_dimension=1, tiled=True)  169 us
    all_gather x2, waiting for transfers between devices, share_general(): every = lax.all_gather(mine, 'tensor')  139 us
    pallas_call x4, Pallas kernels, mlp_call(): pl.pallas_call(mlp_kernel, out_shape=(jax.ShapeDtypeStruct((D, F), BF), j...  106 us
    pallas_call x4, Pallas kernels, attn_bwd(): pl.pallas_call(functools.partial(attn_bwd_kernel, length, heads=heads), o...  102 us
    all_gather x2, waiting for transfers between devices, spread_general(): piece = lax.all_gather(piece, 'tensor')  77.8 us
    reduce_scatter x2, waiting for transfers between devices, collect_general(): lax.psum_scatter(part, 'tensor', scatter_dimension=0, tiled=True)[0]  73.8 us
    pallas_call x4, Pallas kernels, attn_fwd(): pl.pallas_call(functools.partial(attn_fwd_kernel, length, heads=heads), o...  63.7 us
    psum x1, blocking collectives, shards(): vector = lax.psum(vector, ('dp', 'tensor'))  46.9 us
  transfers between devices with their start and end apart: 10, of which 10 were waited for; matrix products, arithmetic and copies ran while one was open for 13% of the time, Pallas kernels for 6%

profile of v1, /device:TPU:1, one launch (start us, length us, event | category | flops | bytes accessed | tf_op | source)
XLA Modules:
  0.0 1092.7 jit_solution(15356471681712951836)
XLA Ops:
  12.2 3.6 concatenate.24
  17.6 4.1 copy.119
  21.7 5.2 copy.120
  29.0 23.1 %all-gather.18.cloned.1.call-done = bf16[576,1152]{1,0:T(8,128)(2,1)} async-done(((bf16[144,1152]{1,0:T(8,128)(2,1)}), bf16[576,1152]{1,0:T(8,128)(2,1)}) %all-gather.18.cloned.1.call-update) | async-done | bytes 1327120 | tf_op jit(solution)/shard_map/all_gather | solution.py:181
  52.2 54.6 %all-gather.20.cloned.1.call-done = bf16[576,2152]{1,0:T(8,128)(2,1)} async-done(((bf16[144,2152]{1,0:T(8,128)(2,1)}), bf16[576,2152]{1,0:T(8,128)(2,1)}) %all-gather.20.cloned.1.call-update) | async-done | bytes 2479120 | tf_op jit(solution)/shard_map/all_gather | solution.py:181
  106.9 3.4 constant_dynamic-slice_fusion.3
  115.9 5.4 copy.112.acc_in
  123.0 13.8 %all-reduce.2 = f32[6608]{0:T(1024)S(1)} all-reduce(f32[6608]{0:T(1024)S(1)} %dynamic-update-slice), channel_id=3, replica_groups=mesh['dp'=8,'tensor'=4] {'tensor'}, use_global_device_ids=true, to_apply=%add.2 | all-reduce | flops 6608 | bytes 52864
  149.4 3.4 fusion.24.firstT
  152.8 19.0 %all-gather.14.cloned.1.call-done = bf16[4,1152,1152]{2,1,0:T(8,128)(2,1)} async-done(((bf16[4,144,1152]{2,1,0:T(8,128)(2,1)}), bf16[4,1152,1152]{2,1,0:T(8,128)(2,1)}) %all-gather.14.cloned.1.call-update) | async-done | bytes 10616848 | tf_op jit(solution)/shard_map/all_gather | solution.py:182
  171.8 7.7 slice_bitcast_fusion.4
  179.5 16.6 %attn_fwd.4 = (bf16[12,768,72]{2,1,0:T(8,128)(2,1)}, bf16[768,288]{1,0:T(8,128)(2,1)S(1)}, f32[4,768,1]{2,1,0:T(8,128)S(1)}, f32[4,128]{1,0:T(4,128)S(1)}, f32[768,1152]{1,0:T(8,128)}) custom-call(bf16[768,1152]{1,0:T(8,128)(2,1)S(1)} %copy.116.first, bf16[1152,1152]{1,0:T(8,128)(2,1)} %get-tuple-element.184.W, ...), custom_call_target="tpu_custom_call", output_to_operand_aliasing={{4}: (4, {})} | custom-call | flops 4076863488 | bytes 20971520 | tf_op jit(solution)/shard_map/attn_fwd/pallas_call | solution.py:53
  198.1 15.4 %attn_fwd.5 = (bf16[12,768,72]{2,1,0:T(8,128)(2,1)}, bf16[768,288]{1,0:T(8,128)(2,1)S(1)}, f32[4,768,1]{2,1,0:T(8,128)S(1)}, f32[4,128]{1,0:T(4,128)S(1)}, f32[768,1152]{1,0:T(8,128)}) custom-call(bf16[768,1152]{1,0:T(8,128)(2,1)S(1)} %copy.116.first, bf16[1152,1152]{1,0:T(8,128)(2,1)} %get-tuple-element.185.W, ...), custom_call_target="tpu_custom_call", output_to_operand_aliasing={{4}: (4, {})} | custom-call | flops 4076863488 | bytes 20971520 | tf_op jit(solution)/shard_map/attn_fwd/pallas_call | solution.py:53
  215.5 15.4 %attn_fwd.6 = (bf16[12,768,72]{2,1,0:T(8,128)(2,1)}, bf16[768,288]{1,0:T(8,128)(2,1)S(1)}, f32[4,768,1]{2,1,0:T(8,128)S(1)}, f32[4,128]{1,0:T(4,128)S(1)}, f32[768,1152]{1,0:T(8,128)}) custom-call(bf16[768,1152]{1,0:T(8,128)(2,1)S(1)} %copy.116.first, bf16[1152,1152]{1,0:T(8,128)(2,1)} %get-tuple-element.186.W, ...), custom_call_target="tpu_custom_call", output_to_operand_aliasing={{4}: (4, {})} | custom-call | flops 4076863488 | bytes 20971520 | tf_op jit(solution)/shard_map/attn_fwd/pallas_call | solution.py:53
  231.8 16.2 %attn_fwd.7 = (bf16[12,768,72]{2,1,0:T(8,128)(2,1)}, bf16[768,288]{1,0:T(8,128)(2,1)S(1)}, f32[4,768,1]{2,1,0:T(8,128)S(1)}, f32[4,128]{1,0:T(4,128)S(1)}, f32[768,1152]{1,0:T(8,128)}) custom-call(bf16[768,1152]{1,0:T(8,128)(2,1)S(1)} %copy.116.first, bf16[1152,1152]{1,0:T(8,128)(2,1)} %get-tuple-element.187.W, ...), custom_call_target="tpu_custom_call", output_to_operand_aliasing={{4}: (4, {})} | custom-call | flops 4076863488 | bytes 20971520 | tf_op jit(solution)/shard_map/attn_fwd/pallas_call | solution.py:53
  249.9 3.3 copy.117
  253.2 4.1 broadcast_add_fusion
  260.3 3.9 copy.127.second
  266.6 10.7 all-gather.16.cloned.1.call-done
  277.3 7.5 slice_bitcast_fusion
  284.8 5.3 fusion.16
  290.2 5.4 fusion.18
  297.6 26.6 %mlp.4 = (bf16[1152,1076]{1,0:T(8,128)(2,1)}, bf16[1152,1076]{1,0:T(8,128)(2,1)}, f32[1,1076]{1,0:T(1,128)}, f32[768,1152]{1,0:T(8,128)}, f32[768,1152]{1,0:T(8,128)}) custom-call(bf16[768,1152]{1,0:T(8,128)(2,1)} %copy.127.second, bf16[1152,768]{1,0:T(8,128)(2,1)} %fusion.25.secondT, ...), custom_call_target="tpu_custom_call", output_to_operand_aliasing={{3}: (7, {}), {4}: (8, {})} | custom-call | flops 11423711232 | bytes 31457280 | tf_op jit(solution)/shard_map/mlp/pallas_call | solution.py:89
  324.2 26.4 %mlp.5 = (bf16[1152,1076]{1,0:T(8,128)(2,1)}, bf16[1152,1076]{1,0:T(8,128)(2,1)}, f32[1,1076]{1,0:T(1,128)}, f32[768,1152]{1,0:T(8,128)}, f32[768,1152]{1,0:T(8,128)}) custom-call(bf16[768,1152]{1,0:T(8,128)(2,1)} %copy.127.second, bf16[1152,768]{1,0:T(8,128)(2,1)} %fusion.25.secondT, ...), custom_call_target="tpu_custom_call", output_to_operand_aliasing={{3}: (7, {}), {4}: (8, {})} | custom-call | flops 11423711232 | bytes 31457280 | tf_op jit(solution)/shard_map/mlp/pallas_call | solution.py:89
  350.6 26.9 %mlp.6 = (bf16[1152,1076]{1,0:T(8,128)(2,1)}, bf16[1152,1076]{1,0:T(8,128)(2,1)}, f32[1,1076]{1,0:T(1,128)}, f32[768,1152]{1,0:T(8,128)}, f32[768,1152]{1,0:T(8,128)}) custom-call(bf16[768,1152]{1,0:T(8,128)(2,1)} %copy.127.second, bf16[1152,768]{1,0:T(8,128)(2,1)} %fusion.25.secondT, ...), custom_call_target="tpu_custom_call", output_to_operand_aliasing={{3}: (7, {}), {4}: (8, {})} | custom-call | flops 11423711232 | bytes 31457280 | tf_op jit(solution)/shard_map/mlp/pallas_call | solution.py:89
  377.5 26.2 %mlp.7 = (bf16[1152,1076]{1,0:T(8,128)(2,1)}, bf16[1152,1076]{1,0:T(8,128)(2,1)}, f32[1,1076]{1,0:T(1,128)}, f32[768,1152]{1,0:T(8,128)}, f32[768,1152]{1,0:T(8,128)}) custom-call(bf16[768,1152]{1,0:T(8,128)(2,1)} %copy.127.second, bf16[1152,768]{1,0:T(8,128)(2,1)} %fusion.25.secondT, ...), custom_call_target="tpu_custom_call", output_to_operand_aliasing={{3}: (7, {}), {4}: (8, {})} | custom-call | flops 11423711232 | bytes 31457280 | tf_op jit(solution)/shard_map/mlp/pallas_call | solution.py:89
  403.7 5.2 copy.129
  408.8 3.9 multiply_reduce_fusion
  422.3 25.4 %attn_bwd.4 = (bf16[1152,1152]{1,0:T(8,128)(2,1)}, f32[1,288]{1,0:T(1,128)}, f32[1,288]{1,0:T(1,128)}, f32[768,1152]{1,0:T(8,128)}) custom-call(bf16[768,1152]{1,0:T(8,128)(2,1)} %copy.133.gmid, bf16[1152,768]{1,0:T(8,128)(2,1)} %convert_bitcast_fusion.gmidT, bf16[1152,768]{1,0:T(8,128)(2,1)} %fusion.24.firstT, ...), custom_call_target="tpu_custom_call", output_to_operand_aliasing={{3}: (7, {})} | custom-call | flops 9172942848 | bytes 26214400 | tf_op jit(solution)/shard_map/attn_bwd/pallas_call | solution.py:145
  447.7 25.3 %attn_bwd.5 = (bf16[1152,1152]{1,0:T(8,128)(2,1)}, f32[1,288]{1,0:T(1,128)}, f32[1,288]{1,0:T(1,128)}, f32[768,1152]{1,0:T(8,128)}) custom-call(bf16[768,1152]{1,0:T(8,128)(2,1)} %copy.133.gmid, bf16[1152,768]{1,0:T(8,128)(2,1)} %convert_bitcast_fusion.gmidT, bf16[1152,768]{1,0:T(8,128)(2,1)} %fusion.24.firstT, ...), custom_call_target="tpu_custom_call", output_to_operand_aliasing={{3}: (7, {})} | custom-call | flops 9172942848 | bytes 26214400 | tf_op jit(solution)/shard_map/attn_bwd/pallas_call | solution.py:145
  473.0 25.5 %attn_bwd.6 = (bf16[1152,1152]{1,0:T(8,128)(2,1)}, f32[1,288]{1,0:T(1,128)}, f32[1,288]{1,0:T(1,128)}, f32[768,1152]{1,0:T(8,128)}) custom-call(bf16[768,1152]{1,0:T(8,128)(2,1)} %copy.133.gmid, bf16[1152,768]{1,0:T(8,128)(2,1)} %convert_bitcast_fusion.gmidT, bf16[1152,768]{1,0:T(8,128)(2,1)} %fusion.24.firstT, ...), custom_call_target="tpu_custom_call", output_to_operand_aliasing={{3}: (7, {})} | custom-call | flops 9172942848 | bytes 26214400 | tf_op jit(solution)/shard_map/attn_bwd/pallas_call | solution.py:145
  498.5 25.4 %attn_bwd.7 = (bf16[1152,1152]{1,0:T(8,128)(2,1)}, f32[1,288]{1,0:T(1,128)}, f32[1,288]{1,0:T(1,128)}, f32[768,1152]{1,0:T(8,128)}) custom-call(bf16[768,1152]{1,0:T(8,128)(2,1)} %copy.133.gmid, bf16[1152,768]{1,0:T(8,128)(2,1)} %convert_bitcast_fusion.gmidT, bf16[1152,768]{1,0:T(8,128)(2,1)} %fusion.24.firstT, ...), custom_call_target="tpu_custom_call", output_to_operand_aliasing={{3}: (7, {})} | custom-call | flops 9172942848 | bytes 26214400 | tf_op jit(solution)/shard_map/attn_bwd/pallas_call | solution.py:145
  523.9 7.7 pad_maximum_fusion.1
  533.3 3.5 maximum_bitcast_fusion
  538.9 4.0 maximum_bitcast_fusion.2
  542.9 7.5 maximum_bitcast_fusion.3
  550.4 11.1 %pad_maximum_fusion = bf16[4,1152,2152]{2,1,0:T(8,128)(2,1)} fusion(bf16[1,1152,2152]{2,1,0:T(8,128)(2,1)} %maximum_bitcast_fusion.3, bf16[1,1152,2152]{2,1,0:T(8,128)(2,1)S(1)} %maximum_bitcast_fusion.2, bf16[1,1152,2152]{2,1,0:T(8,128)(2,1)S(1)} %maximum_bitcast_fusion.1, bf16[1,1152,2152]{2,1,0:T(8,128)(2,1)S(1)} %maximum_bitcast_fusion), kind=kLoop, calls=%fused_computation | loop fusion | flops 29749248 | bytes 39665664 | tf_op jit(solution)/shard_map/stack | solution.py:187
  565.0 5.4 copy.134
  570.4 4.1 fusion.12
  577.7 35.8 %reduce-scatter.5.cloned.1.call-done = bf16[4,144,1152]{2,1,0:T(8,128)(2,1)} async-done(((bf16[4,1152,1152]{2,1,0:T(8,128)(2,1)}), bf16[4,144,1152]{2,1,0:T(8,128)(2,1)}) %reduce-scatter.5.cloned.1.call-update) | async-done | bytes 1327120 | tf_op jit(solution)/shard_map/reduce_scatter | solution.py:187
  615.0 133.5 %reduce-scatter.9.cloned.1.call-done = bf16[4,144,2152]{2,1,0:T(8,128)(2,1)} async-done(((bf16[4,1152,2152]{2,1,0:T(8,128)(2,1)}), bf16[4,144,2152]{2,1,0:T(8,128)(2,1)}) %reduce-scatter.9.cloned.1.call-update) | async-done | bytes 2479120 | tf_op jit(solution)/shard_map/reduce_scatter | solution.py:187
  749.4 44.3 %pmax.7 = f32[4,4]{1,0:T(4,128)S(1)} all-reduce(f32[4,4]{1,0:T(4,128)S(1)} %maximum_select_fusion), channel_id=1, replica_groups=mesh['dp'=8,'tensor'=4] {'dp','tensor'}, use_global_device_ids=true, to_apply=%region_19.20 | all-reduce | flops 16 | bytes 128 | tf_op jit(solution)/shard_map/pmax | solution.py:264
  806.0 46.9 %psum.7 = f32[13520]{0:T(1024)S(1)} all-reduce(f32[13520]{0:T(1024)S(1)} %concatenate.27), channel_id=1, replica_groups=mesh['dp'=8,'tensor'=4] {'dp','tensor'}, use_global_device_ids=true, to_apply=%region_16.17 | all-reduce | flops 13520 | bytes 108160 | tf_op jit(solution)/shard_map/psum | solution.py:260
  855.0 21.4 %all-gather.22.cloned.1.call-done = bf16[4,729,1152]{2,1,0:T(8,128)(2,1)} async-done(((bf16[1,729,1152]{2,1,0:T(8,128)(2,1)}), bf16[4,729,1152]{2,1,0:T(8,128)(2,1)}) %all-gather.22.cloned.1.call-update) | async-done | bytes 6718480 | tf_op jit(solution)/shard_map/all_gather | solution.py:192
  882.2 117.5 %all-gather.24.cloned.1.call-done = bf16[4,729,1152]{2,1,0:T(8,128)(2,1)} async-done(((bf16[1,729,1152]{2,1,0:T(8,128)(2,1)}), bf16[4,729,1152]{2,1,0:T(8,128)(2,1)}) %all-gather.24.cloned.1.call-update) | async-done | bytes 6718480 | tf_op jit(solution)/shard_map/all_gather | solution.py:192
  1002.5 4.8 maximum_convert_fusion
  1007.3 24.3 %reduce-scatter.7.cloned.1.call-done = bf16[1,144,1152]{2,1,0:T(8,128)(2,1)} async-done(((bf16[4,144,1152]{2,1,0:T(8,128)(2,1)}), bf16[1,144,1152]{2,1,0:T(8,128)(2,1)}) %reduce-scatter.7.cloned.1.call-update) | async-done | bytes 331792 | tf_op jit(solution)/shard_map/reduce_scatter | solution.py:188
  1033.7 49.5 %reduce-scatter.11.cloned.1.call-done = bf16[1,144,2152]{2,1,0:T(8,128)(2,1)} async-done(((bf16[4,144,2152]{2,1,0:T(8,128)(2,1)}), bf16[1,144,2152]{2,1,0:T(8,128)(2,1)}) %reduce-scatter.11.cloned.1.call-update) | async-done | bytes 619792 | tf_op jit(solution)/shard_map/reduce_scatter | solution.py:188
  (178 shorter events, 91.6 us)
Async XLA Ops:
  7.2 3.1 copy-start.22
  7.2 44.9 %all-gather.18.cloned.1.call-start = ((), (), s32[]{:S(2)}) async-start(), calls=%async_computation.10 | async-start | bytes 1658880 | tf_op jit(solution)/shard_map/all_gather | solution.py:181
  17.6 89.2 %all-gather.20.cloned.1.call-start = ((), (), s32[]{:S(2)}) async-start(), calls=%async_computation.11 | async-start | bytes 3133440 | tf_op jit(solution)/shard_map/all_gather | solution.py:181
  28.9 142.9 %all-gather.14.cloned.1.call-start = ((), (), s32[]{:S(2)}) async-start(), calls=%async_computation.4 | async-start | bytes 11943936 | tf_op jit(solution)/shard_map/all_gather | solution.py:182
  52.1 225.2 %all-gather.16.cloned.1.call-start = ((), (), s32[]{:S(2)}) async-start(), calls=%async_computation.5 | async-start | bytes 22560768 | tf_op jit(solution)/shard_map/all_gather | solution.py:182
  106.8 506.7 %reduce-scatter.5.cloned.1.call-start = ((), (), s32[]{:S(2)}) async-start(), calls=%async_computation.6 | async-start | bytes 11943936 | tf_op jit(solution)/shard_map/reduce_scatter | solution.py:187
  110.3 1.3 copy-start.39
  111.3 2.8 copy-start.8
  111.3 2.8 copy-start.35
  111.3 2.8 copy-start.37
  111.7 2.4 copy-start.33
  114.1 35.3 %copy-start.29 = (f32[768]{0:T(1024)}, f32[768]{0:T(1024)S(1)}, u32[]{:S(2)}) copy-start(f32[768]{0:T(1024)S(1)} %add_rsqrt_fusion.1) | copy-start | bytes 9220
  115.9 5.5 copy-start.44
  115.9 6.7 copy-start.40
  115.9 6.7 copy-start.42
  115.9 6.7 copy-start.43
  115.9 22.2 %copy-start.17 = (bf16[1,729,1152]{2,1,0:T(8,128)(2,1)S(1)}, bf16[1,729,1152]{2,1,0:T(8,128)(2,1)}, u32[]{:S(2)}) copy-start(bf16[1,729,1152]{2,1,0:T(8,128)(2,1)} %get-tuple-element.235) | copy-start | bytes 5038852
  143.3 1.2 copy-start.14
  196.1 1.2 copy-start.3
  213.6 1.1 copy-start.2
  231.8 16.2 %copy-start = (f32[4,768,1]{2,1,0:T(8,128)}, f32[4,768,1]{2,1,0:T(8,128)S(1)}, u32[]{:S(2)}) copy-start(f32[4,768,1]{2,1,0:T(8,128)S(1)} %get-tuple-element.92.lse) | copy-start | bytes 36868
  257.3 1.2 copy-start.27
  257.3 1.2 copy-start.38
  408.8 3.9 copy-start.12
  408.8 3.9 copy-start.15
  408.8 3.9 copy-start.26
  408.8 3.9 copy-start.28
  408.8 3.9 copy-start.32
  414.9 1.7 copy-start.10
  498.5 25.4 %copy-start.23 = (bf16[1152,1152]{1,0:T(8,128)(2,1)S(1)}, bf16[1152,1152]{1,0:T(8,128)(2,1)}, u32[]{:S(2)}) copy-start(bf16[1152,1152]{1,0:T(8,128)(2,1)} %get-tuple-element.103) | copy-start | bytes 7962628
  498.5 25.4 %copy-start.24 = (bf16[1152,1152]{1,0:T(8,128)(2,1)S(1)}, bf16[1152,1152]{1,0:T(8,128)(2,1)}, u32[]{:S(2)}) copy-start(bf16[1152,1152]{1,0:T(8,128)(2,1)} %get-tuple-element.104) | copy-start | bytes 7962628
  531.5 1.7 copy-start.18
  531.6 216.9 %reduce-scatter.9.cloned.1.call-start = ((), (), s32[]{:S(2)}) async-start(), calls=%async_computation.8 | async-start | bytes 22560768 | tf_op jit(solution)/shard_map/reduce_scatter | solution.py:187
  533.3 3.5 copy-start.19
  533.3 3.5 copy-start.20
  536.8 2.1 copy-start.21
  561.5 2.0 copy-start.16
  561.5 314.8 %all-gather.22.cloned.1.call-start = ((), (), s32[]{:S(2)}) async-start(), calls=%async_computation.12 | async-start | bytes 8478720 | tf_op jit(solution)/shard_map/all_gather | solution.py:192
  565.0 434.7 %all-gather.24.cloned.1.call-start = ((), (), s32[]{:S(2)}) async-start(), calls=%async_computation.13 | async-start | bytes 8478720 | tf_op jit(solution)/shard_map/all_gather | solution.py:192
  565.0 5.4 copy-start.9
  565.0 5.4 copy-start.30
  565.0 5.4 copy-start.34
  565.0 5.4 copy-start.36
  570.4 4.2 copy-start.11
  577.7 218.9 %copy-start.41 = (f32[1,1076]{1,0:T(1,128)S(1)}, f32[1,1076]{1,0:T(1,128)}, u32[]{:S(2)}) copy-start(f32[1,1076]{1,0:T(1,128)} %get-tuple-element.115) | copy-start | bytes 12916
  577.7 453.9 %reduce-scatter.7.cloned.1.call-start = ((), (), s32[]{:S(2)}) async-start(), calls=%async_computation.7 | async-start | bytes 1658880 | tf_op jit(solution)/shard_map/reduce_scatter | solution.py:188
  613.5 469.7 %reduce-scatter.11.cloned.1.call-start = ((), (), s32[]{:S(2)}) async-start(), calls=%async_computation.9 | async-start | bytes 3133440 | tf_op jit(solution)/shard_map/reduce_scatter | solution.py:188
  748.5 55.8 %copy-start.13 = (f32[768,1152]{1,0:T(8,128)S(1)}, f32[768,1152]{1,0:T(8,128)}, u32[]{:S(2)}) copy-start(f32[768,1152]{1,0:T(8,128)} %get-tuple-element.86) | copy-start | bytes 10616836
  (7 other events, 5.6 us)
Sparse Core Ops, SparseCore 0:
  17.7 34.3 all-gather.17
  54.2 52.5 all-gather.19
  108.7 63.0 all-gather.13
  173.6 103.6 all-gather.15
  531.7 81.7 reduce-scatter.4
  617.1 131.3 reduce-scatter.8
  750.7 125.6 all-gather.21
  878.0 121.6 all-gather.23
  1002.1 29.4 reduce-scatter.6
  1033.9 49.2 reduce-scatter.10

commit v2 on v1

v2 whole, which is shorter than its diff:
```python
import functools
import math

import jax
import jax.numpy as jnp
from jax import lax
from jax.experimental import pallas as pl
from jax.experimental.pallas import tpu as pltpu
from jax.sharding import PartitionSpec as P

HD = 72
TOK = 768
RT = 256
SC = 1 / math.sqrt(HD)
LOG2E = 1.4426950408889634
F32 = jnp.float32
BF = jnp.bfloat16
norm_eps = 1e-06
clip_limit = 3.0
tanh_coef = 0.7978845608028654
cube_coef = 0.044715
VM = pl.BlockSpec(memory_space=pltpu.VMEM)
HB = pl.BlockSpec(memory_space=pl.ANY)
MESH = pl.DeviceIdType.MESH


def nn(a, b):
    return jnp.dot(a, b, preferred_element_type=F32)


def nt(a, b):
    return lax.dot_general(a, b, (((1,), (1,)), ((), ())), preferred_element_type=F32)


def tn(a, b):
    return lax.dot_general(a, b, (((0,), (0,)), ((), ())), preferred_element_type=F32)


def shape(dims, dtype):
    return jax.ShapeDtypeStruct(dims, dtype)


def cut_rows(rows):
    first = (rows // 2 + 15) // 16 * 16
    return first, rows - first


class Plan:
    def __init__(self, number):
        self.number, self.ins, self.outs, self.copies = number, [], [], []

    def take(self, array):
        self.ins.append(array)
        return ("in", len(self.ins) - 1)

    def give(self, dims, dtype=BF):
        self.outs.append(shape(dims, dtype))
        return ("out", len(self.outs) - 1)

    def copy(self, start, until, src, src_row, dst, dst_row, size, dp=0, z=0, sends=None):
        self.copies.append((start, until, src, src_row, dst, dst_row, size, dp, z, sends))


class Bound:
    def __init__(self, plan, ins, outs, send_sem, recv_sem):
        self.plan, self.refs, self.sems = plan, {"in": ins, "out": outs}, (send_sem, recv_sem)
        self.d, self.z = lax.axis_index("dp"), lax.axis_index("tensor")

    def barrier(self, more=()):
        masks = sorted({(c[7], c[8]) for c in self.plan.copies if c[7] or c[8]} | set(more))
        if masks:
            sem = pltpu.get_barrier_semaphore()
            for dp, z in masks:
                pl.semaphore_signal(sem, inc=1, device_id=(self.d ^ dp, self.z ^ z), device_id_type=MESH)
            pl.semaphore_wait(sem, len(masks))

    def place(self, handle, row, size):
        ref = self.refs[handle[0]][handle[1]]
        row = pl.multiple_of(row(self.d), 16) if callable(row) else row
        return ref.at[pl.ds(row, size), :]

    def tick(self, t, last=False):
        todo = list(enumerate(self.plan.copies))
        for i, c in todo:
            if c[1] == t or (last and c[1] is None):
                self.one(i, c, False)
        for i, c in todo:
            if c[0] == t:
                self.one(i, c, True)

    def one(self, i, c, start):
        _, _, src, src_row, dst, dst_row, size, dp, z, sends = c
        s, r = self.sems
        a, b = self.place(src, src_row, size), self.place(dst, dst_row, size)
        if not dp and not z:
            copy = pltpu.make_async_copy(a, b, s.at[i])
            copy.start() if start else copy.wait()
            return
        copy = pltpu.make_async_remote_copy(src_ref=a, dst_ref=b, send_sem=s.at[i], recv_sem=r.at[i], device_id=(self.d ^ dp, self.z ^ z), device_id_type=MESH)
        if sends is None:
            copy.start() if start else copy.wait()
            return
        core = self.d % 2

        def any_of(z_here):
            hit = None
            for zz, cc in sends:
                this = z_here == zz
                if cc is not None:
                    this = this & (core == cc)
                hit = this if hit is None else hit | this
            return hit

        if start:
            pl.when(any_of(self.z))(copy.start)
        else:
            pl.when(any_of(self.z))(copy.wait_send)
            pl.when(any_of(self.z ^ z))(copy.wait_recv)


def plan_args(plan):
    n = max(len(plan.copies), 1)
    return [HB] * len(plan.ins), (HB,) * len(plan.outs), [pltpu.SemaphoreType.DMA((n,)), pltpu.SemaphoreType.DMA((n,))]


def params(plan, mib):
    if plan.copies:
        return pltpu.CompilerParams(vmem_limit_bytes=mib * 2**20, collective_id=plan.number, has_side_effects=True)
    return pltpu.CompilerParams(vmem_limit_bytes=mib * 2**20)


def block_rows(lhs, rhs, half, write):
    if half is None:
        @pl.loop(0, lhs.shape[0] // 384)
        def _(t):
            place = pl.ds(pl.multiple_of(t * 384, 128), 384)
            write(place, nn(lhs[place, :], rhs[...]))
    else:
        rows = lhs.shape[0] // 8
        d = lax.axis_index("dp")

        @pl.loop(0, 2)
        def _(t):
            r = 4 * t + 1 - half
            both = [lhs[pl.ds(pl.multiple_of((d ^ q) * rows, 16), rows), :] for q in (r, r + 2)]
            write(pl.ds(pl.multiple_of(t * 2 * rows, 16), 2 * rows), nn(jnp.concatenate(both, axis=0), rhs[...]))


def core_copy(src, dst, sems):
    d, z = lax.axis_index("dp"), lax.axis_index("tensor")
    return pltpu.make_async_remote_copy(src_ref=src, dst_ref=dst, send_sem=sems.at[0], recv_sem=sems.at[1], device_id=(d ^ 1, z), device_id_type=MESH)


def attn_fwd_kernel(length, heads, plan, first, qb, vb, acc_in, W_ref, *rest):
    ni, no = len(plan.ins), len(plan.outs)
    ins, (qkv, att, lse, tops, acc), rest = rest[:ni], rest[ni:ni + 5], rest[ni + 5:]
    outs, (W, sem, s_sem, r_sem) = rest[:no], rest[no:]
    net = Bound(plan, ins, outs, s_sem, r_sem)
    load = pltpu.make_async_copy(W_ref, W, sem)
    load.start()
    net.barrier()
    net.tick(0)
    load.wait()
    cw = heads * HD

    @pl.loop(0, TOK // RT)
    def _(i):
        rows = pl.ds(pl.multiple_of(i * RT, RT), RT)
        t = nn(first[rows, :], W[:, :3 * cw])
        q = (t[:, :cw] + qb[...]).astype(BF)
        k = t[:, cw:2 * cw].astype(BF)
        v = (t[:, 2 * cw:] + vb[...]).astype(BF)
        for h in range(heads):
            qkv[h, rows, :] = q[:, h * HD:(h + 1) * HD]
            qkv[heads + h, rows, :] = k[:, h * HD:(h + 1) * HD]
            qkv[2 * heads + h, rows, :] = v[:, h * HD:(h + 1) * HD]

    tops[...] = jnp.full(tops.shape, -1e30, F32)

    @pl.loop(0, TOK // RT)
    def _(i):
        for t in range(TOK // RT):
            pl.when(i == t)(functools.partial(net.tick, t + 1))
        rows = pl.ds(pl.multiple_of(i * RT, RT), RT)
        rid = lax.broadcasted_iota(jnp.int32, (RT, 1), 0) + i * RT
        cid = lax.broadcasted_iota(jnp.int32, (1, TOK), 1)
        res = []
        for h in range(heads):
            s = nt(qkv[h, rows, :], qkv[heads + h])
            s = jnp.where(cid < length, s, -1e30)
            m = jnp.max(s, axis=1, keepdims=True)
            e = jnp.exp2((s - m) * (SC * LOG2E))
            l = jnp.sum(e, axis=1, keepdims=True)
            o = nn(e.astype(BF), qkv[2 * heads + h]) * (1.0 / l)
            res.append(o.astype(BF))
            lse[h, rows, :] = m * (SC * LOG2E) + jnp.log2(l)
            tops[h:h + 1, :] = jnp.maximum(tops[h:h + 1, :], jnp.max(jnp.where(rid < length, m, -1e30)) * SC)
        a = jnp.concatenate(res, axis=1)
        att[rows, :] = a
        acc[rows, :] = acc_in[rows, :] + nt(a, W[:, 3 * cw:])

    net.tick(4)
    net.tick(5)
    net.tick(6, True)


def attn_fwd(plan, first, W, qb, vb, acc, length):
    D = first.shape[1]
    cw = W.shape[1] // 4
    heads = cw // HD
    in_p, out_p, sems = plan_args(plan)
    got = pl.pallas_call(
        functools.partial(attn_fwd_kernel, length, heads, plan),
        out_shape=(shape((3 * heads, TOK, HD), BF), shape((TOK, cw), BF), shape((heads, TOK, 1), F32), shape((heads, 128), F32), shape((TOK, D), F32), *plan.outs),
        in_specs=[VM] * 4 + [HB] + in_p,
        out_specs=(VM,) * 5 + out_p,
        scratch_shapes=[pltpu.VMEM((D, 4 * cw), BF), pltpu.SemaphoreType.DMA] + sems,
        compiler_params=params(plan, 44),
        cost_estimate=pl.CostEstimate(flops=2 * TOK * (D * cw * 4 + heads * 2 * TOK * HD * 6), bytes_accessed=25 * 2**20, transcendentals=heads * TOK * TOK),
        name="attn_fwd",
    )(first, qb, vb, acc, W, *plan.ins)
    return got[:5], got[5:]


def mlp_kernel(fw, split, plan, second, secondT, gout, goutT, eb, mlp_in, sec_in, W_ref, *rest):
    ni, no = len(plan.ins), len(plan.outs)
    ins, (G, geb, mlp, sec), rest = rest[:ni], rest[ni:ni + 4], rest[ni + 4:]
    outs, (W, E, ST, act_s, gpre_s, out_s, peer_s, sem, c_sem, s_sem, r_sem) = rest[:no], rest[no:]
    net = Bound(plan, ins, outs, s_sem, r_sem)
    load = pltpu.make_async_copy(W_ref, W, sem)
    load.start()
    if split:
        net.barrier([(1, 0)])
    net.tick(0)
    load.wait()
    cut = fw // 128 * 128
    tail = fw - cut
    E[:, :cut] = W[:, :cut]
    ST[:, :cut] = W[:, cut:2 * cut]
    last = W[:, 2 * cut:]
    blank = jnp.zeros((last.shape[0], 128 - tail), BF)
    E[:, cut:] = jnp.concatenate([last[:, :tail], blank], axis=1)
    ST[:, cut:] = jnp.concatenate([last[:, tail:], blank], axis=1)
    geb[...] = jnp.zeros_like(geb)

    @pl.loop(0, TOK // RT)
    def _(i):
        for t in range(1, TOK // RT):
            pl.when(i == t)(functools.partial(net.tick, t))
        rows = pl.ds(pl.multiple_of(i * RT, RT), RT)
        u = nn(second[rows, :], E[...]) + eb[...]
        ga = nn(gout[rows, :], ST[...])
        u2 = u * u
        t = jnp.tanh(u * (tanh_coef + (tanh_coef * cube_coef) * u2))
        hu = 0.5 * (1.0 + t)
        act_s[rows, :] = (u * hu).astype(BF)
        slope = hu + u * (0.5 * tanh_coef) * (1.0 - t * t) * (1.0 + (3.0 * cube_coef) * u2)
        gp = ga * slope
        geb[...] += jnp.sum(gp, axis=0, keepdims=True)
        gpre_s[rows, :] = gp.astype(BF)

    net.tick(3)

    def write_e(dst, peer):
        def write(place, v):
            a, b = v[:, :cut], v[:, cut:fw]
            if peer is not None:
                a = a + peer[place, :cut].astype(F32)
                b = b + peer[place, 2 * cut:2 * cut + tail].astype(F32)
            dst[place, :cut] = a.astype(BF)
            dst[place, 2 * cut:2 * cut + tail] = b.astype(BF)
        return write

    def write_s(dst, peer):
        def write(place, v):
            a, b = v[:, :cut], v[:, cut:fw]
            if peer is not None:
                a = a + peer[place, cut:2 * cut].astype(F32)
                b = b + peer[place, 2 * cut + tail:].astype(F32)
            dst[place, cut:2 * cut] = a.astype(BF)
            dst[place, 2 * cut + tail:] = b.astype(BF)
        return write

    if split:
        block_rows(secondT, gpre_s, 0, write_e(out_s, None))
        block_rows(goutT, act_s, 0, write_s(out_s, None))
        exchange = core_copy(out_s, peer_s, c_sem)
        exchange.start()

    @pl.loop(0, TOK // RT)
    def _(i):
        rows = pl.ds(pl.multiple_of(i * RT, RT), RT)
        mlp[rows, :] = mlp_in[rows, :] + nt(act_s[rows, :], ST[...])
        sec[rows, :] = sec_in[rows, :] + nt(gpre_s[rows, :], E[...])

    net.tick(4)
    if split:
        exchange.wait()
    peer = peer_s if split else None
    block_rows(secondT, gpre_s, 1 if split else None, write_e(G, peer))
    block_rows(goutT, act_s, 1 if split else None, write_s(G, peer))
    net.tick(5)
    net.tick(6, True)


def mlp_call(plan, second, secondT, gout, goutT, W, eb, mlp, sec, split):
    D = second.shape[1]
    fw = W.shape[1] // 2
    wide = fw // 128 * 128 + 128
    eb = jnp.pad(eb, ((0, 0), (0, wide - fw)))
    in_p, out_p, sems = plan_args(plan)
    side = pltpu.VMEM((D // 2, 2 * fw) if split else (16, 128), BF)
    got = pl.pallas_call(
        functools.partial(mlp_kernel, fw, split, plan),
        out_shape=(shape((D // (1 + split), 2 * fw), BF), shape((1, wide), F32), shape((TOK, D), F32), shape((TOK, D), F32), *plan.outs),
        in_specs=[VM] * 7 + [HB] + in_p,
        out_specs=(VM,) * 4 + out_p,
        scratch_shapes=[pltpu.VMEM((D, 2 * fw), BF)] + [pltpu.VMEM((D, wide), BF)] * 2 + [pltpu.VMEM((TOK, wide), BF)] * 2 + [side, side] + [pltpu.SemaphoreType.DMA, pltpu.SemaphoreType.DMA((2,))] + sems,
        compiler_params=params(plan, 56) if plan.copies or not split else pltpu.CompilerParams(vmem_limit_bytes=56 * 2**20, collective_id=plan.number, has_side_effects=True),
        cost_estimate=pl.CostEstimate(flops=2 * 9 * TOK * D * fw, bytes_accessed=35 * 2**20, transcendentals=TOK * fw),
        name="mlp",
    )(second, secondT, gout, goutT, eb, mlp, sec, W, *plan.ins)
    return got[:4], got[4:]


def attn_bwd_kernel(length, heads, split, plan, gmid, gmidT, firstT, qkv, att, lse, acc_in, W_ref, *rest):
    ni, no = len(plan.ins), len(plan.outs)
    ins, (G, gqb, gvb, acc), rest = rest[:ni], rest[ni:ni + 4], rest[ni + 4:]
    outs, (W, ga_s, d_s, dk_s, dv_s, out_s, peer_s, sem, c_sem, s_sem, r_sem) = rest[:no], rest[no:]
    net = Bound(plan, ins, outs, s_sem, r_sem)
    load = pltpu.make_async_copy(W_ref, W, sem)
    load.start()
    if split:
        net.barrier([(1, 0)])
    net.tick(0)
    load.wait()
    cw = heads * HD

    @pl.loop(0, TOK // RT)
    def _(i):
        rows = pl.ds(pl.multiple_of(i * RT, RT), RT)
        g = nn(gmid[rows, :], W[:, 3 * cw:]).astype(BF)
        for h in range(heads):
            ga_s[h, rows, :] = g[:, h * HD:(h + 1) * HD]

    gqb[...] = jnp.zeros_like(gqb)
    dk_s[...] = jnp.zeros_like(dk_s)
    dv_s[...] = jnp.zeros_like(dv_s)

    @pl.loop(0, TOK // RT)
    def _(i):
        rows = pl.ds(pl.multiple_of(i * RT, RT), RT)
        cid = lax.broadcasted_iota(jnp.int32, (1, TOK), 1)
        dqs = []
        for h in range(heads):
            q, k, v, g = qkv[h, rows, :], qkv[heads + h], qkv[2 * heads + h], ga_s[h, rows, :]
            s = nt(q, k)
            p = jnp.exp2(s * (SC * LOG2E) - lse[h, rows, :])
            p = jnp.where(cid < length, p, 0.0)
            dp = nt(g, v)
            dd = jnp.sum(g.astype(F32) * att[rows, h * HD:(h + 1) * HD].astype(F32), axis=1, keepdims=True)
            ds = (p * (dp - dd)).astype(BF)
            dqs.append(nn(ds, k) * SC)
            dk_s[h] += tn(ds, q)
            dv_s[h] += tn(p.astype(BF), g)
        dq = jnp.concatenate(dqs, axis=1)
        gqb[...] += jnp.sum(dq, axis=0, keepdims=True)
        d_s[rows, :cw] = dq.astype(BF)

    dk = jnp.concatenate([dk_s[h] * SC for h in range(heads)], axis=1)
    d_s[:, cw:2 * cw] = dk.astype(BF)
    dv = jnp.concatenate([dv_s[h] for h in range(heads)], axis=1)
    gvb[...] = jnp.sum(dv, axis=0, keepdims=True)
    d_s[:, 2 * cw:] = dv.astype(BF)

    def write(dst, peer, lo, hi):
        def put(place, v):
            if peer is not None:
                v = v + peer[place, lo:hi].astype(F32)
            dst[place, lo:hi] = v.astype(BF)
        return put

    if split:
        block_rows(firstT, d_s, 0, write(out_s, None, 0, 3 * cw))
        block_rows(gmidT, att, 0, write(out_s, None, 3 * cw, 4 * cw))
        exchange = core_copy(out_s, peer_s, c_sem)
        exchange.start()

    @pl.loop(0, TOK // RT)
    def _(i):
        rows = pl.ds(pl.multiple_of(i * RT, RT), RT)
        acc[rows, :] = acc_in[rows, :] + nt(d_s[rows, :], W[:, :3 * cw])

    if split:
        exchange.wait()
    peer = peer_s if split else None
    block_rows(firstT, d_s, 1 if split else None, write(G, peer, 0, 3 * cw))
    block_rows(gmidT, att, 1 if split else None, write(G, peer, 3 * cw, 4 * cw))
    net.tick(6, True)


def attn_bwd(plan, gmid, gmidT, firstT, W, qkv, att, lse, acc, length, split):
    D = gmid.shape[1]
    cw = W.shape[1] // 4
    heads = cw // HD
    in_p, out_p, sems = plan_args(plan)
    side = pltpu.VMEM((D // 2, 4 * cw) if split else (16, 128), BF)
    got = pl.pallas_call(
        functools.partial(attn_bwd_kernel, length, heads, split, plan),
        out_shape=(shape((D // (1 + split), 4 * cw), BF), shape((1, cw), F32), shape((1, cw), F32), shape((TOK, D), F32), *plan.outs),
        in_specs=[VM] * 7 + [HB] + in_p,
        out_specs=(VM,) * 4 + out_p,
        scratch_shapes=[pltpu.VMEM((D, 4 * cw), BF), pltpu.VMEM((heads, TOK, HD), BF), pltpu.VMEM((TOK, 3 * cw), BF), pltpu.VMEM((heads, TOK, HD), F32), pltpu.VMEM((heads, TOK, HD), F32), side, side, pltpu.SemaphoreType.DMA, pltpu.SemaphoreType.DMA((2,))] + sems,
        compiler_params=params(plan, 52) if plan.copies or not split else pltpu.CompilerParams(vmem_limit_bytes=52 * 2**20, collective_id=plan.number, has_side_effects=True),
        cost_estimate=pl.CostEstimate(flops=2 * TOK * (D * cw * 8 + heads * 5 * TOK * HD * 6), bytes_accessed=30 * 2**20, transcendentals=heads * TOK * TOK),
        name="attn_bwd",
    )(gmid, gmidT, firstT, qkv, att, lse, acc, W, *plan.ins)
    return got[:4], got[4:]


def normalize(values):
    centre = jnp.mean(values, axis=-1, keepdims=True)
    centred = values - centre
    spread = jnp.mean(centred * centred, axis=-1, keepdims=True)
    inverse = lax.rsqrt(spread + norm_eps)
    return centred * inverse, inverse


def norm_back(grad_norm, normed, inverse, gain):
    scaled = grad_norm * gain
    first_mean = jnp.mean(scaled, axis=-1, keepdims=True)
    second_mean = jnp.mean(scaled * normed, axis=-1, keepdims=True)
    grad_input = inverse * (scaled - first_mean - normed * second_mean)
    return grad_input, jnp.sum(grad_norm * normed, axis=0), jnp.sum(grad_norm, axis=0)


def slot_table(d, groups):
    z = lax.axis_index("tensor")
    middle = 1 + d % 2
    return jnp.where(z == 0, 0, jnp.where(z == groups - 1, 1, 2)), (z == 0) | (z == groups - 1) | (z == middle)


class General:
    split = 0

    def __init__(self, groups, attn_own, mlp_own):
        self.groups = groups
        self.attn, self.mlp = self.spread(attn_own), self.spread(mlp_own)

    def vectors(self, own):
        every = lax.all_gather(own, "tensor")
        return [every[i] for i in range(self.groups)]

    def spread(self, own):
        d, count = lax.axis_index("dp"), lax.axis_size("dp")
        rows = own.shape[0] // count
        piece = lax.dynamic_slice_in_dim(own, d * rows, rows, 0)
        piece = lax.all_gather(piece, "tensor")
        whole = lax.all_gather(piece, "dp", axis=1, tiled=True)
        return [whole[i] for i in range(self.groups)]

    def plan(self, name):
        return Plan(0)

    def done(self, name, got):
        pass

    def reduce(self, parts):
        part = lax.psum_scatter(jnp.stack(parts), "dp", scatter_dimension=1, tiled=True)
        return lax.psum_scatter(part, "tensor", scatter_dimension=0, tiled=True)[0].astype(F32)

    def collect(self, grad_attn, grad_mlp):
        return self.reduce(grad_attn), self.reduce(grad_mlp)

    def by_index(self, items):
        return jnp.stack(items)

    def give(self, mine):
        self.mine = mine

    def gathered(self):
        return self.share(self.mine)

    def share(self, mine):
        every = lax.all_gather(mine, "tensor")
        middle = 1 + lax.axis_index("dp") % 2
        return jnp.stack([every[0], every[self.groups - 1], lax.dynamic_index_in_dim(every, middle, 0, keepdims=False)])


BOTH_UP = ((0, None),)
HOPS = {
    "u1": (1, ((0, None),)), "u2": (3, ((1, None),)), "u3": (1, ((2, None),)),
    "w1": (1, ((3, None),)), "w2": (3, ((2, None),)), "w3": (1, ((1, None),)),
    "v1": (3, ((1, 0), (2, 1))), "v2": (1, ((2, 0), (1, 1))), "v3": (1, ((1, 0), (2, 1))),
}
HOP_FROM = {"u1": "me", "u2": "u1", "u3": "u2", "w1": "me", "w2": "w1", "w3": "w2", "v1": "me", "v2": "v1", "v3": "me"}


class Line:
    split = 1
    groups = 4
    work = {
        "A0": ("z a1", "z a2", "g a1"),
        "A1": ("g a2", "z a3", "z m1", "zl m2"),
        "A2": ("g a3", "zh m2"),
        "A3": ("g m1", "z m3"),
        "M0": ("g m2",),
        "M1": ("g m3", "r1 m0"),
        "M2": ("r2 m0", "r1 m1"),
        "M3": ("r3 m0", "r2 m1", "r1 m2"),
        "B3": ("r3 m1", "r2 m2", "r1 m3", "h u1 0", "h w1 0", "h v1 0", "h v3 0", "h v1 1", "h v3 1"),
        "B2": ("r3 m2", "r2 m3", "r1 b3", "h u2 0", "h w2 0", "h u1 1", "h w1 1", "h v2 0", "h v2 1"),
        "B1": ("r3 m3", "r2 b3", "r1 b2", "h u3 0", "h w3 0", "h u2 1", "h w2 1"),
        "B0": ("r3 b3", "r2 b2", "r1 b1", "h u3 1", "h w3 1"),
    }

    def __init__(self, groups, attn_own, mlp_own):
        d = lax.axis_index("dp")
        self.rows = attn_own.shape[0] // 8
        self.one, self.two = cut_rows(self.rows)
        self.attn, self.mlp = [attn_own, None, None, None], [mlp_own, None, None, None]
        self.piece = {}
        for name, own in (("a", attn_own), ("m", mlp_own)):
            self.piece[name + "0"] = lax.dynamic_slice_in_dim(own, d * self.rows, self.rows, 0)
        self.state, self.hops = {}, {}

    def vectors(self, own):
        return [own] + [lax.ppermute(own, "tensor", [(i, i ^ k) for i in range(4)]) for k in (1, 2, 3)]

    def plan(self, name):
        plan = Plan(list(self.work).index(name))
        self.made = made = []
        rows, one, two = self.rows, self.one, self.two
        fresh = {}
        for job in self.work[name]:
            kind, what, *more = job.split()
            if kind == "z":
                k = int(what[1])
                src = self.piece[what[0] + ("2" if k == 3 else "0")]
                out = plan.give(src.shape)
                plan.copy(0, 2 if "g " + what in self.work[name] else None, plan.take(src), 0, out, 0, rows, z=1 if k == 3 else k)
                fresh[what] = out
                made.append((self.piece, what))
            elif kind in ("zl", "zh"):
                src = self.piece[what[0] + "0"]
                lo, size = (0, two) if kind == "zl" else (two, one)
                out = plan.give((size, src.shape[1]))
                plan.copy(0, None, plan.take(src), lo, out, 0, size, z=2)
                made.append((self.piece, what + kind))
            elif kind == "g":
                t = (2, 3, 4) if what in fresh else (0, 2, 4) if name[0] == "M" else (0, 2, 3)
                src = fresh[what] if what in fresh else plan.take(self.piece[what])
                out = plan.give((rows * 8, self.piece[what[0] + "0"].shape[1]))
                at = lambda mask, off=0: lambda d: (d ^ mask) * rows + off
                plan.copy(t[0], None, src, 0, out, at(0), rows)
                for mask in (2, 4, 1):
                    plan.copy(t[0], t[1], src, 0, out, at(0), rows, dp=mask)
                plan.copy(t[1], t[2], out, at(2), out, at(2), one, dp=4)
                plan.copy(t[1], t[2], out, at(4, one), out, at(4, one), two, dp=2)
                for mask in (2, 4):
                    plan.copy(t[1], None, out, at(mask), out, at(mask), rows, dp=1)
                plan.copy(t[2], None, out, at(6), out, at(6), rows, dp=1)
                made.append((self.attn if what[0] == "a" else self.mlp, int(what[1])))
            elif kind == "r1":
                s = self.state[what]
                columns = s["h"].shape[1]
                h, ax, by = plan.take(s["h"]), plan.give((2 * one, columns)), plan.give((2 * two, columns))
                plan.copy(0, None, h, rows, ax, 0, one, dp=2)
                plan.copy(0, None, h, 3 * rows, ax, one, one, dp=2)
                plan.copy(0, None, h, 2 * rows + one, by, 0, two, dp=4)
                plan.copy(0, None, h, 3 * rows + one, by, two, two, dp=4)
                made += [(s, "ax"), (s, "by")]
            elif kind == "r2":
                s = self.state[what]
                src = self.second(s)
                t, ay, bx = plan.take(src), plan.give((one, src.shape[1])), plan.give((two, src.shape[1]))
                plan.copy(0, None, t, 0, ay, 0, one, dp=4)
                plan.copy(0, None, t, one, bx, 0, two, dp=2)
                made += [(s, "ay"), (s, "bx")]
            elif kind == "r3":
                s, k = self.state[what], int(what[1])
                s["whole"] = self.third(s)
                if k:
                    src = s["whole"].astype(BF)
                    plan.copy(0, None, plan.take(src), 0, plan.give(src.shape), 0, rows, z=k)
                    made.append((s, "z"))
            elif kind == "h":
                half = int(more[0])
                mask, sends = HOPS[what]
                begin = HOP_FROM[what]
                src = self.mine if begin == "me" else self.hops[begin, half]
                size = self.mine.shape[0] // 2
                plan.copy(0, None, plan.take(src), half * size if begin == "me" else 0, plan.give((size, src.shape[1])), 0, size, z=mask, sends=sends)
                made.append((self.hops, (what, half)))
        return plan

    def done(self, name, got):
        for (store, key), value in zip(self.made, got, strict=True):
            store[key] = value
        if name == "A2":
            self.piece["m2"] = jnp.concatenate([self.piece.pop("m2zl"), self.piece.pop("m2zh")])

    def summed(self, name, h):
        self.state[name] = {"h": h}

    def h(self, s, q, lo, hi):
        return s["h"][q * self.rows + lo:q * self.rows + hi].astype(F32)

    def second(self, s):
        one, two = self.one, self.two
        return jnp.concatenate([self.h(s, 2, 0, one) + s["ax"][one:].astype(F32), self.h(s, 1, one, self.rows) + s["by"][two:].astype(F32)]).astype(BF)

    def third(self, s):
        one, two = self.one, self.two
        a = self.h(s, 0, 0, one) + s["ax"][:one].astype(F32) + s["ay"].astype(F32)
        b = self.h(s, 0, one, self.rows) + s["by"][:two].astype(F32) + s["bx"].astype(F32)
        return jnp.concatenate([a, b])

    def dp(self, a, m):
        return lax.ppermute(a, "dp", [(i, i ^ m) for i in range(8)])

    def collect(self, grad_attn, grad_mlp):
        rows, one, two = self.rows, self.one, self.two
        out = []
        for name in ("b", "m"):
            total = None
            for k in range(4):
                s = self.state[name + str(k)]
                if "ax" not in s:
                    s["ax"] = self.dp(jnp.concatenate([s["h"][rows:rows + one], s["h"][3 * rows:3 * rows + one]]), 2)
                    s["by"] = self.dp(jnp.concatenate([s["h"][2 * rows + one:3 * rows], s["h"][3 * rows + one:]]), 4)
                if "ay" not in s:
                    t = self.second(s)
                    s["ay"], s["bx"] = self.dp(t[:one], 4), self.dp(t[one:], 2)
                if "whole" not in s:
                    s["whole"] = self.third(s)
                if k and "z" not in s:
                    s["z"] = lax.ppermute(s["whole"].astype(BF), "tensor", [(i, i ^ k) for i in range(4)])
                part = s["z"].astype(F32) if k else s["whole"]
                total = part if total is None else total + part
            out.append(total)
        return out

    def by_index(self, items):
        return jnp.take(jnp.stack(items), lax.axis_index("tensor") ^ jnp.arange(4), axis=0)

    def give(self, mine):
        self.mine = jnp.pad(mine, ((0, -mine.shape[0] % 32), (0, 0)))

    def select(self, a, g):
        z, c = lax.axis_index("tensor"), lax.axis_index("dp") % 2
        near = jnp.where(c == 0, z, 3 - z)

        def pick(who, options):
            out = options[3]
            for i in (2, 1, 0):
                out = jnp.where(who == i, options[i], out)
            return out

        return jnp.stack([pick(z, [a, g["u1"], g["u2"], g["u3"]]), pick(z, [g["w3"], g["w2"], g["w1"], a]), pick(near, [g["v3"], a, g["v1"], g["v2"]])])

    def gathered(self):
        size = self.mine.shape[0] // 2
        return jnp.concatenate([self.select(self.mine[h * size:(h + 1) * size], {n: self.hops[n, h] for n in HOPS}) for h in (0, 1)], axis=1)

    def share(self, mine):
        rows = -(-mine.shape[0] // 3 // 16) * 16
        result = []
        for start in range(0, mine.shape[0], rows):
            have = {"me": mine[start:start + rows]}
            for name in ("u1", "w1", "v1", "v3", "u2", "w2", "v2", "u3", "w3"):
                mask, sends = HOPS[name]
                pairs = [(i * 4 + s, i * 4 + (s ^ mask)) for i in range(8) for s, c in sends if c is None or c == i % 2]
                have[name] = lax.ppermute(have[HOP_FROM[name]], ("dp", "tensor"), pairs)
            result.append(self.select(have["me"], have))
        return jnp.concatenate(result, axis=1)


def shards(images, counts, cotangent, query_w, query_b, key_w, value_w, value_b, out_w, out_b, norm1_gain, norm1_shift,
           norm2_gain, norm2_shift, expand_w, expand_b, shrink_w, shrink_b):
    slots, length, width = images.shape
    groups = lax.axis_size("tensor")
    d, z = lax.axis_index("dp"), lax.axis_index("tensor")
    cw, fw = query_w.shape[1], expand_w.shape[1]
    cut = fw // 128 * 128
    slot, used = slot_table(d, groups)
    live = jnp.where(used & (slot < counts[0]), 1.0, 0.0).astype(F32)
    pad = lambda a: jnp.pad(a, ((0, TOK - length), (0, 0)))

    attn_own = jnp.concatenate([query_w, key_w, value_w, out_w.T], axis=1)
    shrink_t = shrink_w.T
    mlp_own = jnp.concatenate([expand_w[:, :cut], shrink_t[:, :cut], expand_w[:, cut:], shrink_t[:, cut:]], axis=1)
    net = (Line if (groups, lax.axis_size("dp")) == (4, 8) else General)(groups, attn_own, mlp_own)
    split = net.split
    biases = net.vectors(jnp.concatenate([query_b, value_b, expand_b]))

    x = pad(lax.dynamic_index_in_dim(images, slot, 0, keepdims=False)).astype(F32)
    gout = pad(lax.dynamic_index_in_dim(cotangent, slot, 0, keepdims=False)) * live.astype(BF)
    gout_t = gout.T
    normed1, inverse1 = normalize(x)
    first = (normed1 * norm1_gain + norm1_shift).astype(BF)
    first_t = first.T
    acc = x + out_b
    kept, tops = [], []
    for k in range(groups):
        b = biases[k]
        plan = net.plan(f"A{k}")
        (qkv, att, lse, top, acc), got = attn_fwd(plan, first, net.attn[k], b[None, :cw], b[None, cw:2 * cw], acc, length)
        net.done(f"A{k}", got)
        kept.append((qkv, att, lse))
        tops.append(top[:, 0])
    midway = acc
    normed2, inverse2 = normalize(midway)
    second = (normed2 * norm2_gain + norm2_shift).astype(BF)
    second_t = second.T
    mlp = midway + shrink_b
    sec = jnp.zeros((TOK, width), F32)
    grad_mlp, geb = [], []
    for k in range(groups):
        plan = net.plan(f"M{k}")
        (grad, g_b, mlp, sec), got = mlp_call(plan, second, second_t, gout, gout_t, net.mlp[k], biases[k][None, 2 * cw:], mlp, sec, split)
        net.done(f"M{k}", got)
        if split:
            net.summed(f"m{k}", grad)
        grad_mlp.append(grad)
        geb.append(g_b[0, :fw])
    net.give((mlp[:length] * live).astype(BF))
    back2, gn2g, gn2s = norm_back(sec, normed2, inverse2, norm2_gain)
    gout32 = gout.astype(F32)
    gmid = gout32 + back2
    gmid_low = gmid.astype(BF)
    gmid_t = gmid_low.T
    acc = jnp.zeros((TOK, width), F32)
    grad_attn, gqb, gvb = [None] * groups, [None] * groups, [None] * groups
    for k in reversed(range(groups)):
        plan = net.plan(f"B{k}")
        (grad, g_q, g_v, acc), got = attn_bwd(plan, gmid_low, gmid_t, first_t, net.attn[k], *kept[k], acc, length, split)
        net.done(f"B{k}", got)
        if split:
            net.summed(f"b{k}", grad)
        grad_attn[k], gqb[k], gvb[k] = grad, g_q[0], g_v[0]
    back1, gn1g, gn1s = norm_back(acc, normed1, inverse1, norm1_gain)
    input_grad = ((gmid + back1) * live)[:length].astype(BF)

    outputs = net.gathered()[:, :length]
    input_grads = net.share(input_grad).astype(F32)
    sum_attn, sum_mlp = net.collect(grad_attn, grad_mlp)
    flat = lambda items: net.by_index(items).reshape(-1)
    vector = jnp.concatenate([flat(gqb), flat(gvb), flat(geb), jnp.sum(gmid, axis=0), jnp.sum(gout32, axis=0), gn1g, gn1s, gn2g, gn2s])
    vector = lax.psum(vector, ("dp", "tensor"))
    part = lambda start, size: lax.dynamic_slice_in_dim(vector, start, size, 0)
    whole, hidden = cw * groups, fw * groups
    tail = [vector[2 * whole + hidden + i * width:][:width] for i in range(6)]
    logit_top = lax.pmax(jnp.where(live > 0.0, net.by_index(tops), -1e30), ("dp", "tensor"))
    logit_top = lax.dynamic_index_in_dim(logit_top, z, 0, keepdims=False)
    factor = jnp.sqrt(clip_limit / jnp.maximum(logit_top, clip_limit))
    column_factor = jnp.repeat(factor, HD)
    clipped_query = (query_w.astype(F32) * column_factor).astype(BF)
    clipped_key = (key_w.astype(F32) * column_factor).astype(BF)
    unpack = lambda a, i: jnp.concatenate([a[:, i * cut:(i + 1) * cut], a[:, 2 * cut + i * (fw - cut):][:, :fw - cut]], axis=1)
    return (outputs, input_grads, sum_attn[:, :cw], part(z * cw, cw), sum_attn[:, cw:2 * cw], sum_attn[:, 2 * cw:3 * cw], part(whole + z * cw, cw),
            sum_attn[:, 3 * cw:].T, tail[0], tail[2], tail[3], tail[4], tail[5], unpack(sum_mlp, 0), part(2 * whole + z * fw, fw), unpack(sum_mlp, 1).T,
            tail[1], clipped_query, clipped_key)


def solution(mesh):
    columns, rows, vector = P(None, "tensor"), P("tensor", None), P("tensor")
    whole = P("dp", None, None)
    return jax.shard_map(
        shards, mesh=mesh,
        in_specs=(whole, P("dp"), whole, columns, vector, columns, columns, vector, rows, P(), P(), P(), P(), P(), columns, vector, rows, P()),
        out_specs=(whole, whole, P("dp", "tensor"), vector, P("dp", "tensor"), P("dp", "tensor"), vector, P("tensor", "dp"), P(), P(), P(), P(), P(),
                   P("dp", "tensor"), vector, P("tensor", "dp"), P(), columns, columns),
        check_vma=False)
```

time: 1100 us -> 949 us (0.86)
  the two profiles are of different devices: /device:TPU:1 before, /device:TPU:18 now
where the time goes in v2:
time: 949 us; the launch traced here: 936 us
  Pallas kernels  466 us (49%)
  local copies, waits for them, and re-layouts  165 us (17%)
  other arithmetic  108 us (11%)
  blocking collectives  85.1 us (9%)
  starting transfers between devices  60.8 us (6%)
  waiting for transfers between devices  48.1 us (5%)
    pallas_call x4, Pallas kernels, attn_bwd(): pl.pallas_call(functools.partial(attn_bwd_kernel, length, heads, split, p...  186 us
    pallas_call x4, Pallas kernels, mlp_call(): pl.pallas_call(functools.partial(mlp_kernel, fw, split, plan), out_shape=...  155 us
    pallas_call x4, Pallas kernels, attn_fwd(): pl.pallas_call(functools.partial(attn_fwd_kernel, length, heads, plan), o...  124 us
    unnamed x203, local copies, waits for them, and re-layouts  50.9 us
    ppermute x27, starting transfers between devices, share(): have[name] = lax.ppermute(have[HOP_FROM[name]], ('dp', 'tensor'), pairs)  50.4 us
    psum x1, blocking collectives, shards(): vector = lax.psum(vector, ('dp', 'tensor'))  44.4 us
    pmax x1, blocking collectives, shards(): lax.pmax(jnp.where(live > 0.0, net.by_index(tops), -1e+30), ('dp', 'tenso...  40.7 us
    ppermute x27, waiting for transfers between devices, share(): have[name] = lax.ppermute(have[HOP_FROM[name]], ('dp', 'tensor'), pairs)  33.3 us
  transfers between devices with their start and end apart: 38, of which 11 were waited for; matrix products, arithmetic and copies ran while one was open for 17% of the time, Pallas kernels for 4%

profile of v2, /device:TPU:18, one launch (start us, length us, event | category | flops | bytes accessed | tf_op | source)
XLA Modules:
  0.0 936.0 jit_solution(842371910551317741)
XLA Ops:
  2.5 3.5 collective-permute-start.1
  7.4 3.3 slice.366
  12.2 4.1 copy.109
  27.8 5.2 copy.107.acc_in
  39.6 4.3 copy.146
  45.8 5.5 concatenate.92.W_ref
  52.3 8.6 concatenate.93.W_ref
  62.7 2.8 constant_dynamic-slice_fusion.1
  65.5 3.8 copy.115
  70.5 33.3 %attn_fwd.4 = (bf16[12,768,72]{2,1,0:T(8,128)(2,1)S(1)}, bf16[768,288]{1,0:T(8,128)(2,1)S(1)}, f32[4,768,1]{2,1,0:T(8,128)S(1)}, f32[4,128]{1,0:T(4,128)S(1)}, f...) custom-call(bf16[768,1152]{1,0:T(8,128)(2,1)S(1)} %copy.113.first, ...), custom_call_target="tpu_custom_call" | custom-call | flops 6115295232 | bytes 26214400 | tf_op jit(solution)/shard_map/attn_fwd/pallas_call | solution.py:212
  112.1 3.8 copy.123.gout
  119.1 38.5 %attn_fwd.5 = (bf16[12,768,72]{2,1,0:T(8,128)(2,1)S(1)}, bf16[768,288]{1,0:T(8,128)(2,1)S(1)}, f32[4,768,1]{2,1,0:T(8,128)S(1)}, f32[4,128]{1,0:T(4,128)S(1)}, f...) custom-call(bf16[768,1152]{1,0:T(8,128)(2,1)S(1)} %copy.113.first, ...), custom_call_target="tpu_custom_call" | custom-call | flops 6115295232 | bytes 26214400 | tf_op jit(solution)/shard_map/attn_fwd/pallas_call | solution.py:212
  161.0 21.4 %attn_fwd.6 = (bf16[12,768,72]{2,1,0:T(8,128)(2,1)S(1)}, bf16[768,288]{1,0:T(8,128)(2,1)S(1)}, f32[4,768,1]{2,1,0:T(8,128)S(1)}, f32[4,128]{1,0:T(4,128)S(1)}, f...) custom-call(bf16[768,1152]{1,0:T(8,128)(2,1)S(1)} %copy.113.first, ...), custom_call_target="tpu_custom_call" | custom-call | flops 6115295232 | bytes 26214400 | tf_op jit(solution)/shard_map/attn_fwd/pallas_call | solution.py:212
  187.3 31.2 %attn_fwd.7 = (bf16[12,768,72]{2,1,0:T(8,128)(2,1)S(1)}, bf16[768,288]{1,0:T(8,128)(2,1)S(1)}, f32[4,768,1]{2,1,0:T(8,128)S(1)}, f32[4,128]{1,0:T(4,128)S(1)}, f...) custom-call(bf16[768,1152]{1,0:T(8,128)(2,1)S(1)} %copy.113.first, ...), custom_call_target="tpu_custom_call" | custom-call | flops 6115295232 | bytes 26214400 | tf_op jit(solution)/shard_map/attn_fwd/pallas_call | solution.py:212
  222.8 3.4 copy.114
  226.1 4.1 broadcast_add_fusion
  234.5 4.2 copy.122.second
  244.9 40.3 %mlp.4 = (bf16[576,2152]{1,0:T(8,128)(2,1)}, f32[1,1152]{1,0:T(1,128)}, f32[768,1152]{1,0:T(8,128)}, f32[768,1152]{1,0:T(8,128)}, bf16[1152,2152]{1,0:T(8,128)(2,1)}) custom-call(bf16[768,1152]{1,0:T(8,128)(2,1)} %copy.122.second, bf16[1152,768]{1,0:T(8,128)(2,1)} %fusion.35.secondT, bf16[768,1152]{1,0:T(8,128)(2,1)} %copy.123.gout, ...), custom_call_target="tpu_custom_call" | custom-call | flops 17135566848 | bytes 36700160 | tf_op jit(solution)/shard_map/mlp/pallas_call | solution.py:313
  285.1 49.6 %mlp.5 = (bf16[576,2152]{1,0:T(8,128)(2,1)}, f32[1,1152]{1,0:T(1,128)}, f32[768,1152]{1,0:T(8,128)}, f32[768,1152]{1,0:T(8,128)}, bf16[1152,2152]{1,0:T(8,128)(2...) custom-call(bf16[768,1152]{1,0:T(8,128)(2,1)} %copy.122.second, bf16[1152,768]{1,0:T(8,128)(2,1)} %fusion.35.secondT, ...), custom_call_target="tpu_custom_call" | custom-call | flops 17135566848 | bytes 36700160 | tf_op jit(solution)/shard_map/mlp/pallas_call | solution.py:313
  337.9 32.4 %mlp.6 = (bf16[576,2152]{1,0:T(8,128)(2,1)}, f32[1,1152]{1,0:T(1,128)}, f32[768,1152]{1,0:T(8,128)}, f32[768,1152]{1,0:T(8,128)}, bf16[80,2152]{1,0:T(8,128)(2,1...) custom-call(bf16[768,1152]{1,0:T(8,128)(2,1)} %copy.122.second, ...), custom_call_target="tpu_custom_call" | custom-call | flops 17135566848 | bytes 36700160 | tf_op jit(solution)/shard_map/mlp/pallas_call | solution.py:313
  373.4 32.6 %mlp.7 = (bf16[576,2152]{1,0:T(8,128)(2,1)}, f32[1,1152]{1,0:T(1,128)}, f32[768,1152]{1,0:T(8,128)}, f32[768,1152]{1,0:T(8,128)}, bf16[80,2152]{1,0:T(8,128)(2,1...) custom-call(bf16[768,1152]{1,0:T(8,128)(2,1)} %copy.122.second, ...), custom_call_target="tpu_custom_call" | custom-call | flops 17135566848 | bytes 36700160 | tf_op jit(solution)/shard_map/mlp/pallas_call | solution.py:313
  406.0 5.2 copy.124
  411.2 3.9 multiply_reduce_fusion
  434.5 41.5 %attn_bwd.4 = (bf16[576,1152]{1,0:T(8,128)(2,1)}, f32[1,288]{1,0:T(1,128)S(1)}, f32[1,288]{1,0:T(1,128)S(1)}, f32[768,1152]{1,0:T(8,128)}, bf16[144,2152]{1,0:T(...) custom-call(bf16[768,1152]{1,0:T(8,128)(2,1)} %copy.125.gmid, ...), custom_call_target="tpu_custom_call" | custom-call | flops 14269022208 | bytes 31457280 | tf_op jit(solution)/shard_map/attn_bwd/pallas_call | solution.py:408
  480.3 55.7 %attn_bwd.5 = (bf16[576,1152]{1,0:T(8,128)(2,1)}, f32[1,288]{1,0:T(1,128)S(1)}, f32[1,288]{1,0:T(1,128)S(1)}, f32[768,1152]{1,0:T(8,128)}, bf16[144,2152]{1,0:T(...) custom-call(bf16[768,1152]{1,0:T(8,128)(2,1)} %copy.125.gmid, ...), custom_call_target="tpu_custom_call" | custom-call | flops 14269022208 | bytes 31457280 | tf_op jit(solution)/shard_map/attn_bwd/pallas_call | solution.py:408
  537.3 54.4 %attn_bwd.6 = (bf16[576,1152]{1,0:T(8,128)(2,1)}, f32[1,288]{1,0:T(1,128)S(1)}, f32[1,288]{1,0:T(1,128)S(1)}, f32[768,1152]{1,0:T(8,128)}, bf16[144,2152]{1,0:T(...) custom-call(bf16[768,1152]{1,0:T(8,128)(2,1)} %copy.125.gmid, ...), custom_call_target="tpu_custom_call" | custom-call | flops 14269022208 | bytes 31457280 | tf_op jit(solution)/shard_map/attn_bwd/pallas_call | solution.py:408
  593.9 34.8 %attn_bwd.7 = (bf16[576,1152]{1,0:T(8,128)(2,1)}, f32[1,288]{1,0:T(1,128)S(1)}, f32[1,288]{1,0:T(1,128)S(1)}, f32[768,1152]{1,0:T(8,128)}, bf16[144,1152]{1,0:T(...) custom-call(bf16[768,1152]{1,0:T(8,128)(2,1)} %copy.125.gmid, ...), custom_call_target="tpu_custom_call" | custom-call | flops 14269022208 | bytes 31457280 | tf_op jit(solution)/shard_map/attn_bwd/pallas_call | solution.py:408
  628.7 5.2 copy.129
  633.9 4.5 fusion.15
  638.5 3.2 fusion.14
  652.2 2.9 reduce_sum.137
  655.1 2.8 reduce_sum.139
  681.4 44.4 %psum.7 = f32[13520]{0:T(1024)} all-reduce(f32[13520]{0:T(1024)} %concatenate.112), channel_id=1, replica_groups=mesh['dp'=8,'tensor'=4] {'dp','tensor'}, use_global_device_ids=true, to_apply=%region_14.16 | all-reduce | flops 13520 | bytes 108160 | tf_op jit(solution)/shard_map/psum | solution.py:750
  725.8 40.7 %pmax.7 = f32[4,4]{1,0:T(4,128)S(1)} all-reduce(f32[4,4]{1,0:T(4,128)S(1)} %select_select_fusion), channel_id=1, replica_groups=mesh['dp'=8,'tensor'=4] {'dp','tensor'}, use_global_device_ids=true, to_apply=%region_15.17 | all-reduce | flops 16 | bytes 128 | tf_op jit(solution)/shard_map/pmax | solution.py:754
  789.0 3.3 collective-permute-done.34
  792.3 6.4 collective-permute-done.37
  805.2 3.0 collective-permute-start.7
  813.3 7.2 collective-permute-done.24
  824.5 7.8 collective-permute-start.25
  853.1 5.1 collective-permute-done.10
  861.6 2.9 collective-permute-done.23
  880.2 5.5 collective-permute-start.5
  889.1 4.6 collective-permute-start.16
  895.4 4.8 collective-permute-done.13
  902.3 8.7 collective-permute-done.20
  912.7 4.5 collective-permute-done.14
  918.4 4.6 maximum_convert_fusion
  923.1 12.5 %copy.145 = f32[3,729,1152]{2,1,0:T(8,128)} copy(f32[3,729,1152]{1,2,0:T(8,128)} %maximum_convert_fusion) | data formatting | bytes 20155392
  (420 shorter events, 216.8 us)
Async XLA Ops:
  2.1 114.5 %collective-permute-start = (f32[1652]{0:T(1024)}, f32[1652]{0:T(1024)}, u32[]{:S(2)}, u32[]{:S(2)}) collective-permute-start(f32[1652]{0:T(1024)} %concatenate.91), channel_id=1, source_target_pairs={{0,3},{1,2},{2,1},{3,0},{4,7},{5,6},{6,5},{7,4},{8,11},{9,10},{10,... | collective-permute-start | bytes 19832 | tf_op jit(solution)/shard_map/ppermute | solution.py:528
  2.5 114.9 %collective-permute-start.1 = (f32[1652]{0:T(1024)}, f32[1652]{0:T(1024)}, u32[]{:S(2)}, u32[]{:S(2)}) collective-permute-start(f32[1652]{0:T(1024)} %concatenate.91), channel_id=1, source_target_pairs={{0,2},{1,3},{2,0},{3,1},{4,6},{5,7},{6,4},{7,5},{8,10},{9,11},{10,... | collective-permute-start | bytes 19832 | tf_op jit(solution)/shard_map/ppermute | solution.py:528
  6.0 112.2 %collective-permute-start.2 = (f32[1652]{0:T(1024)}, f32[1652]{0:T(1024)}, u32[]{:S(2)}, u32[]{:S(2)}) collective-permute-start(f32[1652]{0:T(1024)} %concatenate.91), channel_id=1, source_target_pairs={{0,1},{1,0},{2,3},{3,2},{4,5},{5,4},{6,7},{7,6},{8,9},{9,8},{10,11... | collective-permute-start | bytes 19832 | tf_op jit(solution)/shard_map/ppermute | solution.py:528
  70.5 38.9 %copy-start.29 = (bf16[1,729,1152]{1,2,0:T(8,128)(2,1)S(1)}, bf16[1,729,1152]{1,2,0:T(8,128)(2,1)}, u32[]{:S(2)}) copy-start(bf16[1,729,1152]{1,2,0:T(8,128)(2,1)} %copy.115) | copy-start | bytes 5038852
  186.5 32.0 %copy-start = (bf16[144,2152]{1,0:T(8,128)(2,1)}, bf16[144,2152]{1,0:T(8,128)(2,1)S(1)}, u32[]{:S(2)}) copy-start(bf16[144,2152]{1,0:T(8,128)(2,1)S(1)} %constant_dynamic-update-slice_fusion.rest_1_.rest_0_) | copy-start | bytes 1859332
  434.5 41.5 %copy-start.60 = (bf16[128,2152]{1,0:T(8,128)(2,1)S(1)}, bf16[128,2152]{1,0:T(8,128)(2,1)}, u32[]{:S(2)}) copy-start(bf16[128,2152]{1,0:T(8,128)(2,1)} %get-tuple-element.169) | copy-start | bytes 1652740
  434.5 43.8 %copy-start.52 = (bf16[576,2152]{1,0:T(8,128)(2,1)S(1)}, bf16[576,2152]{1,0:T(8,128)(2,1)}, u32[]{:S(2)}) copy-start(bf16[576,2152]{1,0:T(8,128)(2,1)} %get-tuple-element.170.rest_2_) | copy-start | bytes 7437316
  480.3 56.0 %copy-start.73 = (bf16[576,1152]{1,0:T(8,128)(2,1)S(1)}, bf16[576,1152]{1,0:T(8,128)(2,1)}, u32[]{:S(2)}) copy-start(bf16[576,1152]{1,0:T(8,128)(2,1)} %get-tuple-element.180.rest_2_) | copy-start | bytes 3981316
  643.9 164.3 %collective-permute-start.21 = (bf16[217,1152]{1,0:T(8,128)(2,1)}, bf16[217,1152]{1,0:T(8,128)(2,1)}, u32[]{:S(2)}, u32[]{:S(2)}) collective-permute-start(bf16[217,1152]{1,0:T(8,128)(2,1)} %copy.130), channel_id=1, source_target_pairs={{0,1},{4,5},{8,9},{12,13},{16,17},{20,21},{24,25},{28,29}} | collective-permute-start | bytes 1499912 | tf_op jit(solution)/shard_map/ppermute | solution.py:674
  645.4 164.3 %collective-permute-start.27 = (bf16[217,1152]{1,0:T(8,128)(2,1)}, bf16[217,1152]{1,0:T(8,128)(2,1)}, u32[]{:S(2)}, u32[]{:S(2)}) collective-permute-start(bf16[217,1152]{1,0:T(8,128)(2,1)} %copy.130), channel_id=1, source_target_pairs={{1,0},{6,7},{9,8},{14,15},{17,16},{22,23},{25,24},{30,31}} | collective-permute-start | bytes 1499912 | tf_op jit(solution)/shard_map/ppermute | solution.py:674
  659.8 106.9 %copy-start.31 = (bf16[1152,288]{0,1:T(8,128)(2,1)S(1)}, bf16[1152,288]{0,1:T(8,128)(2,1)}, u32[]{:S(2)}) copy-start(bf16[1152,288]{0,1:T(8,128)(2,1)} %param.23) | copy-start | bytes 1990660
  661.7 143.5 %collective-permute-start.6 = (bf16[256,1152]{0,1:T(8,128)(2,1)}, bf16[256,1152]{0,1:T(8,128)(2,1)}, u32[]{:S(2)}, u32[]{:S(2)}) collective-permute-start(bf16[256,1152]{0,1:T(8,128)(2,1)} %slice.494), channel_id=1, source_target_pairs={{3,2},{7,6},{11,10},{15,14},{19,18},{23,22},{27,26},{31,30}} | collective-permute-start | bytes 1769480 | tf_op jit(solution)/shard_map/ppermute | solution.py:674
  663.7 122.9 %collective-permute-start.32 = (bf16[128,1152]{1,0:T(8,128)(2,1)}, bf16[128,1152]{1,0:T(8,128)(2,1)}, u32[]{:S(2)}, u32[]{:S(2)}) collective-permute-start(bf16[128,1152]{1,0:T(8,128)(2,1)} %pad_maximum_fusion.18), channel_id=1, source_target_pairs={{0,16},{4,20},{8,24},{12,28},{16,0},{20,4},{24,8},{28,12},{1,17},{... | collective-permute-start | bytes 884744 | tf_op jit(solution)/shard_map/ppermute | solution.py:620
  669.5 114.9 %collective-permute-start.35 = (bf16[64,1152]{1,0:T(8,128)(2,1)}, bf16[64,1152]{1,0:T(8,128)(2,1)}, u32[]{:S(2)}, u32[]{:S(2)}) collective-permute-start(bf16[64,1152]{1,0:T(8,128)(2,1)} %add_convert_fusion.24), channel_id=1, source_target_pairs={{0,8},{4,12},{8,0},{12,4},{16,24},{20,28},{24,16},{28,20},{1,9},{5... | collective-permute-start | bytes 442376 | tf_op jit(solution)/shard_map/ppermute | solution.py:620
  676.6 98.3 %copy-start.24 = (bf16[729,1152]{1,0:T(8,128)(2,1)S(1)}, bf16[729,1152]{1,0:T(8,128)(2,1)}, u32[]{:S(2)}) copy-start(bf16[729,1152]{1,0:T(8,128)(2,1)} %copy-done.23) | copy-start | bytes 5038852
  784.4 14.3 %collective-permute-start.37 = (bf16[144,1152]{1,0:T(8,128)(2,1)S(1)}, bf16[144,1152]{1,0:T(8,128)(2,1)S(1)}, u32[]{:S(2)}, u32[]{:S(2)}) collective-permute-start(bf16[144,1152]{1,0:T(8,128)(2,1)S(1)} %pad_maximum_fusion.17), channel_id=1, source_target_pairs={{0,2},{1,3},{2,0},{3,1},{4,6},{5,7},{6,4},{7,5},{8,10},{9,11},{10,... | collective-permute-start | bytes 995336 | tf_op jit(solution)/shard_map/ppermute | solution.py:638
  786.7 5.6 collective-permute-start.34
  792.3 8.5 collective-permute-start.30
  798.7 5.1 collective-permute-start.33
  799.9 49.9 %copy-start.27 = (bf16[768,1152]{0,1:T(8,128)(2,1)S(1)}, bf16[768,1152]{0,1:T(8,128)(2,1)}, u32[]{:S(2)}) copy-start(bf16[768,1152]{0,1:T(8,128)(2,1)} %copy-done.26) | copy-start | bytes 5308420
  800.8 33.0 %copy-start.66 = (bf16[160,1152]{1,0:T(8,128)(2,1)}, bf16[160,1152]{1,0:T(8,128)(2,1)S(1)}, u32[]{:S(2)}) copy-start(bf16[160,1152]{1,0:T(8,128)(2,1)S(1)} %collective-permute-done.30) | copy-start | bytes 1105924
  800.8 11.7 %collective-permute-start.28 = (bf16[217,1152]{1,0:T(8,128)(2,1)S(1)}, bf16[217,1152]{1,0:T(8,128)(2,1)S(1)}, u32[]{:S(2)}, u32[]{:S(2)}) collective-permute-start(bf16[217,1152]{1,0:T(8,128)(2,1)S(1)} %copy-done.61), channel_id=1, source_target_pairs={{1,2},{6,5},{9,10},{14,13},{17,18},{22,21},{25,26},{30,29}} | collective-permute-start | bytes 1499912 | tf_op jit(solution)/shard_map/ppermute | solution.py:674
  803.9 16.7 %collective-permute-start.24 = (bf16[217,1152]{1,0:T(8,128)(2,1)S(1)}, bf16[217,1152]{1,0:T(8,128)(2,1)}, u32[]{:S(2)}, u32[]{:S(2)}) collective-permute-start(bf16[217,1152]{1,0:T(8,128)(2,1)S(1)} %copy-done.61), channel_id=1, source_target_pairs={{3,2},{7,6},{11,10},{15,14},{19,18},{23,22},{27,26},{31,30}} | collective-permute-start | bytes 1499912 | tf_op jit(solution)/shard_map/ppermute | solution.py:674
  805.2 27.2 %collective-permute-start.7 = (bf16[256,1152]{0,1:T(8,128)(2,1)}, bf16[256,1152]{0,1:T(8,128)(2,1)S(1)}, u32[]{:S(2)}, u32[]{:S(2)}) collective-permute-start(bf16[256,1152]{0,1:T(8,128)(2,1)} %collective-permute-done.6), channel_id=1, source_target_pairs={{2,1},{6,5},{10,9},{14,13},{18,17},{22,21},{26,25},{30,29}} | collective-permute-start | bytes 1769480 | tf_op jit(solution)/shard_map/ppermute | solution.py:674
  808.2 35.8 %collective-permute-start.3 = (bf16[256,1152]{0,1:T(8,128)(2,1)}, bf16[256,1152]{0,1:T(8,128)(2,1)}, u32[]{:S(2)}, u32[]{:S(2)}) collective-permute-start(bf16[256,1152]{0,1:T(8,128)(2,1)} %slice.494), channel_id=1, source_target_pairs={{0,1},{4,5},{8,9},{12,13},{16,17},{20,21},{24,25},{28,29}} | collective-permute-start | bytes 1769480 | tf_op jit(solution)/shard_map/ppermute | solution.py:674
  809.7 14.8 %collective-permute-start.36 = (bf16[144,1152]{1,0:T(8,128)(2,1)S(1)}, bf16[144,1152]{1,0:T(8,128)(2,1)S(1)}, u32[]{:S(2)}, u32[]{:S(2)}) collective-permute-start(bf16[144,1152]{1,0:T(8,128)(2,1)S(1)} %pad_maximum_fusion.16), channel_id=1, source_target_pairs={{0,1},{1,0},{2,3},{3,2},{4,5},{5,4},{6,7},{7,6},{8,9},{9,8},{10,11... | collective-permute-start | bytes 995336 | tf_op jit(solution)/shard_map/ppermute | solution.py:638
  812.5 30.7 %collective-permute-start.31 = (bf16[80,1152]{1,0:T(8,128)(2,1)}, bf16[80,1152]{1,0:T(8,128)(2,1)S(1)}, u32[]{:S(2)}, u32[]{:S(2)}) collective-permute-start(bf16[80,1152]{1,0:T(8,128)(2,1)} %add_convert_fusion.18), channel_id=1, source_target_pairs={{0,16},{4,20},{8,24},{12,28},{16,0},{20,4},{24,8},{28,12},{1,17},{... | collective-permute-start | bytes 552968 | tf_op jit(solution)/shard_map/ppermute | solution.py:620
  820.5 25.8 %collective-permute-start.22 = (bf16[217,1152]{1,0:T(8,128)(2,1)}, bf16[217,1152]{1,0:T(8,128)(2,1)}, u32[]{:S(2)}, u32[]{:S(2)}) collective-permute-start(bf16[217,1152]{1,0:T(8,128)(2,1)} %collective-permute-done.21), channel_id=1, source_target_pairs={{1,2},{5,6},{9,10},{13,14},{17,18},{21,22},{25,26},{29,30}} | collective-permute-start | bytes 1499912 | tf_op jit(solution)/shard_map/ppermute | solution.py:674
  824.5 23.2 %collective-permute-start.25 = (bf16[217,1152]{1,0:T(8,128)(2,1)}, bf16[217,1152]{1,0:T(8,128)(2,1)}, u32[]{:S(2)}, u32[]{:S(2)}) collective-permute-start(bf16[217,1152]{1,0:T(8,128)(2,1)} %collective-permute-done.24), channel_id=1, source_target_pairs={{2,1},{6,5},{10,9},{14,13},{18,17},{22,21},{26,25},{30,29}} | collective-permute-start | bytes 1499912 | tf_op jit(solution)/shard_map/ppermute | solution.py:674
  832.3 16.7 %collective-permute-start.8 = (bf16[256,1152]{0,1:T(8,128)(2,1)S(1)}, bf16[256,1152]{0,1:T(8,128)(2,1)}, u32[]{:S(2)}, u32[]{:S(2)}) collective-permute-start(bf16[256,1152]{0,1:T(8,128)(2,1)S(1)} %collective-permute-done.7), channel_id=1, source_target_pairs={{1,0},{5,4},{9,8},{13,12},{17,16},{21,20},{25,24},{29,28}} | collective-permute-start | bytes 1769480 | tf_op jit(solution)/shard_map/ppermute | solution.py:674
  843.1 8.7 collective-permute-start.9
  844.0 14.3 %collective-permute-start.10 = (bf16[256,1152]{0,1:T(8,128)(2,1)}, bf16[256,1152]{0,1:T(8,128)(2,1)}, u32[]{:S(2)}, u32[]{:S(2)}) collective-permute-start(bf16[256,1152]{0,1:T(8,128)(2,1)} %slice.494), channel_id=1, source_target_pairs={{1,2},{6,5},{9,10},{14,13},{17,18},{22,21},{25,26},{30,29}} | collective-permute-start | bytes 1769480 | tf_op jit(solution)/shard_map/ppermute | solution.py:674
  846.4 14.0 %collective-permute-start.29 = (bf16[217,1152]{1,0:T(8,128)(2,1)}, bf16[217,1152]{1,0:T(8,128)(2,1)S(1)}, u32[]{:S(2)}, u32[]{:S(2)}) collective-permute-start(bf16[217,1152]{1,0:T(8,128)(2,1)} %copy-done.62), channel_id=1, source_target_pairs={{2,3},{5,4},{10,11},{13,12},{18,19},{21,20},{26,27},{29,28}} | collective-permute-start | bytes 1499912 | tf_op jit(solution)/shard_map/ppermute | solution.py:674
  847.7 16.8 %collective-permute-start.23 = (bf16[217,1152]{1,0:T(8,128)(2,1)}, bf16[217,1152]{1,0:T(8,128)(2,1)S(1)}, u32[]{:S(2)}, u32[]{:S(2)}) collective-permute-start(bf16[217,1152]{1,0:T(8,128)(2,1)} %collective-permute-done.22), channel_id=1, source_target_pairs={{2,3},{6,7},{10,11},{14,15},{18,19},{22,23},{26,27},{30,31}} | collective-permute-start | bytes 1499912 | tf_op jit(solution)/shard_map/ppermute | solution.py:674
  849.1 17.0 %collective-permute-start.26 = (bf16[217,1152]{1,0:T(8,128)(2,1)}, bf16[217,1152]{1,0:T(8,128)(2,1)S(1)}, u32[]{:S(2)}, u32[]{:S(2)}) collective-permute-start(bf16[217,1152]{1,0:T(8,128)(2,1)} %collective-permute-done.25), channel_id=1, source_target_pairs={{1,0},{5,4},{9,8},{13,12},{17,16},{21,20},{25,24},{29,28}} | collective-permute-start | bytes 1499912 | tf_op jit(solution)/shard_map/ppermute | solution.py:674
  851.8 28.4 %collective-permute-start.4 = (bf16[256,1152]{0,1:T(8,128)(2,1)}, bf16[256,1152]{0,1:T(8,128)(2,1)}, u32[]{:S(2)}, u32[]{:S(2)}) collective-permute-start(bf16[256,1152]{0,1:T(8,128)(2,1)} %collective-permute-done.3), channel_id=1, source_target_pairs={{1,2},{5,6},{9,10},{13,14},{17,18},{21,22},{25,26},{29,30}} | collective-permute-start | bytes 1769480 | tf_op jit(solution)/shard_map/ppermute | solution.py:674
  858.2 27.5 %collective-permute-start.11 = (bf16[256,1152]{0,1:T(8,128)(2,1)}, bf16[256,1152]{0,1:T(8,128)(2,1)}, u32[]{:S(2)}, u32[]{:S(2)}) collective-permute-start(bf16[256,1152]{0,1:T(8,128)(2,1)} %collective-permute-done.10), channel_id=1, source_target_pairs={{2,3},{5,4},{10,11},{13,12},{18,19},{21,20},{26,27},{29,28}} | collective-permute-start | bytes 1769480 | tf_op jit(solution)/shard_map/ppermute | solution.py:674
  860.4 26.1 %collective-permute-start.19 = (bf16[256,1152]{0,1:T(8,128)(2,1)}, bf16[256,1152]{0,1:T(8,128)(2,1)}, u32[]{:S(2)}, u32[]{:S(2)}) collective-permute-start(bf16[256,1152]{0,1:T(8,128)(2,1)} %get-tuple-element.317), channel_id=1, source_target_pairs={{1,2},{6,5},{9,10},{14,13},{17,18},{22,21},{25,26},{30,29}} | collective-permute-start | bytes 1769480 | tf_op jit(solution)/shard_map/ppermute | solution.py:674
  864.6 23.2 %collective-permute-start.12 = (bf16[256,1152]{0,1:T(8,128)(2,1)}, bf16[256,1152]{0,1:T(8,128)(2,1)}, u32[]{:S(2)}, u32[]{:S(2)}) collective-permute-start(bf16[256,1152]{0,1:T(8,128)(2,1)} %get-tuple-element.317), channel_id=1, source_target_pairs={{0,1},{4,5},{8,9},{12,13},{16,17},{20,21},{24,25},{28,29}} | collective-permute-start | bytes 1769480 | tf_op jit(solution)/shard_map/ppermute | solution.py:674
  866.1 23.0 %collective-permute-start.15 = (bf16[256,1152]{0,1:T(8,128)(2,1)}, bf16[256,1152]{0,1:T(8,128)(2,1)}, u32[]{:S(2)}, u32[]{:S(2)}) collective-permute-start(bf16[256,1152]{0,1:T(8,128)(2,1)} %get-tuple-element.317), channel_id=1, source_target_pairs={{3,2},{7,6},{11,10},{15,14},{19,18},{23,22},{27,26},{31,30}} | collective-permute-start | bytes 1769480 | tf_op jit(solution)/shard_map/ppermute | solution.py:674
  880.2 30.8 %copy-start.54 = (bf16[256,1152]{0,1:T(8,128)(2,1)S(1)}, bf16[256,1152]{0,1:T(8,128)(2,1)}, u32[]{:S(2)}) copy-start(bf16[256,1152]{0,1:T(8,128)(2,1)} %copy-done.53) | copy-start | bytes 1769476
  880.2 22.1 %collective-permute-start.5 = (bf16[256,1152]{0,1:T(8,128)(2,1)}, bf16[256,1152]{0,1:T(8,128)(2,1)S(1)}, u32[]{:S(2)}, u32[]{:S(2)}) collective-permute-start(bf16[256,1152]{0,1:T(8,128)(2,1)} %collective-permute-done.4), channel_id=1, source_target_pairs={{2,3},{6,7},{10,11},{14,15},{18,19},{22,23},{26,27},{30,31}} | collective-permute-start | bytes 1769480 | tf_op jit(solution)/shard_map/ppermute | solution.py:674
  885.7 16.6 %collective-permute-start.18 = (bf16[256,1152]{0,1:T(8,128)(2,1)}, bf16[256,1152]{0,1:T(8,128)(2,1)S(1)}, u32[]{:S(2)}, u32[]{:S(2)}) collective-permute-start(bf16[256,1152]{0,1:T(8,128)(2,1)} %get-tuple-element.317), channel_id=1, source_target_pairs={{1,0},{6,7},{9,8},{14,15},{17,16},{22,23},{25,24},{30,31}} | collective-permute-start | bytes 1769480 | tf_op jit(solution)/shard_map/ppermute | solution.py:674
  886.4 24.5 %collective-permute-start.20 = (bf16[256,1152]{0,1:T(8,128)(2,1)}, bf16[256,1152]{0,1:T(8,128)(2,1)S(1)}, u32[]{:S(2)}, u32[]{:S(2)}) collective-permute-start(bf16[256,1152]{0,1:T(8,128)(2,1)} %collective-permute-done.19), channel_id=1, source_target_pairs={{2,3},{5,4},{10,11},{13,12},{18,19},{21,20},{26,27},{29,28}} | collective-permute-start | bytes 1769480 | tf_op jit(solution)/shard_map/ppermute | solution.py:674
  887.8 12.4 %collective-permute-start.13 = (bf16[256,1152]{0,1:T(8,128)(2,1)}, bf16[256,1152]{0,1:T(8,128)(2,1)S(1)}, u32[]{:S(2)}, u32[]{:S(2)}) collective-permute-start(bf16[256,1152]{0,1:T(8,128)(2,1)} %collective-permute-done.12), channel_id=1, source_target_pairs={{1,2},{5,6},{9,10},{13,14},{17,18},{21,22},{25,26},{29,30}} | collective-permute-start | bytes 1769480 | tf_op jit(solution)/shard_map/ppermute | solution.py:674
  889.1 12.5 %collective-permute-start.16 = (bf16[256,1152]{0,1:T(8,128)(2,1)}, bf16[256,1152]{0,1:T(8,128)(2,1)S(1)}, u32[]{:S(2)}, u32[]{:S(2)}) collective-permute-start(bf16[256,1152]{0,1:T(8,128)(2,1)} %collective-permute-done.15), channel_id=1, source_target_pairs={{2,1},{6,5},{10,9},{14,13},{18,17},{22,21},{26,25},{30,29}} | collective-permute-start | bytes 1769480 | tf_op jit(solution)/shard_map/ppermute | solution.py:674
  900.2 16.9 %collective-permute-start.14 = (bf16[256,1152]{0,1:T(8,128)(2,1)S(1)}, bf16[256,1152]{0,1:T(8,128)(2,1)S(1)}, u32[]{:S(2)}, u32[]{:S(2)}) collective-permute-start(bf16[256,1152]{0,1:T(8,128)(2,1)S(1)} %collective-permute-done.13), channel_id=1, source_target_pairs={{2,3},{6,7},{10,11},{14,15},{18,19},{22,23},{26,27},{30,31}} | collective-permute-start | bytes 1769480 | tf_op jit(solution)/shard_map/ppermute | solution.py:674
  901.6 15.6 %collective-permute-start.17 = (bf16[256,1152]{0,1:T(8,128)(2,1)S(1)}, bf16[256,1152]{0,1:T(8,128)(2,1)S(1)}, u32[]{:S(2)}, u32[]{:S(2)}) collective-permute-start(bf16[256,1152]{0,1:T(8,128)(2,1)S(1)} %collective-permute-done.16), channel_id=1, source_target_pairs={{1,0},{5,4},{9,8},{13,12},{17,16},{21,20},{25,24},{29,28}} | collective-permute-start | bytes 1769480 | tf_op jit(solution)/shard_map/ppermute | solution.py:674
  (87 other events, 470.2 us)

commit v3 on v2

--- a/solution.py
+++ b/solution.py
@@ -193,7 +193,7 @@
             l = jnp.sum(e, axis=1, keepdims=True)
             o = nn(e.astype(BF), qkv[2 * heads + h]) * (1.0 / l)
             res.append(o.astype(BF))
-            lse[h, rows, :] = m * (SC * LOG2E) + jnp.log2(l)
+            lse[rows, h:h + 1] = m * (SC * LOG2E) + jnp.log2(l)
             tops[h:h + 1, :] = jnp.maximum(tops[h:h + 1, :], jnp.max(jnp.where(rid < length, m, -1e30)) * SC)
         a = jnp.concatenate(res, axis=1)
         att[rows, :] = a
@@ -211,7 +211,7 @@
     in_p, out_p, sems = plan_args(plan)
     got = pl.pallas_call(
         functools.partial(attn_fwd_kernel, length, heads, plan),
-        out_shape=(shape((3 * heads, TOK, HD), BF), shape((TOK, cw), BF), shape((heads, TOK, 1), F32), shape((heads, 128), F32), shape((TOK, D), F32), *plan.outs),
+        out_shape=(shape((3 * heads, TOK, HD), BF), shape((TOK, cw), BF), shape((TOK, 128), F32), shape((heads, 128), F32), shape((TOK, D), F32), *plan.outs),
         in_specs=[VM] * 4 + [HB] + in_p,
         out_specs=(VM,) * 5 + out_p,
         scratch_shapes=[pltpu.VMEM((D, 4 * cw), BF), pltpu.SemaphoreType.DMA] + sems,
@@ -355,7 +355,7 @@
         for h in range(heads):
             q, k, v, g = qkv[h, rows, :], qkv[heads + h], qkv[2 * heads + h], ga_s[h, rows, :]
             s = nt(q, k)
-            p = jnp.exp2(s * (SC * LOG2E) - lse[h, rows, :])
+            p = jnp.exp2(s * (SC * LOG2E) - lse[rows, h:h + 1])
             p = jnp.where(cid < length, p, 0.0)
             dp = nt(g, v)
             dd = jnp.sum(g.astype(F32) * att[rows, h * HD:(h + 1) * HD].astype(F32), axis=1, keepdims=True)
@@ -440,6 +440,401 @@
     return jnp.where(z == 0, 0, jnp.where(z == groups - 1, 1, 2)), (z == 0) | (z == groups - 1) | (z == middle)
 
 
+HOPS = {
+    "u1": (1, ((0, None),)), "u2": (3, ((1, None),)), "u3": (1, ((2, None),)),
+    "w1": (1, ((3, None),)), "w2": (3, ((2, None),)), "w3": (1, ((1, None),)),
+    "v1": (3, ((1, 0), (2, 1))), "v2": (1, ((2, 0), (1, 1))), "v3": (1, ((1, 0), (2, 1))),
+}
+HOP_FROM = {"u1": "me", "u2": "u1", "u3": "u2", "w1": "me", "w2": "w1", "w3": "w2", "v1": "me", "v2": "v1", "v3": "me"}
+NAMES = ("u1", "w1", "v1", "v3"), ("u2", "w2", "v2"), ("u3", "w3")
+BEGIN = {"u": 0, "w": 1, "v": 2}
+
+
+class Wires:
+    def __init__(self, s_sem, r_sem):
+        self.s, self.r, self.n = s_sem, r_sem, 0
+        self.d, self.z = lax.axis_index("dp"), lax.axis_index("tensor")
+
+    def local(self, src, dst, used):
+        i = self.n
+        self.n += 1
+        make = lambda: pltpu.make_async_copy(src, dst, self.s.at[i])
+        return (lambda: pl.when(used)(lambda: make().start())), (lambda: pl.when(used)(lambda: make().wait()))
+
+    def swap(self, src, dst, dp=0, z=0, sends=None):
+        i = self.n
+        self.n += 1
+        make = lambda: pltpu.make_async_remote_copy(src_ref=src, dst_ref=dst, send_sem=self.s.at[i], recv_sem=self.r.at[i], device_id=(self.d ^ dp, self.z ^ z), device_id_type=MESH)
+        if sends is None:
+            return (lambda: make().start()), (lambda: make().wait())
+
+        def any_of(z_here):
+            hit = None
+            for zz, cc in sends:
+                this = z_here == zz
+                if cc is not None:
+                    this = this & (self.d % 2 == cc)
+                hit = this if hit is None else hit | this
+            return hit
+
+        def start():
+            pl.when(any_of(self.z))(lambda: make().start())
+
+        def wait():
+            pl.when(any_of(self.z))(lambda: make().wait_send())
+            pl.when(any_of(self.z ^ z))(lambda: make().wait_recv())
+
+        return start, wait
+
+
+def greet(d, z, masks):
+    sem = pltpu.get_barrier_semaphore()
+    for dp, t in masks:
+        pl.semaphore_signal(sem, inc=1, device_id=(d ^ dp, z ^ t), device_id_type=MESH)
+    pl.semaphore_wait(sem, len(masks))
+
+
+class Summing:
+    def __init__(self, wires, H, land, zr, k):
+        self.H, self.k = H, k
+        self.rows = r = H.shape[0] // 4
+        self.one, self.two = one, two = cut_rows(r)
+        ax, by = land.at[pl.ds(0, 2 * one), :], land.at[pl.ds(2 * one, 2 * two), :]
+        ay, bx = land.at[pl.ds(2 * r, one), :], land.at[pl.ds(2 * r + one, two), :]
+        self.land = land
+        h = lambda lo, n: H.at[pl.ds(lo, n), :]
+        at = lambda ref, lo, n: ref.at[pl.ds(lo, n), :]
+        self.c1 = [wires.swap(h(r, one), at(land, 0, one), dp=2), wires.swap(h(3 * r, one), at(land, one, one), dp=2),
+                   wires.swap(h(2 * r + one, two), at(land, 2 * one, two), dp=4), wires.swap(h(3 * r + one, two), at(land, 2 * one + two, two), dp=4)]
+        self.c2 = [wires.swap(h(2 * r, one), ay, dp=4), wires.swap(h(r + one, two), bx, dp=2)]
+        self.c3 = [wires.swap(h(0, r), zr, z=k)] if k else []
+
+    def add(self, lo, n, *froms):
+        total = self.H[lo:lo + n, :].astype(F32)
+        for f in froms:
+            total = total + self.land[f:f + n, :].astype(F32)
+        self.H[lo:lo + n, :] = total.astype(BF)
+
+    def step1(self):
+        for s, _ in self.c1:
+            s()
+
+    def step2(self):
+        r, one, two = self.rows, self.one, self.two
+        for _, w in self.c1:
+            w()
+        self.add(2 * r, one, one)
+        self.add(r + one, two, 2 * one + two)
+        for s, _ in self.c2:
+            s()
+
+    def step3(self):
+        r, one, two = self.rows, self.one, self.two
+        for _, w in self.c2:
+            w()
+        self.add(0, one, 0, 2 * r)
+        self.add(one, two, 2 * one, 2 * r + one)
+        for s, _ in self.c3:
+            s()
+
+    def step4(self):
+        for _, w in self.c3:
+            w()
+
+
+class Sharing:
+    def __init__(self, wires, mine, O, chunks):
+        self.stages = []
+        for lo, n in chunks:
+            here = []
+            for names in NAMES:
+                row = []
+                for name in names:
+                    mask, sends = HOPS[name]
+                    place = O.at[pl.ds(BEGIN[name[0]] * TOK + lo, n), :]
+                    row.append(wires.swap(mine.at[pl.ds(lo, n), :] if HOP_FROM[name] == "me" else place, place, z=mask, sends=sends))
+                here.append(row)
+            self.stages.append(here)
+
+    def start(self, chunk, stage):
+        for s, _ in self.stages[chunk][stage]:
+            s()
+
+    def wait(self, chunk, stage):
+        for _, w in self.stages[chunk][stage]:
+            w()
+
+    def on(self, chunk, stage):
+        self.wait(chunk, stage - 1)
+        self.start(chunk, stage)
+
+
+OUT_CHUNKS = ((0, 256), (256, 256), (512, 224))
+IN_CHUNKS = ((0, 128), (128, 128), (256, 128), (384, 128), (512, 128), (640, 96))
+MASKS = [(1, 0), (2, 0), (4, 0), (0, 1), (0, 2), (0, 3)]
+COPIES = 180
+
+
+def back_kernel(length, heads, gain1, gain2, live, geb, tops, gout, midway, sec, firstT, x, mine, whole0, whole1, h2, h3, *rest):
+    Ws, qkvs, atts, lses, rest = rest[:4], rest[4:8], rest[8:12], rest[12:16], rest[16:]
+    (O_out, O_in, sum_a, sum_m, vec, g_s, gm_s, acc, gT, fT, x_s, W_s, Wo, qkv_s, att_s, lse_s, ga_s, d_s, dk_s, dv_s, out_s,
+     Ha, La, Hm, Lm, za, zm, vr, w0_s, w1_s, l_sem, s_sem, r_sem) = rest
+    cw = heads * HD
+    D = g_s.shape[1]
+    wires = Wires(s_sem, r_sem)
+    d, z = wires.d, wires.z
+    loads = {}
+    order = [3, 2, 1, 0]
+    names = iter(range(100))
+
+    def load(key, src, dst):
+        loads[key] = pltpu.make_async_copy(src, dst, l_sem.at[next(names)])
+
+    load("midway", midway, acc)
+    load("sec", sec, gm_s)
+    load("gout", gout, g_s)
+    load("firstT", firstT, fT)
+    load("x", x, x_s)
+    load("h2", h2, Hm.at[0])
+    load("h3", h3, Hm.at[1])
+    load("w0", whole0, w0_s)
+    load("w1", whole1, w1_s)
+    for i, k in enumerate(order):
+        b = i % 2
+        load(f"W{i}", Ws[k], W_s.at[b])
+        load(f"qkv{i}", qkvs[k], qkv_s.at[b])
+        load(f"att{i}", atts[k], att_s.at[b])
+        load(f"lse{i}", lses[k], lse_s.at[b])
+    for key in ("midway", "sec", "gout", "h2", "h3", "w1", "w0", "firstT", "W0", "qkv0", "att0", "lse0", "x"):
+        loads[key].start()
+    slot = jnp.where(z == 0, 0, jnp.where(z == 3, 1, 2))
+    own_place = pl.ds(pl.multiple_of(slot * TOK, 256), TOK)
+    used = (z == 0) | (z == 3) | (z == 1 + d % 2)
+    own_out, own_in = wires.local(mine, O_out.at[own_place, :], used), wires.local(g_s, O_in.at[own_place, :], used)
+    share_out = Sharing(wires, mine, O_out, OUT_CHUNKS)
+    share_in = Sharing(wires, g_s, O_in, IN_CHUNKS)
+    sums = {"m2": Summing(wires, Hm.at[0], Lm.at[0], zm.at[1], 2), "m3": Summing(wires, Hm.at[1], Lm.at[1], zm.at[2], 3)}
+    for k in range(4):
+        sums[f"b{k}"] = Summing(wires, Ha.at[k], La.at[k], za.at[max(k - 1, 0)], k)
+    z_m1 = wires.swap(w1_s, zm.at[0], z=1)
+    exchange = {k: wires.swap(out_s, Ha.at[k], dp=1) for k in range(4)}
+    spread = [wires.swap(vec, vr.at[i], dp=dp, z=t) for i, (dp, t) in enumerate(((1, 0), (2, 0), (4, 0), (0, 1), (0, 2)))]
+    greet(d, z, MASKS)
+
+    todo = {
+        -3: [lambda: share_out.start(0, 0), own_out[0]],
+        -2: [lambda: loads["h2"].wait(), sums["m2"].step1, lambda: loads["w1"].wait(), z_m1[0]],
+        0: [lambda: loads["h3"].wait(), lambda: loads["w0"].wait()],
+        2: [lambda: share_out.on(0, 1), lambda: share_out.start(1, 0)],
+        3: [sums["m2"].step2, sums["m3"].step1],
+        5: [sums["m2"].step3],
+        8: [sums["b3"].step1, lambda: share_out.on(0, 2), lambda: share_out.on(1, 1), lambda: share_out.start(2, 0)],
+        12: [sums["m3"].step2],
+        13: [sums["b3"].step2],
+        15: [sums["m3"].step3, sums["b3"].step3],
+        18: [sums["b2"].step1, lambda: share_out.on(1, 2), lambda: share_out.on(2, 1)],
+        23: [sums["b2"].step2],
+        25: [sums["b2"].step3],
+        28: [sums["b1"].step1, lambda: share_out.on(2, 2)],
+        33: [sums["b1"].step2],
+        35: [sums["b1"].step3],
+        38: [sums["b0"].step1],
+    }
+
+    def tick(t):
+        for action in todo.get(t, ()):
+            action()
+
+    vec[...] = jnp.zeros_like(vec)
+    for key in ("midway", "sec", "gout"):
+        loads[key].wait()
+
+    def total_of(row, value):
+        vec[row:row + 1, :D] += jnp.sum(value, axis=0, keepdims=True)
+
+    def put_row(where, lo, value):
+        n = value.shape[1]
+        hit = lax.broadcasted_iota(jnp.int32, (8, n), 0) == where
+        vec[0:8, lo:lo + n] += jnp.where(hit, jnp.broadcast_to(value, (8, n)), 0.0)
+
+    @pl.loop(0, TOK // RT)
+    def _(i):
+        for t in range(3):
+            pl.when(i == t)(functools.partial(tick, t - 3))
+        rows = pl.ds(pl.multiple_of(i * RT, RT), RT)
+        normed, inverse = normalize(acc[rows, :])
+        e = gm_s[rows, :]
+        go = g_s[rows, :].astype(F32)
+        scaled = e * gain2[...]
+        mean1 = jnp.mean(scaled, axis=-1, keepdims=True)
+        mean2 = jnp.mean(scaled * normed, axis=-1, keepdims=True)
+        gm = go + inverse * (scaled - mean1 - normed * mean2)
+        total_of(4, gm)
+        total_of(5, go)
+        total_of(8, e * normed)
+        total_of(9, e)
+        gm_s[rows, :] = gm
+        g_s[rows, :] = gm.astype(BF)
+        gT[:, rows] = gm.T.astype(BF)
+
+    loads["firstT"].wait()
+    acc[...] = jnp.zeros_like(acc)
+    for i, k in enumerate(order):
+        base, b = 10 * i, i % 2
+        W, qkv, att, lse, H = W_s.at[b], qkv_s.at[b], att_s.at[b], lse_s.at[b], Ha.at[k]
+        for key in ("W", "qkv", "att", "lse"):
+            loads[f"{key}{i}"].wait()
+        if i < 3:
+            for key in ("W", "qkv", "att", "lse"):
+                loads[f"{key}{i + 1}"].start()
+        tick(base)
+        Wo[...] = W[:, 3 * cw:]
+
+        @pl.loop(0, TOK // RT)
+        def _(t):
+            rows = pl.ds(pl.multiple_of(t * RT, RT), RT)
+            g = nn(g_s[rows, :], Wo[...]).astype(BF)
+            for h in range(heads):
+                ga_s[h, rows, :] = g[:, h * HD:(h + 1) * HD]
+
+        tick(base + 1)
+        dk_s[...] = jnp.zeros_like(dk_s)
+        dv_s[...] = jnp.zeros_like(dv_s)
+        place = z ^ k
+
+        @pl.loop(0, TOK // RT)
+        def _(t):
+            for n in range(3):
+                pl.when(t == n)(functools.partial(tick, base + 2 + n))
+            rows = pl.ds(pl.multiple_of(t * RT, RT), RT)
+            cid = lax.broadcasted_iota(jnp.int32, (1, TOK), 1)
+            dqs = []
+            for h in range(heads):
+                q, kk, v, g = qkv[h, rows, :], qkv[heads + h], qkv[2 * heads + h], ga_s[h, rows, :]
+                s = nt(q, kk)
+                p = jnp.exp2(s * (SC * LOG2E) - lse[rows, h:h + 1])
+                p = jnp.where(cid < length, p, 0.0)
+                dp = nt(g, v)
+                dd = jnp.sum(g.astype(F32) * att[rows, h * HD:(h + 1) * HD].astype(F32), axis=1, keepdims=True)
+                ds = (p * (dp - dd)).astype(BF)
+                dqs.append(nn(ds, kk) * SC)
+                dk_s[h] += tn(ds, q)
+                dv_s[h] += tn(p.astype(BF), g)
+            dq = jnp.concatenate(dqs, axis=1)
+            put_row(place, 0, jnp.sum(dq, axis=0, keepdims=True))
+            d_s[rows, :cw] = dq.astype(BF)
+
+        d_s[:, cw:2 * cw] = jnp.concatenate([dk_s[h] * SC for h in range(heads)], axis=1).astype(BF)
+        dv = jnp.concatenate([dv_s[h] for h in range(heads)], axis=1)
+        put_row(place, 384, jnp.sum(dv, axis=0, keepdims=True))
+        d_s[:, 2 * cw:] = dv.astype(BF)
+        put_row(place, 768, geb[k])
+        put_row(place, 1920, tops[k])
+        tick(base + 5)
+
+        def write(dst, lo, hi, add):
+            def put(where, val):
+                if add:
+                    val = val + dst[where, lo:hi].astype(F32)
+                dst[where, lo:hi] = val.astype(BF)
+            return put
+
+        block_rows(fT, d_s, 0, write(out_s, 0, 3 * cw, False))
+        block_rows(gT, att, 0, write(out_s, 3 * cw, 4 * cw, False))
+        exchange[k][0]()
+        tick(base + 6)
+
+        @pl.loop(0, TOK // RT)
+        def _(t):
+            rows = pl.ds(pl.multiple_of(t * RT, RT), RT)
+            acc[rows, :] += nt(d_s[rows, :], W[:, :3 * cw])
+
+        tick(base + 7)
+        exchange[k][1]()
+        block_rows(fT, d_s, 1, write(H, 0, 3 * cw, True))
+        block_rows(gT, att, 1, write(H, 3 * cw, 4 * cw, True))
+        tick(base + 8)
+
+    loads["x"].wait()
+
+    @pl.loop(0, TOK // RT)
+    def _(i):
+        rows = pl.ds(pl.multiple_of(i * RT, RT), RT)
+        normed, inverse = normalize(x_s[rows, :].astype(F32))
+        e = acc[rows, :]
+        scaled = e * gain1[...]
+        mean1 = jnp.mean(scaled, axis=-1, keepdims=True)
+        mean2 = jnp.mean(scaled * normed, axis=-1, keepdims=True)
+        total_of(6, e * normed)
+        total_of(7, e)
+        g_s[rows, :] = ((gm_s[rows, :] + inverse * (scaled - mean1 - normed * mean2)) * live[...]).astype(BF)
+        for t in range(3):
+            @pl.when(i == t)
+            def _():
+                share_in.start(2 * t, 0)
+                share_in.start(2 * t + 1, 0)
+
+    own_in[0]()
+    after = {0: [spread[0][0], sums["b0"].step2], 1: [], 2: [sums["b0"].step3]}
+    row = lax.broadcasted_iota(jnp.int32, vec.shape, 1)
+
+    def fold(i):
+        spread[i][1]()
+        a, c = vec[...], vr[i]
+        vec[...] = jnp.where(row < 1920, a + c, jnp.maximum(a, c))
+        if i < 4:
+            spread[i + 1][0]()
+
+    n = len(IN_CHUNKS)
+    for t in range(n + 2):
+        if t < n:
+            share_in.on(t, 1)
+        for action in after.get(t, ()):
+            action()
+        if 1 <= t <= n:
+            share_in.on(t - 1, 2)
+        if 1 <= t <= 5:
+            fold(t - 1)
+    for c in range(3):
+        share_out.wait(c, 2)
+    own_out[1]()
+    own_in[1]()
+    z_m1[1]()
+    for s in ("m2", "m3", "b3", "b2", "b1"):
+        sums[s].step4()
+    r = sum_a.shape[0]
+    sum_a[...] = Ha[0, :r, :].astype(F32) + za[0].astype(F32) + za[1].astype(F32) + za[2].astype(F32)
+    sum_m[...] = w0_s[...] + zm[0].astype(F32) + zm[1].astype(F32) + zm[2].astype(F32)
+    for c in range(n):
+        share_in.wait(c, 2)
+
+
+def back(number, gain1, gain2, live, geb, tops, gout, midway, sec, firstT, x, mine, whole0, whole1, h2, h3, kept, Ws, length):
+    D = gout.shape[1]
+    cw = Ws[0].shape[1] // 4
+    cm = h2.shape[1]
+    heads = cw // HD
+    r = D // 8
+    qkvs, atts, lses = zip(*kept)
+    vm = pltpu.VMEM
+    dma = pltpu.SemaphoreType.DMA
+    return pl.pallas_call(
+        functools.partial(back_kernel, length, heads),
+        out_shape=(shape((3 * TOK, D), BF), shape((3 * TOK, D), BF), shape((r, 4 * cw), F32), shape((r, cm), F32), shape((16, 2048), F32)),
+        in_specs=[VM] * 5 + [HB] * 26,
+        out_specs=(HB, HB, VM, VM, VM),
+        scratch_shapes=[vm((TOK, D), BF), vm((TOK, D), F32), vm((TOK, D), F32), vm((D, TOK), BF), vm((D, TOK), BF), vm((TOK, D), BF),
+                        vm((2, D, 4 * cw), BF), vm((D, cw), BF), vm((2, 3 * heads, TOK, HD), BF), vm((2, TOK, cw), BF), vm((2, TOK, 128), F32),
+                        vm((heads, TOK, HD), BF), vm((TOK, 3 * cw), BF), vm((heads, TOK, HD), F32), vm((heads, TOK, HD), F32), vm((4 * r, 4 * cw), BF),
+                        vm((4, 4 * r, 4 * cw), BF), vm((4, 3 * r, 4 * cw), BF), vm((2, 4 * r, cm), BF), vm((2, 3 * r, cm), BF),
+                        vm((3, r, 4 * cw), BF), vm((3, r, cm), BF), vm((5, 16, 2048), F32), vm((r, cm), F32), vm((r, cm), BF),
+                        dma((32,)), dma((COPIES,)), dma((COPIES,))],
+        compiler_params=pltpu.CompilerParams(vmem_limit_bytes=63 * 2**20, collective_id=number, has_side_effects=True),
+        cost_estimate=pl.CostEstimate(flops=4 * 2 * TOK * (D * cw * 8 + heads * 5 * TOK * HD * 6), bytes_accessed=60 * 2**20, transcendentals=4 * heads * TOK * TOK),
+        name="back",
+    )(gain1, gain2, live, geb, tops, gout, midway, sec, firstT, x, mine, whole0, whole1, h2, h3, *Ws, *qkvs, *atts, *lses)
+
+
 class General:
     split = 0
 
@@ -485,15 +880,6 @@
         every = lax.all_gather(mine, "tensor")
         middle = 1 + lax.axis_index("dp") % 2
         return jnp.stack([every[0], every[self.groups - 1], lax.dynamic_index_in_dim(every, middle, 0, keepdims=False)])
-
-
-BOTH_UP = ((0, None),)
-HOPS = {
-    "u1": (1, ((0, None),)), "u2": (3, ((1, None),)), "u3": (1, ((2, None),)),
-    "w1": (1, ((3, None),)), "w2": (3, ((2, None),)), "w3": (1, ((1, None),)),
-    "v1": (3, ((1, 0), (2, 1))), "v2": (1, ((2, 0), (1, 1))), "v3": (1, ((1, 0), (2, 1))),
-}
-HOP_FROM = {"u1": "me", "u2": "u1", "u3": "u2", "w1": "me", "w2": "w1", "w3": "w2", "v1": "me", "v2": "v1", "v3": "me"}
 
 
 class Line:
@@ -507,11 +893,7 @@
         "M0": ("g m2",),
         "M1": ("g m3", "r1 m0"),
         "M2": ("r2 m0", "r1 m1"),
-        "M3": ("r3 m0", "r2 m1", "r1 m2"),
-        "B3": ("r3 m1", "r2 m2", "r1 m3", "h u1 0", "h w1 0", "h v1 0", "h v3 0", "h v1 1", "h v3 1"),
-        "B2": ("r3 m2", "r2 m3", "r1 b3", "h u2 0", "h w2 0", "h u1 1", "h w1 1", "h v2 0", "h v2 1"),
-        "B1": ("r3 m3", "r2 b3", "r1 b2", "h u3 0", "h w3 0", "h u2 1", "h w2 1"),
-        "B0": ("r3 b3", "r2 b2", "r1 b1", "h u3 1", "h w3 1"),
+        "M3": ("r2 m1",),
     }
 
     def __init__(self, groups, attn_own, mlp_own):
@@ -528,6 +910,8 @@
         return [own] + [lax.ppermute(own, "tensor", [(i, i ^ k) for i in range(4)]) for k in (1, 2, 3)]
 
     def plan(self, name):
+        if name == "end":
+            return None
         plan = Plan(list(self.work).index(name))
         self.made = made = []
         rows, one, two = self.rows, self.one, self.two
@@ -682,6 +1066,7 @@
     groups = lax.axis_size("tensor")
     d, z = lax.axis_index("dp"), lax.axis_index("tensor")
     cw, fw = query_w.shape[1], expand_w.shape[1]
+    heads = cw // HD
     cut = fw // 128 * 128
     slot, used = slot_table(d, groups)
     live = jnp.where(used & (slot < counts[0]), 1.0, 0.0).astype(F32)
@@ -694,7 +1079,8 @@
     split = net.split
     biases = net.vectors(jnp.concatenate([query_b, value_b, expand_b]))
 
-    x = pad(lax.dynamic_index_in_dim(images, slot, 0, keepdims=False)).astype(F32)
+    x_low = pad(lax.dynamic_index_in_dim(images, slot, 0, keepdims=False))
+    x = x_low.astype(F32)
     gout = pad(lax.dynamic_index_in_dim(cotangent, slot, 0, keepdims=False)) * live.astype(BF)
     gout_t = gout.T
     normed1, inverse1 = normalize(x)
@@ -723,43 +1109,52 @@
         if split:
             net.summed(f"m{k}", grad)
         grad_mlp.append(grad)
-        geb.append(g_b[0, :fw])
-    net.give((mlp[:length] * live).astype(BF))
-    back2, gn2g, gn2s = norm_back(sec, normed2, inverse2, norm2_gain)
-    gout32 = gout.astype(F32)
-    gmid = gout32 + back2
-    gmid_low = gmid.astype(BF)
-    gmid_t = gmid_low.T
-    acc = jnp.zeros((TOK, width), F32)
-    grad_attn, gqb, gvb = [None] * groups, [None] * groups, [None] * groups
-    for k in reversed(range(groups)):
-        plan = net.plan(f"B{k}")
-        (grad, g_q, g_v, acc), got = attn_bwd(plan, gmid_low, gmid_t, first_t, net.attn[k], *kept[k], acc, length, split)
-        net.done(f"B{k}", got)
-        if split:
-            net.summed(f"b{k}", grad)
-        grad_attn[k], gqb[k], gvb[k] = grad, g_q[0], g_v[0]
-    back1, gn1g, gn1s = norm_back(acc, normed1, inverse1, norm1_gain)
-    input_grad = ((gmid + back1) * live)[:length].astype(BF)
-
-    outputs = net.gathered()[:, :length]
-    input_grads = net.share(input_grad).astype(F32)
-    sum_attn, sum_mlp = net.collect(grad_attn, grad_mlp)
-    flat = lambda items: net.by_index(items).reshape(-1)
-    vector = jnp.concatenate([flat(gqb), flat(gvb), flat(geb), jnp.sum(gmid, axis=0), jnp.sum(gout32, axis=0), gn1g, gn1s, gn2g, gn2s])
-    vector = lax.psum(vector, ("dp", "tensor"))
-    part = lambda start, size: lax.dynamic_slice_in_dim(vector, start, size, 0)
-    whole, hidden = cw * groups, fw * groups
-    tail = [vector[2 * whole + hidden + i * width:][:width] for i in range(6)]
-    logit_top = lax.pmax(jnp.where(live > 0.0, net.by_index(tops), -1e30), ("dp", "tensor"))
-    logit_top = lax.dynamic_index_in_dim(logit_top, z, 0, keepdims=False)
+        geb.append(g_b[0, :fw] if not split else g_b[0])
+    if split:
+        net.plan("end")
+        mine = (mlp * live).astype(BF)
+        state = net.state
+        out_all, in_all, sum_attn, sum_mlp, vec = back(
+            12, norm1_gain[None], norm2_gain[None], live[None, None], jnp.stack(geb)[:, None], jnp.where(live > 0.0, jnp.stack(tops), -1e30)[:, None],
+            gout, midway, sec, first_t, x_low, mine, net.third(state["m0"]), net.third(state["m1"]).astype(BF), state["m2"]["h"], state["m3"]["h"], kept, net.attn, length)
+        outputs = out_all.reshape(3, TOK, width)[:, :length]
+        input_grads = in_all.reshape(3, TOK, width)[:, :length].astype(F32)
+        own = lax.dynamic_index_in_dim(vec, z, 0, keepdims=False)
+        grad_query_b, grad_value_b, grad_expand_b, logit_top = own[:cw], own[384:384 + cw], own[768:768 + fw], own[1920:1920 + heads]
+        tail = [vec[4 + i, :width] for i in range(6)]
+    else:
+        back2, gn2g, gn2s = norm_back(sec, normed2, inverse2, norm2_gain)
+        gout32 = gout.astype(F32)
+        gmid = gout32 + back2
+        gmid_low = gmid.astype(BF)
+        gmid_t = gmid_low.T
+        acc = jnp.zeros((TOK, width), F32)
+        grad_attn, gqb, gvb = [None] * groups, [None] * groups, [None] * groups
+        for k in reversed(range(groups)):
+            (grad, g_q, g_v, acc), _ = attn_bwd(Plan(0), gmid_low, gmid_t, first_t, net.attn[k], *kept[k], acc, length, split)
+            grad_attn[k], gqb[k], gvb[k] = grad, g_q[0], g_v[0]
+        back1, gn1g, gn1s = norm_back(acc, normed1, inverse1, norm1_gain)
+        input_grad = ((gmid + back1) * live)[:length].astype(BF)
+
+        outputs = net.share((mlp[:length] * live).astype(BF))
+        input_grads = net.share(input_grad).astype(F32)
+        sum_attn, sum_mlp = net.collect(grad_attn, grad_mlp)
+        flat = lambda items: net.by_index(items).reshape(-1)
+        vector = jnp.concatenate([flat(gqb), flat(gvb), flat(geb), jnp.sum(gmid, axis=0), jnp.sum(gout32, axis=0), gn1g, gn1s, gn2g, gn2s])
+        vector = lax.psum(vector, ("dp", "tensor"))
+        part = lambda start, size: lax.dynamic_slice_in_dim(vector, start, size, 0)
+        whole, hidden = cw * groups, fw * groups
+        tail = [vector[2 * whole + hidden + i * width:][:width] for i in range(6)]
+        logit_top = lax.pmax(jnp.where(live > 0.0, net.by_index(tops), -1e30), ("dp", "tensor"))
+        logit_top = lax.dynamic_index_in_dim(logit_top, z, 0, keepdims=False)
+        grad_query_b, grad_value_b, grad_expand_b = part(z * cw, cw), part(whole + z * cw, cw), part(2 * whole + z * fw, fw)
     factor = jnp.sqrt(clip_limit / jnp.maximum(logit_top, clip_limit))
     column_factor = jnp.repeat(factor, HD)
     clipped_query = (query_w.astype(F32) * column_factor).astype(BF)
     clipped_key = (key_w.astype(F32) * column_factor).astype(BF)
     unpack = lambda a, i: jnp.concatenate([a[:, i * cut:(i + 1) * cut], a[:, 2 * cut + i * (fw - cut):][:, :fw - cut]], axis=1)
-    return (outputs, input_grads, sum_attn[:, :cw], part(z * cw, cw), sum_attn[:, cw:2 * cw], sum_attn[:, 2 * cw:3 * cw], part(whole + z * cw, cw),
-            sum_attn[:, 3 * cw:].T, tail[0], tail[2], tail[3], tail[4], tail[5], unpack(sum_mlp, 0), part(2 * whole + z * fw, fw), unpack(sum_mlp, 1).T,
+    return (outputs, input_grads, sum_attn[:, :cw], grad_query_b, sum_attn[:, cw:2 * cw], sum_attn[:, 2 * cw:3 * cw], grad_value_b,
+            sum_attn[:, 3 * cw:].T, tail[0], tail[2], tail[3], tail[4], tail[5], unpack(sum_mlp, 0), grad_expand_b, unpack(sum_mlp, 1).T,
             tail[1], clipped_query, clipped_key)
 
 

time: 949 us -> 695 us (0.73)
  the two profiles are of different devices: /device:TPU:18 before, /device:TPU:1 now
where the time goes in v3:
time: 695 us; the launch traced here: 685 us
  Pallas kernels  537 us (77%)
  local copies, waits for them, and re-layouts  101 us (15%)
  other arithmetic  40.4 us (6%)
    pallas_call x1, Pallas kernels, back(): pl.pallas_call(functools.partial(back_kernel, length, heads), out_shape=(...  257 us
    pallas_call x4, Pallas kernels, mlp_call(): pl.pallas_call(functools.partial(mlp_kernel, fw, split, plan), out_shape=...  151 us
    pallas_call x4, Pallas kernels, attn_fwd(): pl.pallas_call(functools.partial(attn_fwd_kernel, length, heads, plan), o...  128 us
    unnamed x98, local copies, waits for them, and re-layouts  30.1 us
  transfers between devices with their start and end apart: 3, of which 0 were waited for; matrix products, arithmetic and copies ran while one was open for 10% of the time, Pallas kernels for 11%

profile of v3, /device:TPU:1, one launch (start us, length us, event | category | flops | bytes accessed | tf_op | source)
XLA Modules:
  0.0 684.8 jit_solution(11473538369846814181)
XLA Ops:
  0.7 1.4 concatenate.40
  2.1 2.1 collective-permute-start.2
  4.2 2.3 collective-permute-start.1
  7.9 5.2 copy.59
  13.1 3.5 slice.233
  16.5 1.7 slice.234
  18.2 1.6 slice.177
  20.5 3.5 dynamic-slice_bitcast_fusion
  23.9 2.3 convert_add_fusion
  27.6 1.9 fusion.13
  30.0 1.5 copy.55
  31.5 2.3 copy.56
  33.8 2.3 copy.57
  36.1 4.3 copy.71
  40.4 1.8 copy.72
  42.2 5.5 concatenate.41.W_ref.rest_0_
  48.7 8.6 %concatenate.42.W_ref = bf16[1152,2152]{1,0:T(8,128)(2,1)} concatenate(bf16[1152,1024]{1,0:T(8,128)(2,1)} %copy.71, bf16[1152,1024]{1,0:T(8,128)(2,1)} %slice.233, bf16[1152,52]{1,0:T(8,128)(2,1)} %copy.72, bf16[1152,52]{1,0:T(8,128)(2,1)} %slice.234), dimensions={1} | concatenate | bytes 9916416 | tf_op jit(solution)/shard_map/concatenate | solution.py:1077
  59.1 3.6 fusion.7
  62.7 40.1 %attn_fwd.4 = (bf16[12,768,72]{2,1,0:T(8,128)(2,1)S(1)}, bf16[768,288]{1,0:T(8,128)(2,1)S(1)}, f32[768,128]{1,0:T(8,128)S(1)}, f32[4,128]{1,0:T(4,128)S(1)}, f32...) custom-call(bf16[768,1152]{1,0:T(8,128)(2,1)S(1)} %fusion.5.first, ...), custom_call_target="tpu_custom_call" | custom-call | flops 6115295232 | bytes 26214400 | tf_op jit(solution)/shard_map/attn_fwd/pallas_call | solution.py:212
  102.9 1.5 copy-done.1
  104.4 1.4 copy-done.7
  108.1 3.9 copy.63.goutT
  112.6 3.9 copy.70.firstT
  116.5 2.8 pad.20.x
  120.7 32.8 %attn_fwd.5 = (bf16[12,768,72]{2,1,0:T(8,128)(2,1)S(1)}, bf16[768,288]{1,0:T(8,128)(2,1)S(1)}, f32[768,128]{1,0:T(8,128)S(1)}, f32[4,128]{1,0:T(4,128)S(1)}, f32...) custom-call(bf16[768,1152]{1,0:T(8,128)(2,1)S(1)} %fusion.5.first, ...), custom_call_target="tpu_custom_call" | custom-call | flops 6115295232 | bytes 26214400 | tf_op jit(solution)/shard_map/attn_fwd/pallas_call | solution.py:212
  153.5 1.5 copy-done.2
  155.0 1.4 copy-done.4
  158.9 21.8 %attn_fwd.6 = (bf16[12,768,72]{2,1,0:T(8,128)(2,1)S(1)}, bf16[768,288]{1,0:T(8,128)(2,1)S(1)}, f32[768,128]{1,0:T(8,128)S(1)}, f32[4,128]{1,0:T(4,128)S(1)}, f32...) custom-call(bf16[768,1152]{1,0:T(8,128)(2,1)S(1)} %fusion.5.first, ...), custom_call_target="tpu_custom_call" | custom-call | flops 6115295232 | bytes 26214400 | tf_op jit(solution)/shard_map/attn_fwd/pallas_call | solution.py:212
  181.6 33.6 %attn_fwd.7 = (bf16[12,768,72]{2,1,0:T(8,128)(2,1)S(1)}, bf16[768,288]{1,0:T(8,128)(2,1)S(1)}, f32[768,128]{1,0:T(8,128)S(1)}, f32[4,128]{1,0:T(4,128)S(1)}, f32...) custom-call(bf16[768,1152]{1,0:T(8,128)(2,1)S(1)} %fusion.5.first, ...), custom_call_target="tpu_custom_call" | custom-call | flops 6115295232 | bytes 26214400 | tf_op jit(solution)/shard_map/attn_fwd/pallas_call | solution.py:212
  215.2 1.4 copy-done.5
  218.2 5.4 copy.61
  223.6 4.2 broadcast_add_fusion
  228.5 1.8 fusion.14.secondT
  230.8 2.4 copy.62.second
  234.6 2.0 broadcast_in_dim.81.sec_in
  236.7 39.7 %mlp.4 = (bf16[576,2152]{1,0:T(8,128)(2,1)}, f32[1,1152]{1,0:T(1,128)}, f32[768,1152]{1,0:T(8,128)}, f32[768,1152]{1,0:T(8,128)}, bf16[1152,2152]{1,0:T(8,128)(2,1)}) custom-call(bf16[768,1152]{1,0:T(8,128)(2,1)} %copy.62.second, bf16[1152,768]{1,0:T(8,128)(2,1)} %fusion.14.secondT, bf16[768,1152]{1,0:T(8,128)(2,1)} %get-tuple-element.152.gout, ...), custom_call_target="tpu_custom_call" | custom-call | flops 17135566848 | bytes 36700160 | tf_op jit(solution)/shard_map/mlp/pallas_call | solution.py:313
  276.4 49.1 %mlp.5 = (bf16[576,2152]{1,0:T(8,128)(2,1)}, f32[1,1152]{1,0:T(1,128)}, f32[768,1152]{1,0:T(8,128)}, f32[768,1152]{1,0:T(8,128)}, bf16[1152,2152]{1,0:T(8,128)(2...) custom-call(bf16[768,1152]{1,0:T(8,128)(2,1)} %copy.62.second, bf16[1152,768]{1,0:T(8,128)(2,1)} %fusion.14.secondT, ...), custom_call_target="tpu_custom_call" | custom-call | flops 17135566848 | bytes 36700160 | tf_op jit(solution)/shard_map/mlp/pallas_call | solution.py:313
  329.9 32.1 %mlp.6 = (bf16[576,2152]{1,0:T(8,128)(2,1)}, f32[1,1152]{1,0:T(1,128)}, f32[768,1152]{1,0:T(8,128)}, f32[768,1152]{1,0:T(8,128)}, bf16[80,2152]{1,0:T(8,128)(2,1...) custom-call(bf16[768,1152]{1,0:T(8,128)(2,1)} %copy.62.second, ...), custom_call_target="tpu_custom_call" | custom-call | flops 17135566848 | bytes 36700160 | tf_op jit(solution)/shard_map/mlp/pallas_call | solution.py:313
  366.5 30.3 %mlp.7 = (bf16[576,2152]{1,0:T(8,128)(2,1)}, f32[1,1152]{1,0:T(1,128)}, f32[768,1152]{1,0:T(8,128)}, f32[768,1152]{1,0:T(8,128)}, bf16[80,2152]{1,0:T(8,128)(2,1)}, /*index=5*/bf16[64,2152]{1,0:T(8,128)(2,1)}) custom-call(bf16[768,1152]{1,0:T(8,128)(2,1)} %copy.62.second, bf16[1152,768]{1,0:T(8,128)(2,1)} %fusion.14.secondT, ...), custom_call_target="tpu_custom_call" | custom-call | flops 17135566848 | bytes 36700160 | tf_op jit(solution)/shard_map/mlp/pallas_call | solution.py:313
  396.8 1.4 add_convert_fusion.1
  399.7 1.5 multiply_convert_fusion.mine
  404.8 257.5 %back.1 = (bf16[2304,1152]{1,0:T(8,128)(2,1)}, bf16[2304,1152]{1,0:T(8,128)(2,1)}, f32[144,1152]{1,0:T(8,128)}, f32[144,2152]{1,0:T(8,128)}, f32[16,2048]{1,0:T(8,128)}) custom-call(f32[1,1152]{1,0:T(1,128)} %broadcast_in_dim.69.gain1, f32[1,1152]{1,0:T(1,128)} %broadcast_in_dim.70.gain2, f32[1,1]{1,0:T(1,128)} %bitcast.1.live, ...), custom_call_target="tpu_custom_call" | custom-call | flops 57076088832 | bytes 62914560 | tf_op jit(solution)/shard_map/back/pallas_call | solution.py:821
  662.3 1.4 fusion.8
  664.8 7.3 %slice_convert_fusion = f32[3,729,1152]{2,1,0:T(8,128)} fusion(bf16[3,768,1152]{2,1,0:T(8,128)(2,1)} %bitcast.32), kind=kLoop, calls=%fused_computation.3 | loop fusion | flops 2519424 | bytes 15116544 | tf_op jit(solution)/shard_map/convert_element_type | solution.py:1121
  672.1 2.7 slice.238
  674.8 1.6 slice_reduce_fusion
  679.8 1.5 dynamic-slice_reduce_fusion
  681.2 1.4 dynamic-slice_reduce_fusion.1
  (154 shorter events, 37.9 us)
Async XLA Ops:
  2.1 117.8 %collective-permute-start.2 = (f32[1652]{0:T(1024)}, f32[1652]{0:T(1024)}, u32[]{:S(2)}, u32[]{:S(2)}) collective-permute-start(f32[1652]{0:T(1024)} %concatenate.40), channel_id=1, source_target_pairs={{0,1},{1,0},{2,3},{3,2},{4,5},{5,4},{6,7},{7,6},{8,9},{9,8},{10,11... | collective-permute-start | bytes 19832 | tf_op jit(solution)/shard_map/ppermute | solution.py:910
  4.2 153.0 %collective-permute-start.1 = (f32[1652]{0:T(1024)}, f32[1652]{0:T(1024)}, u32[]{:S(2)}, u32[]{:S(2)}) collective-permute-start(f32[1652]{0:T(1024)} %concatenate.40), channel_id=1, source_target_pairs={{0,2},{1,3},{2,0},{3,1},{4,6},{5,7},{6,4},{7,5},{8,10},{9,11},{10,... | collective-permute-start | bytes 19832 | tf_op jit(solution)/shard_map/ppermute | solution.py:910
  6.5 151.6 %collective-permute-start = (f32[1652]{0:T(1024)}, f32[1652]{0:T(1024)}, u32[]{:S(2)}, u32[]{:S(2)}) collective-permute-start(f32[1652]{0:T(1024)} %concatenate.40), channel_id=1, source_target_pairs={{0,3},{1,2},{2,1},{3,0},{4,7},{5,6},{6,5},{7,4},{8,11},{9,10},{10,... | collective-permute-start | bytes 19832 | tf_op jit(solution)/shard_map/ppermute | solution.py:910
  13.1 5.1 copy-start.22
  19.8 4.1 copy-start.37
  23.9 3.7 copy-start.17
  23.9 3.0 copy-start.32
  23.9 3.0 copy-start.34
  26.9 2.7 copy-start.26
  62.7 44.8 %copy-start.36 = (f32[1076]{0:T(1024)S(1)}, f32[1076]{0:T(1024)}, u32[]{:S(2)}) copy-start(f32[1076]{0:T(1024)} %param.33) | copy-start | bytes 12916
  102.9 1.5 copy-start.1
  104.4 1.4 copy-start.7
  105.8 0.8 copy-start.12
  106.7 0.7 copy-start.16
  112.0 7.3 %copy-start.33 = (f32[1152]{0:T(1024)S(1)}, f32[1152]{0:T(1024)}, u32[]{:S(2)}) copy-start(f32[1152]{0:T(1024)} %param.30) | copy-start | bytes 13828
  153.5 1.5 copy-start.2
  155.0 1.4 copy-start.4
  156.4 0.8 copy-start.8
  157.2 23.6 %copy-start.13 = (f32[768,128]{1,0:T(8,128)}, f32[768,128]{1,0:T(8,128)S(1)}, u32[]{:S(2)}) copy-start(f32[768,128]{1,0:T(8,128)S(1)} %get-tuple-element.133.rest_13_) | copy-start | bytes 1179652
  180.8 0.7 copy-start.15
  181.5 33.7 %copy-start.3 = (bf16[1152,1152]{1,0:T(8,128)(2,1)}, bf16[1152,1152]{1,0:T(8,128)(2,1)S(1)}, u32[]{:S(2)}) copy-start(bf16[1152,1152]{1,0:T(8,128)(2,1)S(1)} %get-tuple-element.87.W_ref.rest_3_) | copy-start | bytes 7962628
  181.5 33.7 %copy-start.6 = (bf16[12,768,72]{2,1,0:T(8,128)(2,1)}, bf16[12,768,72]{2,1,0:T(8,128)(2,1)S(1)}, u32[]{:S(2)}) copy-start(bf16[12,768,72]{2,1,0:T(8,128)(2,1)S(1)} %get-tuple-element.126.rest_6_) | copy-start | bytes 3981316
  181.5 33.7 %copy-start.11 = (bf16[768,288]{1,0:T(8,128)(2,1)}, bf16[768,288]{1,0:T(8,128)(2,1)S(1)}, u32[]{:S(2)}) copy-start(bf16[768,288]{1,0:T(8,128)(2,1)S(1)} %get-tuple-element.130.rest_10_) | copy-start | bytes 1327108
  181.5 33.7 %copy-start = (bf16[144,2152]{1,0:T(8,128)(2,1)}, bf16[144,2152]{1,0:T(8,128)(2,1)S(1)}, u32[]{:S(2)}) copy-start(bf16[144,2152]{1,0:T(8,128)(2,1)S(1)} %constant_dynamic-update-slice_fusion.rest_1_.rest_0_) | copy-start | bytes 1859332
  215.2 1.4 copy-start.5
  216.6 0.8 copy-start.9
  217.4 0.8 copy-start.14
  218.2 5.4 copy-start.10
  218.2 5.4 copy-start.38
  223.6 4.2 copy-start.18
  227.8 0.7 copy-start.35
  276.4 49.1 %copy-start.27 = (bf16[576,2152]{1,0:T(8,128)(2,1)S(1)}, bf16[576,2152]{1,0:T(8,128)(2,1)}, u32[]{:S(2)}) copy-start(bf16[576,2152]{1,0:T(8,128)(2,1)} %get-tuple-element.97.rest_1_) | copy-start | bytes 7437316
  366.5 30.3 %copy-start.25 = (bf16[160,2152]{1,0:T(8,128)(2,1)S(1)}, bf16[160,2152]{1,0:T(8,128)(2,1)}, u32[]{:S(2)}) copy-start(bf16[160,2152]{1,0:T(8,128)(2,1)} %get-tuple-element.109) | copy-start | bytes 2065924
  366.5 31.7 %copy-start.29 = (bf16[128,2152]{1,0:T(8,128)(2,1)S(1)}, bf16[128,2152]{1,0:T(8,128)(2,1)}, u32[]{:S(2)}) copy-start(bf16[128,2152]{1,0:T(8,128)(2,1)} %get-tuple-element.110) | copy-start | bytes 1652740
  366.5 32.9 %copy-start.24 = (bf16[160,2152]{1,0:T(8,128)(2,1)S(1)}, bf16[160,2152]{1,0:T(8,128)(2,1)}, u32[]{:S(2)}) copy-start(bf16[160,2152]{1,0:T(8,128)(2,1)} %get-tuple-element.102) | copy-start | bytes 2065924
  366.5 32.9 %copy-start.30 = (bf16[80,2152]{1,0:T(8,128)(2,1)S(1)}, bf16[80,2152]{1,0:T(8,128)(2,1)}, u32[]{:S(2)}) copy-start(bf16[80,2152]{1,0:T(8,128)(2,1)} %get-tuple-element.118) | copy-start | bytes 1032964
  366.5 33.1 %copy-start.31 = (bf16[64,2152]{1,0:T(8,128)(2,1)S(1)}, bf16[64,2152]{1,0:T(8,128)(2,1)}, u32[]{:S(2)}) copy-start(bf16[64,2152]{1,0:T(8,128)(2,1)} %get-tuple-element.119) | copy-start | bytes 826372
  396.8 2.8 copy-start.28
  396.8 2.9 copy-start.19
  399.5 2.0 copy-start.39
  399.5 2.0 copy-start.40
  399.6 2.0 copy-start.41
  399.6 2.0 copy-start.42
  663.6 8.4 %slice-start = ((s8[5308416]{0:T(1024)(128)(4,1)}), s8[4194304]{0:T(1024)(128)(4,1)S(1)}, s32[]{:S(2)}) async-start(s8[5308416]{0:T(1024)(128)(4,1)} %bitcast.29), calls=%async_computation | async-start | bytes 8388608
  664.8 7.3 %slice-start.1 = ((s8[5308416]{0:T(1024)(128)(4,1)}), s8[1114112]{0:T(1024)(128)(4,1)S(1)}, s32[]{:S(2)}) async-start(s8[5308416]{0:T(1024)(128)(4,1)} %bitcast.29), calls=%async_computation.1 | async-start | bytes 2228224
  672.1 5.3 copy-start.20
  672.1 5.3 copy-start.21
  672.1 6.6 copy-start.23

commit v4 on v3

v4 whole, which is shorter than its diff:
```python
import functools
import math

import jax
import jax.numpy as jnp
from jax import lax
from jax.experimental import pallas as pl
from jax.experimental.pallas import tpu as pltpu
from jax.sharding import PartitionSpec as P

HD = 72
TOK = 768
RT = 256
SC = 1 / math.sqrt(HD)
LOG2E = 1.4426950408889634
F32 = jnp.float32
BF = jnp.bfloat16
norm_eps = 1e-06
clip_limit = 3.0
tanh_coef = 0.7978845608028654
cube_coef = 0.044715
VM = pl.BlockSpec(memory_space=pltpu.VMEM)
HB = pl.BlockSpec(memory_space=pl.ANY)
MESH = pl.DeviceIdType.MESH


def nn(a, b):
    return jnp.dot(a, b, preferred_element_type=F32)


def nt(a, b):
    return lax.dot_general(a, b, (((1,), (1,)), ((), ())), preferred_element_type=F32)


def tn(a, b):
    return lax.dot_general(a, b, (((0,), (0,)), ((), ())), preferred_element_type=F32)


def shape(dims, dtype):
    return jax.ShapeDtypeStruct(dims, dtype)


def cut_rows(rows):
    first = (rows // 2 + 15) // 16 * 16
    return first, rows - first


def block_rows(lhs, rhs, half, write):
    if half is None:
        @pl.loop(0, lhs.shape[0] // 384)
        def _(t):
            place = pl.ds(pl.multiple_of(t * 384, 128), 384)
            write(place, nn(lhs[place, :], rhs[...]))
    else:
        rows = lhs.shape[0] // 8
        d = lax.axis_index("dp")

        @pl.loop(0, 2)
        def _(t):
            r = 4 * t + 1 - half
            both = [lhs[pl.ds(pl.multiple_of((d ^ q) * rows, 16), rows), :] for q in (r, r + 2)]
            write(pl.ds(pl.multiple_of(t * 2 * rows, 16), 2 * rows), nn(jnp.concatenate(both, axis=0), rhs[...]))


def attn_fwd_kernel(length, heads, first, qb, vb, acc_in, W, qkv, att, lse, tops, acc):
    cw = heads * HD

    @pl.loop(0, TOK // RT)
    def _(i):
        rows = pl.ds(pl.multiple_of(i * RT, RT), RT)
        t = nn(first[rows, :], W[:, :3 * cw])
        q = (t[:, :cw] + qb[...]).astype(BF)
        k = t[:, cw:2 * cw].astype(BF)
        v = (t[:, 2 * cw:] + vb[...]).astype(BF)
        for h in range(heads):
            qkv[h, rows, :] = q[:, h * HD:(h + 1) * HD]
            qkv[heads + h, rows, :] = k[:, h * HD:(h + 1) * HD]
            qkv[2 * heads + h, rows, :] = v[:, h * HD:(h + 1) * HD]

    tops[...] = jnp.full(tops.shape, -1e30, F32)

    @pl.loop(0, TOK // RT)
    def _(i):
        rows = pl.ds(pl.multiple_of(i * RT, RT), RT)
        rid = lax.broadcasted_iota(jnp.int32, (RT, 1), 0) + i * RT
        cid = lax.broadcasted_iota(jnp.int32, (1, TOK), 1)
        res = []
        for h in range(heads):
            s = nt(qkv[h, rows, :], qkv[heads + h])
            s = jnp.where(cid < length, s, -1e30)
            m = jnp.max(s, axis=1, keepdims=True)
            e = jnp.exp2((s - m) * (SC * LOG2E))
            l = jnp.sum(e, axis=1, keepdims=True)
            o = nn(e.astype(BF), qkv[2 * heads + h]) * (1.0 / l)
            res.append(o.astype(BF))
            lse[rows, h:h + 1] = m * (SC * LOG2E) + jnp.log2(l)
            tops[h:h + 1, :] = jnp.maximum(tops[h:h + 1, :], jnp.max(jnp.where(rid < length, m, -1e30)) * SC)
        a = jnp.concatenate(res, axis=1)
        att[rows, :] = a
        acc[rows, :] = acc_in[rows, :] + nt(a, W[:, 3 * cw:])


def attn_fwd(first, W, qb, vb, acc, length):
    D = first.shape[1]
    cw = W.shape[1] // 4
    heads = cw // HD
    return pl.pallas_call(
        functools.partial(attn_fwd_kernel, length, heads),
        out_shape=(shape((3 * heads, TOK, HD), BF), shape((TOK, cw), BF), shape((TOK, 128), F32), shape((heads, 128), F32), shape((TOK, D), F32)),
        in_specs=[VM] * 5,
        out_specs=(VM,) * 5,
        compiler_params=pltpu.CompilerParams(vmem_limit_bytes=44 * 2**20),
        cost_estimate=pl.CostEstimate(flops=2 * TOK * (D * cw * 4 + heads * 2 * TOK * HD * 6), bytes_accessed=25 * 2**20, transcendentals=heads * TOK * TOK),
        name="attn_fwd",
    )(first, qb, vb, acc, W)


def gelu_parts(u):
    u2 = u * u
    t = jnp.tanh(u * (tanh_coef + (tanh_coef * cube_coef) * u2))
    hu = 0.5 * (1.0 + t)
    return u * hu, hu + u * (0.5 * tanh_coef) * (1.0 - t * t) * (1.0 + (3.0 * cube_coef) * u2)


def mlp_kernel(fw, second, secondT, gout, goutT, eb, mlp_in, sec_in, W, G, geb, mlp, sec, E, ST, act_s, gpre_s):
    cut = fw // 128 * 128
    tail = fw - cut
    E[:, :cut] = W[:, :cut]
    ST[:, :cut] = W[:, cut:2 * cut]
    last = W[:, 2 * cut:]
    blank = jnp.zeros((last.shape[0], 128 - tail), BF)
    E[:, cut:] = jnp.concatenate([last[:, :tail], blank], axis=1)
    ST[:, cut:] = jnp.concatenate([last[:, tail:], blank], axis=1)
    geb[...] = jnp.zeros_like(geb)

    @pl.loop(0, TOK // RT)
    def _(i):
        rows = pl.ds(pl.multiple_of(i * RT, RT), RT)
        act, slope = gelu_parts(nn(second[rows, :], E[...]) + eb[...])
        act_s[rows, :] = act.astype(BF)
        gp = nn(gout[rows, :], ST[...]) * slope
        geb[...] += jnp.sum(gp, axis=0, keepdims=True)
        gpre_s[rows, :] = gp.astype(BF)
        mlp[rows, :] = mlp_in[rows, :] + nt(act_s[rows, :], ST[...])
        sec[rows, :] = sec_in[rows, :] + nt(gpre_s[rows, :], E[...])

    def write(lo, last):
        def put(place, v):
            v = v.astype(BF)
            G[place, lo:lo + cut] = v[:, :cut]
            G[place, last:last + tail] = v[:, cut:fw]
        return put

    block_rows(secondT, gpre_s, None, write(0, 2 * cut))
    block_rows(goutT, act_s, None, write(cut, 2 * cut + tail))


def mlp_call(second, secondT, gout, goutT, W, eb, mlp, sec):
    D = second.shape[1]
    fw = W.shape[1] // 2
    wide = fw // 128 * 128 + 128
    eb = jnp.pad(eb, ((0, 0), (0, wide - fw)))
    return pl.pallas_call(
        functools.partial(mlp_kernel, fw),
        out_shape=(shape((D, 2 * fw), BF), shape((1, wide), F32), shape((TOK, D), F32), shape((TOK, D), F32)),
        in_specs=[VM] * 8,
        out_specs=(VM,) * 4,
        scratch_shapes=[pltpu.VMEM((D, wide), BF)] * 2 + [pltpu.VMEM((TOK, wide), BF)] * 2,
        compiler_params=pltpu.CompilerParams(vmem_limit_bytes=56 * 2**20),
        cost_estimate=pl.CostEstimate(flops=2 * 9 * TOK * D * fw, bytes_accessed=35 * 2**20, transcendentals=TOK * fw),
        name="mlp",
    )(second, secondT, gout, goutT, eb, mlp, sec, W)


def attn_bwd_kernel(length, heads, gmid, gmidT, firstT, qkv, att, lse, acc_in, W, G, gqb, gvb, acc, ga_s, d_s, dk_s, dv_s):
    cw = heads * HD

    @pl.loop(0, TOK // RT)
    def _(i):
        rows = pl.ds(pl.multiple_of(i * RT, RT), RT)
        g = nn(gmid[rows, :], W[:, 3 * cw:]).astype(BF)
        for h in range(heads):
            ga_s[h, rows, :] = g[:, h * HD:(h + 1) * HD]

    gqb[...] = jnp.zeros_like(gqb)
    dk_s[...] = jnp.zeros_like(dk_s)
    dv_s[...] = jnp.zeros_like(dv_s)

    @pl.loop(0, TOK // RT)
    def _(i):
        rows = pl.ds(pl.multiple_of(i * RT, RT), RT)
        cid = lax.broadcasted_iota(jnp.int32, (1, TOK), 1)
        dqs = []
        for h in range(heads):
            q, k, v, g = qkv[h, rows, :], qkv[heads + h], qkv[2 * heads + h], ga_s[h, rows, :]
            s = nt(q, k)
            p = jnp.exp2(s * (SC * LOG2E) - lse[rows, h:h + 1])
            p = jnp.where(cid < length, p, 0.0)
            dp = nt(g, v)
            dd = jnp.sum(g.astype(F32) * att[rows, h * HD:(h + 1) * HD].astype(F32), axis=1, keepdims=True)
            ds = (p * (dp - dd)).astype(BF)
            dqs.append(nn(ds, k) * SC)
            dk_s[h] += tn(ds, q)
            dv_s[h] += tn(p.astype(BF), g)
        dq = jnp.concatenate(dqs, axis=1)
        gqb[...] += jnp.sum(dq, axis=0, keepdims=True)
        d_s[rows, :cw] = dq.astype(BF)

    dk = jnp.concatenate([dk_s[h] * SC for h in range(heads)], axis=1)
    d_s[:, cw:2 * cw] = dk.astype(BF)
    dv = jnp.concatenate([dv_s[h] for h in range(heads)], axis=1)
    gvb[...] = jnp.sum(dv, axis=0, keepdims=True)
    d_s[:, 2 * cw:] = dv.astype(BF)

    @pl.loop(0, TOK // RT)
    def _(i):
        rows = pl.ds(pl.multiple_of(i * RT, RT), RT)
        acc[rows, :] = acc_in[rows, :] + nt(d_s[rows, :], W[:, :3 * cw])

    def write(lo, hi):
        def put(place, v):
            G[place, lo:hi] = v.astype(BF)
        return put

    block_rows(firstT, d_s, None, write(0, 3 * cw))
    block_rows(gmidT, att, None, write(3 * cw, 4 * cw))


def attn_bwd(gmid, gmidT, firstT, W, qkv, att, lse, acc, length):
    D = gmid.shape[1]
    cw = W.shape[1] // 4
    heads = cw // HD
    return pl.pallas_call(
        functools.partial(attn_bwd_kernel, length, heads),
        out_shape=(shape((D, 4 * cw), BF), shape((1, cw), F32), shape((1, cw), F32), shape((TOK, D), F32)),
        in_specs=[VM] * 8,
        out_specs=(VM,) * 4,
        scratch_shapes=[pltpu.VMEM((heads, TOK, HD), BF), pltpu.VMEM((TOK, 3 * cw), BF), pltpu.VMEM((heads, TOK, HD), F32), pltpu.VMEM((heads, TOK, HD), F32)],
        compiler_params=pltpu.CompilerParams(vmem_limit_bytes=52 * 2**20),
        cost_estimate=pl.CostEstimate(flops=2 * TOK * (D * cw * 8 + heads * 5 * TOK * HD * 6), bytes_accessed=30 * 2**20, transcendentals=heads * TOK * TOK),
        name="attn_bwd",
    )(gmid, gmidT, firstT, qkv, att, lse, acc, W)


def normalize(values):
    centre = jnp.mean(values, axis=-1, keepdims=True)
    centred = values - centre
    spread = jnp.mean(centred * centred, axis=-1, keepdims=True)
    inverse = lax.rsqrt(spread + norm_eps)
    return centred * inverse, inverse


def norm_back(grad_norm, normed, inverse, gain):
    scaled = grad_norm * gain
    first_mean = jnp.mean(scaled, axis=-1, keepdims=True)
    second_mean = jnp.mean(scaled * normed, axis=-1, keepdims=True)
    grad_input = inverse * (scaled - first_mean - normed * second_mean)
    return grad_input, jnp.sum(grad_norm * normed, axis=0), jnp.sum(grad_norm, axis=0)


def slot_table(d, groups):
    z = lax.axis_index("tensor")
    middle = 1 + d % 2
    return jnp.where(z == 0, 0, jnp.where(z == groups - 1, 1, 2)), (z == 0) | (z == groups - 1) | (z == middle)


HOPS = {
    "u1": (1, ((0, None),)), "u2": (3, ((1, None),)), "u3": (1, ((2, None),)),
    "w1": (1, ((3, None),)), "w2": (3, ((2, None),)), "w3": (1, ((1, None),)),
    "v1": (3, ((1, 0), (2, 1))), "v2": (1, ((2, 0), (1, 1))), "v3": (1, ((1, 0), (2, 1))),
}
HOP_FROM = {"u1": "me", "u2": "u1", "u3": "u2", "w1": "me", "w2": "w1", "w3": "w2", "v1": "me", "v2": "v1", "v3": "me"}
NAMES = ("u1", "w1", "v1", "v3"), ("u2", "w2", "v2"), ("u3", "w3")
BEGIN = {"u": 0, "w": 1, "v": 2}


class Wires:
    def __init__(self, s_sem, r_sem):
        self.s, self.r, self.n = s_sem, r_sem, 0
        self.d, self.z = lax.axis_index("dp"), lax.axis_index("tensor")

    def local(self, src, dst, used):
        i = self.n
        self.n += 1
        make = lambda: pltpu.make_async_copy(src, dst, self.s.at[i])
        return (lambda: pl.when(used)(lambda: make().start())), (lambda: pl.when(used)(lambda: make().wait()))

    def swap(self, src, dst, dp=0, z=0, sends=None):
        i = self.n
        self.n += 1
        make = lambda: pltpu.make_async_remote_copy(src_ref=src, dst_ref=dst, send_sem=self.s.at[i], recv_sem=self.r.at[i], device_id=(self.d ^ dp, self.z ^ z), device_id_type=MESH)
        if sends is None:
            return (lambda: make().start()), (lambda: make().wait())

        def any_of(z_here):
            hit = None
            for zz, cc in sends:
                this = z_here == zz
                if cc is not None:
                    this = this & (self.d % 2 == cc)
                hit = this if hit is None else hit | this
            return hit

        def start():
            pl.when(any_of(self.z))(lambda: make().start())

        def wait():
            pl.when(any_of(self.z))(lambda: make().wait_send())
            pl.when(any_of(self.z ^ z))(lambda: make().wait_recv())

        return start, wait


def greet(d, z, masks):
    sem = pltpu.get_barrier_semaphore()
    for dp, t in masks:
        pl.semaphore_signal(sem, inc=1, device_id=(d ^ dp, z ^ t), device_id_type=MESH)
    pl.semaphore_wait(sem, len(masks))


class Summing:
    def __init__(self, wires, H, land, zr, k):
        self.H, self.k = H, k
        self.rows = r = H.shape[0] // 4
        self.one, self.two = one, two = cut_rows(r)
        ax, by = land.at[pl.ds(0, 2 * one), :], land.at[pl.ds(2 * one, 2 * two), :]
        ay, bx = land.at[pl.ds(2 * r, one), :], land.at[pl.ds(2 * r + one, two), :]
        self.land = land
        h = lambda lo, n: H.at[pl.ds(lo, n), :]
        at = lambda ref, lo, n: ref.at[pl.ds(lo, n), :]
        self.c1 = [wires.swap(h(r, one), at(land, 0, one), dp=2), wires.swap(h(3 * r, one), at(land, one, one), dp=2),
                   wires.swap(h(2 * r + one, two), at(land, 2 * one, two), dp=4), wires.swap(h(3 * r + one, two), at(land, 2 * one + two, two), dp=4)]
        self.c2 = [wires.swap(h(2 * r, one), ay, dp=4), wires.swap(h(r + one, two), bx, dp=2)]
        self.c3 = [wires.swap(h(0, r), zr, z=k)] if k else []

    def add(self, lo, n, *froms):
        total = self.H[lo:lo + n, :].astype(F32)
        for f in froms:
            total = total + self.land[f:f + n, :].astype(F32)
        self.H[lo:lo + n, :] = total.astype(BF)

    def step1(self):
        for s, _ in self.c1:
            s()

    def step2(self):
        r, one, two = self.rows, self.one, self.two
        for _, w in self.c1:
            w()
        self.add(2 * r, one, one)
        self.add(r + one, two, 2 * one + two)
        for s, _ in self.c2:
            s()

    def step3(self):
        r, one, two = self.rows, self.one, self.two
        for _, w in self.c2:
            w()
        self.add(0, one, 0, 2 * r)
        self.add(one, two, 2 * one, 2 * r + one)
        for s, _ in self.c3:
            s()

    def step4(self):
        for _, w in self.c3:
            w()


class Sharing:
    def __init__(self, wires, mine, O, chunks, base=0):
        self.stages = []
        stride = O.shape[0] // 3
        for lo, n in chunks:
            here = []
            for names in NAMES:
                row = []
                for name in names:
                    mask, sends = HOPS[name]
                    place = O.at[pl.ds(BEGIN[name[0]] * stride + lo - base, n), :]
                    row.append(wires.swap(mine.at[pl.ds(lo, n), :] if HOP_FROM[name] == "me" else place, place, z=mask, sends=sends))
                here.append(row)
            self.stages.append(here)

    def start(self, chunk, stage):
        for s, _ in self.stages[chunk][stage]:
            s()

    def wait(self, chunk, stage):
        for _, w in self.stages[chunk][stage]:
            w()

    def on(self, chunk, stage):
        self.wait(chunk, stage - 1)
        self.start(chunk, stage)


OUT_CHUNKS = ((256, 256), (512, 224))
IN_CHUNKS = ((0, 128), (128, 128), (256, 128), (384, 128), (512, 128), (640, 96))
MASKS = [(1, 0), (2, 0), (4, 0), (0, 1), (0, 2), (0, 3)]
COPIES = 180


def back_kernel(length, heads, gain1, gain2, live, geb, tops, gout, midway, sec, firstT, x, mine, whole0, h2, h3, *rest):
    Ws, qkvs, atts, lses, rest = rest[:4], rest[4:8], rest[8:12], rest[12:16], rest[16:]
    (O_out, O_in, sum_a, sum_m, vec, g_s, gm_s, acc, gT, fT, x_s, W_s, Wo, qkv_s, att_s, lse_s, ga_s, d_s, dk_s, dv_s, out_s,
     Ha, La, Hm, Lm, za, zm, vr, w0_s, l_sem, s_sem, r_sem) = rest
    cw = heads * HD
    D = g_s.shape[1]
    wires = Wires(s_sem, r_sem)
    d, z = wires.d, wires.z
    loads = {}
    order = [3, 2, 1, 0]
    names = iter(range(100))

    def load(key, src, dst):
        loads[key] = pltpu.make_async_copy(src, dst, l_sem.at[next(names)])

    load("midway", midway, acc)
    load("sec", sec, gm_s)
    load("gout", gout, g_s)
    load("firstT", firstT, fT)
    load("x", x, x_s)
    load("h2", h2, Hm.at[0])
    load("h3", h3, Hm.at[1])
    load("w0", whole0, w0_s)
    for i, k in enumerate(order):
        b = i % 2
        load(f"W{i}", Ws[k], W_s.at[b])
        load(f"qkv{i}", qkvs[k], qkv_s.at[b])
        load(f"att{i}", atts[k], att_s.at[b])
        load(f"lse{i}", lses[k], lse_s.at[b])
    for key in ("midway", "sec", "gout", "h2", "h3", "w0", "firstT", "W0", "qkv0", "att0", "lse0", "x"):
        loads[key].start()
    slot = jnp.where(z == 0, 0, jnp.where(z == 3, 1, 2))
    own_place = pl.ds(pl.multiple_of(slot * TOK, 256), TOK)
    out_rows = O_out.shape[0] // 3
    out_base = TOK - out_rows
    out_place = pl.ds(pl.multiple_of(slot * out_rows, 256), out_rows)
    used = (z == 0) | (z == 3) | (z == 1 + d % 2)
    own_out, own_in = wires.local(mine.at[pl.ds(out_base, out_rows), :], O_out.at[out_place, :], used), wires.local(g_s, O_in.at[own_place, :], used)
    share_out = Sharing(wires, mine, O_out, OUT_CHUNKS, out_base)
    share_in = Sharing(wires, g_s, O_in, IN_CHUNKS)
    sums = {"m2": Summing(wires, Hm.at[0], Lm.at[0], zm.at[0], 2), "m3": Summing(wires, Hm.at[1], Lm.at[1], zm.at[1], 3)}
    for k in range(4):
        sums[f"b{k}"] = Summing(wires, Ha.at[k], La.at[k], za.at[max(k - 1, 0)], k)
    exchange = {k: wires.swap(out_s, Ha.at[k], dp=1) for k in range(4)}
    spread = [wires.swap(vec, vr.at[i], dp=dp, z=t) for i, (dp, t) in enumerate(((1, 0), (2, 0), (4, 0), (0, 1), (0, 2)))]
    greet(d, z, MASKS)

    todo = {
        -3: [lambda: share_out.start(0, 0), own_out[0]],
        -2: [lambda: loads["h2"].wait(), sums["m2"].step1],
        0: [lambda: loads["h3"].wait(), lambda: loads["w0"].wait()],
        2: [lambda: share_out.on(0, 1), lambda: share_out.start(1, 0)],
        3: [sums["m2"].step2, sums["m3"].step1],
        5: [sums["m2"].step3],
        8: [sums["b3"].step1, lambda: share_out.on(0, 2), lambda: share_out.on(1, 1)],
        12: [sums["m3"].step2],
        13: [sums["b3"].step2],
        15: [sums["m3"].step3, sums["b3"].step3],
        18: [sums["b2"].step1, lambda: share_out.on(1, 2)],
        23: [sums["b2"].step2],
        25: [sums["b2"].step3],
        28: [sums["b1"].step1],
        33: [sums["b1"].step2],
        35: [sums["b1"].step3],
        38: [sums["b0"].step1],
    }

    def tick(t):
        for action in todo.get(t, ()):
            action()

    vec[...] = jnp.zeros_like(vec)
    for key in ("midway", "sec", "gout"):
        loads[key].wait()

    def total_of(row, value):
        vec[row:row + 1, :D] += jnp.sum(value, axis=0, keepdims=True)

    def put_row(where, lo, value):
        n = value.shape[1]
        hit = lax.broadcasted_iota(jnp.int32, (8, n), 0) == where
        vec[0:8, lo:lo + n] += jnp.where(hit, jnp.broadcast_to(value, (8, n)), 0.0)

    @pl.loop(0, TOK // RT)
    def _(i):
        for t in range(3):
            pl.when(i == t)(functools.partial(tick, t - 3))
        rows = pl.ds(pl.multiple_of(i * RT, RT), RT)
        normed, inverse = normalize(acc[rows, :])
        e = gm_s[rows, :]
        go = g_s[rows, :].astype(F32)
        scaled = e * gain2[...]
        mean1 = jnp.mean(scaled, axis=-1, keepdims=True)
        mean2 = jnp.mean(scaled * normed, axis=-1, keepdims=True)
        gm = go + inverse * (scaled - mean1 - normed * mean2)
        total_of(4, gm)
        total_of(5, go)
        total_of(8, e * normed)
        total_of(9, e)
        gm_s[rows, :] = gm
        g_s[rows, :] = gm.astype(BF)
        gT[:, rows] = gm.T.astype(BF)

    loads["firstT"].wait()
    acc[...] = jnp.zeros_like(acc)
    for i, k in enumerate(order):
        base, b = 10 * i, i % 2
        W, qkv, att, lse, H = W_s.at[b], qkv_s.at[b], att_s.at[b], lse_s.at[b], Ha.at[k]
        for key in ("W", "qkv", "att", "lse"):
            loads[f"{key}{i}"].wait()
        if i < 3:
            for key in ("W", "qkv", "att", "lse"):
                loads[f"{key}{i + 1}"].start()
        tick(base)
        Wo[...] = W[:, 3 * cw:]

        @pl.loop(0, TOK // RT)
        def _(t):
            rows = pl.ds(pl.multiple_of(t * RT, RT), RT)
            g = nn(g_s[rows, :], Wo[...]).astype(BF)
            for h in range(heads):
                ga_s[h, rows, :] = g[:, h * HD:(h + 1) * HD]

        tick(base + 1)
        dk_s[...] = jnp.zeros_like(dk_s)
        dv_s[...] = jnp.zeros_like(dv_s)
        place = z ^ k

        @pl.loop(0, TOK // RT)
        def _(t):
            for n in range(3):
                pl.when(t == n)(functools.partial(tick, base + 2 + n))
            rows = pl.ds(pl.multiple_of(t * RT, RT), RT)
            cid = lax.broadcasted_iota(jnp.int32, (1, TOK), 1)
            dqs = []
            for h in range(heads):
                q, kk, v, g = qkv[h, rows, :], qkv[heads + h], qkv[2 * heads + h], ga_s[h, rows, :]
                s = nt(q, kk)
                p = jnp.exp2(s * (SC * LOG2E) - lse[rows, h:h + 1])
                p = jnp.where(cid < length, p, 0.0)
                dp = nt(g, v)
                dd = jnp.sum(g.astype(F32) * att[rows, h * HD:(h + 1) * HD].astype(F32), axis=1, keepdims=True)
                ds = (p * (dp - dd)).astype(BF)
                dqs.append(nn(ds, kk) * SC)
                dk_s[h] += tn(ds, q)
                dv_s[h] += tn(p.astype(BF), g)
            dq = jnp.concatenate(dqs, axis=1)
            put_row(place, 0, jnp.sum(dq, axis=0, keepdims=True))
            d_s[rows, :cw] = dq.astype(BF)

        d_s[:, cw:2 * cw] = jnp.concatenate([dk_s[h] * SC for h in range(heads)], axis=1).astype(BF)
        dv = jnp.concatenate([dv_s[h] for h in range(heads)], axis=1)
        put_row(place, 384, jnp.sum(dv, axis=0, keepdims=True))
        d_s[:, 2 * cw:] = dv.astype(BF)
        put_row(place, 768, geb[k])
        put_row(place, 1920, tops[k])
        tick(base + 5)

        def write(dst, lo, hi, add):
            def put(where, val):
                if add:
                    val = val + dst[where, lo:hi].astype(F32)
                dst[where, lo:hi] = val.astype(BF)
            return put

        block_rows(fT, d_s, 0, write(out_s, 0, 3 * cw, False))
        block_rows(gT, att, 0, write(out_s, 3 * cw, 4 * cw, False))
        exchange[k][0]()
        tick(base + 6)

        @pl.loop(0, TOK // RT)
        def _(t):
            rows = pl.ds(pl.multiple_of(t * RT, RT), RT)
            acc[rows, :] += nt(d_s[rows, :], W[:, :3 * cw])

        tick(base + 7)
        exchange[k][1]()
        block_rows(fT, d_s, 1, write(H, 0, 3 * cw, True))
        block_rows(gT, att, 1, write(H, 3 * cw, 4 * cw, True))
        tick(base + 8)

    loads["x"].wait()

    @pl.loop(0, TOK // RT)
    def _(i):
        rows = pl.ds(pl.multiple_of(i * RT, RT), RT)
        normed, inverse = normalize(x_s[rows, :].astype(F32))
        e = acc[rows, :]
        scaled = e * gain1[...]
        mean1 = jnp.mean(scaled, axis=-1, keepdims=True)
        mean2 = jnp.mean(scaled * normed, axis=-1, keepdims=True)
        total_of(6, e * normed)
        total_of(7, e)
        g_s[rows, :] = ((gm_s[rows, :] + inverse * (scaled - mean1 - normed * mean2)) * live[...]).astype(BF)
        for t in range(3):
            @pl.when(i == t)
            def _():
                share_in.start(2 * t, 0)
                share_in.start(2 * t + 1, 0)

    own_in[0]()
    after = {0: [spread[0][0], sums["b0"].step2], 1: [], 2: [sums["b0"].step3]}
    row = lax.broadcasted_iota(jnp.int32, vec.shape, 1)

    def fold(i):
        spread[i][1]()
        a, c = vec[...], vr[i]
        vec[...] = jnp.where(row < 1920, a + c, jnp.maximum(a, c))
        if i < 4:
            spread[i + 1][0]()

    n = len(IN_CHUNKS)
    for t in range(n + 2):
        if t < n:
            share_in.on(t, 1)
        for action in after.get(t, ()):
            action()
        if 1 <= t <= n:
            share_in.on(t - 1, 2)
        if 1 <= t <= 5:
            fold(t - 1)
    for c in range(len(OUT_CHUNKS)):
        share_out.wait(c, 2)
    own_out[1]()
    own_in[1]()
    for s in ("m2", "m3", "b3", "b2", "b1"):
        sums[s].step4()
    r = sum_a.shape[0]
    sum_a[...] = Ha[0, :r, :].astype(F32) + za[0].astype(F32) + za[1].astype(F32) + za[2].astype(F32)
    sum_m[...] = w0_s[...] + zm[0].astype(F32) + zm[1].astype(F32)
    for c in range(n):
        share_in.wait(c, 2)


def back(number, gain1, gain2, live, geb, tops, gout, midway, sec, firstT, x, mine, whole0, h2, h3, qkvs, atts, lses, Ws, length):
    D = gout.shape[1]
    cw = Ws[0].shape[1] // 4
    cm = h2.shape[1]
    heads = cw // HD
    r = D // 8
    vm = pltpu.VMEM
    dma = pltpu.SemaphoreType.DMA
    return pl.pallas_call(
        functools.partial(back_kernel, length, heads),
        out_shape=(shape((3 * (TOK - OUT_CHUNKS[0][0]), D), BF), shape((3 * TOK, D), BF), shape((r, 4 * cw), F32), shape((r, cm), F32), shape((16, 2048), F32)),
        in_specs=[VM] * 5 + [HB] * 25,
        out_specs=(HB, HB, VM, VM, VM),
        scratch_shapes=[vm((TOK, D), BF), vm((TOK, D), F32), vm((TOK, D), F32), vm((D, TOK), BF), vm((D, TOK), BF), vm((TOK, D), BF),
                        vm((2, D, 4 * cw), BF), vm((D, cw), BF), vm((2, 3 * heads, TOK, HD), BF), vm((2, TOK, cw), BF), vm((2, TOK, 128), F32),
                        vm((heads, TOK, HD), BF), vm((TOK, 3 * cw), BF), vm((heads, TOK, HD), F32), vm((heads, TOK, HD), F32), vm((4 * r, 4 * cw), BF),
                        vm((4, 4 * r, 4 * cw), BF), vm((4, 3 * r, 4 * cw), BF), vm((2, 4 * r, cm), BF), vm((2, 3 * r, cm), BF),
                        vm((3, r, 4 * cw), BF), vm((2, r, cm), BF), vm((5, 16, 2048), F32), vm((r, cm), F32),
                        dma((32,)), dma((COPIES,)), dma((COPIES,))],
        compiler_params=pltpu.CompilerParams(vmem_limit_bytes=63 * 2**20, collective_id=number, has_side_effects=True),
        cost_estimate=pl.CostEstimate(flops=4 * 2 * TOK * (D * cw * 8 + heads * 5 * TOK * HD * 6), bytes_accessed=60 * 2**20, transcendentals=4 * heads * TOK * TOK),
        name="back",
    )(gain1, gain2, live, geb, tops, gout, midway, sec, firstT, x, mine, whole0, h2, h3, *Ws, *qkvs, *atts, *lses)


class Spreading:
    def __init__(self, wires, piece, W):
        rows = W.shape[0] // 8
        one, two = cut_rows(rows)
        d = wires.d
        at = lambda mask, lo=0, n=rows: W.at[pl.ds(pl.multiple_of((d ^ mask) * rows + lo, 16), n), :]
        self.own = wires.local(piece, at(0), d >= 0)
        self.s0 = [wires.swap(piece, at(0), dp=m) for m in (2, 4, 1)]
        self.s1 = [wires.swap(at(2, 0, one), at(2, 0, one), dp=4), wires.swap(at(4, one, two), at(4, one, two), dp=2)]
        self.s1c = [wires.swap(at(m), at(m), dp=1) for m in (2, 4)]
        self.s2 = wires.swap(at(6), at(6), dp=1)

    def step0(self):
        self.own[0]()
        for s, _ in self.s0:
            s()

    def step1(self):
        for _, w in self.s0:
            w()
        for s, _ in self.s1 + self.s1c:
            s()

    def step2(self):
        for _, w in self.s1:
            w()
        self.s2[0]()

    def finish(self):
        for _, w in self.s1c + [self.own, self.s2]:
            w()


class Moves:
    def __init__(self, sem):
        self.sem, self.made = sem, {}

    def add(self, key, src, dst):
        self.made[key] = pltpu.make_async_copy(src, dst, self.sem.at[len(self.made)])

    def start(self, *keys):
        for k in keys:
            self.made[k].start()

    def wait(self, *keys):
        for k in keys:
            self.made[k].wait()


def front_kernel(length, heads, gain1, shift1, gain2, shift2, out_b, bias_own, x, qw, kw, vw, ow, ew, st, te, *rest):
    (qkv0, qkv1, qkv2, qkv3, att0, att1, att2, att3, lse0, lse1, lse2, lse3, firstT, second, secondT, midway, Wa0, Wa1, Wa2, Wa3, Wm0, Wm1, Zm2,
     tops, bias_all, x_s, raw, ow_s, first_s, T_s, second_s, acc, W, Wm, Za, Zm1, qkv_s, att_s, lse_s, bias, l_sem, s_sem, r_sem) = rest
    cw = heads * HD
    D = x_s.shape[1]
    cut = (Wm.shape[1] - 128) // 2
    wires, moves = Wires(s_sem, r_sem), Moves(l_sem)
    d, z = wires.d, wires.z
    rows = D // 8
    own_rows = pl.ds(pl.multiple_of(d * rows, 16), rows)
    for i, ref in enumerate((qw, kw, vw)):
        moves.add(f"w{i}", ref, raw.at[i])
    moves.add("ow", ow, ow_s.at[pl.ds(0, cw), :])
    moves.add("x", x, x_s)
    moves.add("m0", ew.at[:, pl.ds(0, cut)], Wm.at[:, pl.ds(0, cut)])
    moves.add("m1", st.at[:, pl.ds(0, cut)], Wm.at[:, pl.ds(cut, cut)])
    moves.add("m2", te, Wm.at[:, pl.ds(2 * cut, 128)])
    moves.add("oW0", W.at[0], Wa0)
    moves.add("oWm", Wm, Wm0)
    for k, (a, b, c) in enumerate(((qkv0, att0, lse0), (qkv1, att1, lse1), (qkv2, att2, lse2), (qkv3, att3, lse3))):
        moves.add(f"qkv{k}", qkv_s.at[k], a)
        moves.add(f"att{k}", att_s.at[k], b)
        moves.add(f"lse{k}", lse_s.at[k], c)
    for k, ref in enumerate((Wa1, Wa2, Wa3)):
        moves.add(f"oW{k + 1}", W.at[k + 1], ref)
    moves.add("firstT", T_s, firstT)
    moves.add("second", second_s, second)
    moves.add("secondT", T_s, secondT)
    moves.add("midway", acc, midway)
    moves.start("w0", "w1", "w2", "ow", "x", "m0", "m1", "m2")

    zb = [wires.swap(bias.at[0], bias.at[k], z=k) for k in (1, 2, 3)]
    za = [wires.swap(W.at[0, own_rows, :], Za.at[0], z=1), wires.swap(W.at[0, own_rows, :], Za.at[1], z=2), wires.swap(Za.at[1], Za.at[2], z=1)]
    zm = [wires.swap(Wm.at[own_rows, :], Zm1, z=1), wires.swap(Wm.at[own_rows, :], Zm2, z=2)]
    ga = {k: Spreading(wires, Za.at[k - 1], W.at[k]) for k in (1, 2, 3)}
    gm = Spreading(wires, Zm1, Wm1)
    greet(d, z, MASKS)
    bias[0] = bias_own[...]
    for s, _ in zb:
        s()
    moves.wait("w0", "w1", "w2", "ow")

    @pl.loop(0, D // 384)
    def _(i):
        part = pl.ds(pl.multiple_of(i * 384, 128), 384)
        turned = ow_s[:, part].astype(F32).T[:, :cw].astype(BF)
        W[0, part, :] = jnp.concatenate([raw[0, part, :], raw[1, part, :], raw[2, part, :], turned], axis=1)

    za[0][0]()
    za[1][0]()
    moves.start("oW0")
    moves.wait("m0", "m1", "m2")
    moves.start("oWm")
    moves.wait("x")

    @pl.loop(0, TOK // RT)
    def _(i):
        part = pl.ds(pl.multiple_of(i * RT, RT), RT)
        xt = x_s[part, :].astype(F32)
        normed, _ = normalize(xt)
        f = normed * gain1[...] + shift1[...]
        first_s[part, :] = f.astype(BF)
        T_s[:, part] = f.T.astype(BF)
        acc[part, :] = xt + out_b[...]

    moves.start("firstT")
    for _, w in zb:
        w()
    bias_all[...] = bias[...]

    def z_a3():
        za[1][1]()
        za[2][0]()

    todo = {
        0: [za[0][1], ga[1].step0, zm[0][0]],
        2: [],
        3: [ga[1].step1],
        4: [z_a3, ga[2].step0, ga[1].step2],
        10: [],
        11: [ga[2].step1, zm[1][0]],
        12: [za[2][1], ga[3].step0],
        13: [ga[2].step2],
        20: [zm[0][1], gm.step0],
        21: [ga[3].step1],
        23: [ga[3].step2],
        31: [gm.step1],
        34: [gm.step2],
    }

    def tick(t):
        for action in todo.get(t, ()):
            action()

    for k in range(4):
        base = 10 * k
        Wk, qkv, att, lse = W.at[k], qkv_s.at[k], att_s.at[k], lse_s.at[k]
        if k:
            ga[k].finish()
            moves.start(f"oW{k}")
        tick(base)
        qb, vb = bias[k, 0:1, :cw], bias[k, 0:1, 384:384 + cw]

        @pl.loop(0, TOK // RT)
        def _(i):
            part = pl.ds(pl.multiple_of(i * RT, RT), RT)
            t = nn(first_s[part, :], Wk[:, :3 * cw])
            q = (t[:, :cw] + qb).astype(BF)
            kk = t[:, cw:2 * cw].astype(BF)
            v = (t[:, 2 * cw:] + vb).astype(BF)
            for h in range(heads):
                qkv[h, part, :] = q[:, h * HD:(h + 1) * HD]
                qkv[heads + h, part, :] = kk[:, h * HD:(h + 1) * HD]
                qkv[2 * heads + h, part, :] = v[:, h * HD:(h + 1) * HD]

        tick(base + 1)
        moves.start(f"qkv{k}")
        tops[k] = jnp.full(tops.shape[1:], -1e30, F32)

        @pl.loop(0, TOK // RT)
        def _(i):
            for n in range(3):
                pl.when(i == n)(functools.partial(tick, base + 2 + n))
            part = pl.ds(pl.multiple_of(i * RT, RT), RT)
            rid = lax.broadcasted_iota(jnp.int32, (RT, 1), 0) + i * RT
            cid = lax.broadcasted_iota(jnp.int32, (1, TOK), 1)
            res = []
            for h in range(heads):
                s = nt(qkv[h, part, :], qkv[heads + h])
                s = jnp.where(cid < length, s, -1e30)
                m = jnp.max(s, axis=1, keepdims=True)
                e = jnp.exp2((s - m) * (SC * LOG2E))
                l = jnp.sum(e, axis=1, keepdims=True)
                o = nn(e.astype(BF), qkv[2 * heads + h]) * (1.0 / l)
                res.append(o.astype(BF))
                lse[part, h:h + 1] = m * (SC * LOG2E) + jnp.log2(l)
                tops[k, h:h + 1, :] = jnp.maximum(tops[k, h:h + 1, :], jnp.max(jnp.where(rid < length, m, -1e30)) * SC)
            a = jnp.concatenate(res, axis=1)
            att[part, :] = a
            acc[part, :] += nt(a, Wk[:, 3 * cw:])

        moves.start(f"att{k}", f"lse{k}")

    moves.start("midway")
    moves.wait("firstT")

    @pl.loop(0, TOK // RT)
    def _(i):
        part = pl.ds(pl.multiple_of(i * RT, RT), RT)
        normed, _ = normalize(acc[part, :])
        f = normed * gain2[...] + shift2[...]
        second_s[part, :] = f.astype(BF)
        T_s[:, part] = f.T.astype(BF)

    moves.start("second", "secondT")
    gm.finish()
    zm[1][1]()
    for k in range(4):
        moves.wait(f"qkv{k}", f"att{k}", f"lse{k}", f"oW{k}")
    moves.wait("oWm", "second", "secondT", "midway")


def front(number, gain1, shift1, gain2, shift2, out_b, bias_own, x, qw, kw, vw, ow, ew, st, te, length):
    D, cw = qw.shape
    heads = cw // HD
    cut = ew.shape[1] // 128 * 128
    cm = 2 * cut + 128
    r = D // 8
    vm = pltpu.VMEM
    dma = pltpu.SemaphoreType.DMA
    four = lambda s: (s,) * 4
    got = pl.pallas_call(
        functools.partial(front_kernel, length, heads),
        out_shape=(*four(shape((3 * heads, TOK, HD), BF)), *four(shape((TOK, cw), BF)), *four(shape((TOK, 128), F32)),
                   shape((D, TOK), BF), shape((TOK, D), BF), shape((D, TOK), BF), shape((TOK, D), F32), *four(shape((D, 4 * cw), BF)),
                   shape((D, cm), BF), shape((D, cm), BF), shape((r, cm), BF), shape((4, heads, 128), F32), shape((4, 8, 2048), F32)),
        in_specs=[VM] * 6 + [HB] * 8,
        out_specs=(HB,) * 23 + (VM,) * 2,
        scratch_shapes=[vm((TOK, D), BF), vm((3, D, cw), BF), vm((384, D), BF), vm((TOK, D), BF), vm((D, TOK), BF), vm((TOK, D), BF), vm((TOK, D), F32),
                        vm((4, D, 4 * cw), BF), vm((D, cm), BF), vm((3, r, 4 * cw), BF), vm((r, cm), BF), vm((4, 3 * heads, TOK, HD), BF),
                        vm((4, TOK, cw), BF), vm((4, TOK, 128), F32), vm((4, 8, 2048), F32), dma((32,)), dma((64,)), dma((64,))],
        compiler_params=pltpu.CompilerParams(vmem_limit_bytes=62 * 2**20, collective_id=number, has_side_effects=True),
        cost_estimate=pl.CostEstimate(flops=4 * 2 * TOK * (D * cw * 4 + heads * 2 * TOK * HD * 6), bytes_accessed=60 * 2**20, transcendentals=4 * heads * TOK * TOK),
        name="front",
    )(gain1, shift1, gain2, shift2, out_b, bias_own, x, qw, kw, vw, ow, ew, st, te)
    return got[:4], got[4:8], got[8:12], got[12:16], got[16:20], got[20:23], got[23], got[24]


def middle_kernel(fw, live, shrink_b, bias_all, second, secondT, gout, goutT, midway, Wm0, Wm1, Zm2, *rest):
    (mine, sec, O0, H2, H3, geb, part_sum, Wg2, Wg3, Zm3, second_s, secondT_s, gout_s, goutT_s, mlp, sec_s, mine_s, tail_s, E, ST, act_s, slope_s, gpre_s, out_s,
     Hm, Lm, zr, l_sem, s_sem, r_sem) = rest
    D = second_s.shape[1]
    cut = fw // 128 * 128
    tail = fw - cut
    r = D // 8
    wires, moves = Wires(s_sem, r_sem), Moves(l_sem)
    d, z = wires.d, wires.z
    Ws = (Wm0, Wm1, Wg2, Wg3)
    for key, a, b in (("second", second, second_s), ("secondT", secondT, secondT_s), ("gout", gout, gout_s), ("goutT", goutT, goutT_s), ("midway", midway, mlp)):
        moves.add(key, a, b)
    for k in range(4):
        moves.add(f"E{k}", Ws[k].at[:, pl.ds(0, cut)], E.at[k % 2, :, pl.ds(0, cut)])
        moves.add(f"S{k}", Ws[k].at[:, pl.ds(cut, cut)], ST.at[k % 2, :, pl.ds(0, cut)])
        moves.add(f"T{k}", Ws[k].at[:, pl.ds(2 * cut, 128)], tail_s.at[k % 2])
    moves.add("mine", mine_s, mine)
    moves.add("sec", sec_s, sec)
    moves.add("h2", Hm.at[2], H2)
    moves.add("h3", Hm.at[3], H3)
    slot = jnp.where(z == 0, 0, jnp.where(z == 3, 1, 2))
    used = (z == 0) | (z == 3) | (z == 1 + d % 2)
    n0 = O0.shape[0] // 3
    own_out = wires.local(mine_s.at[pl.ds(0, n0), :], O0.at[pl.ds(pl.multiple_of(slot * n0, 256), n0), :], used)
    share = Sharing(wires, mine_s, O0, ((0, n0),))
    z3 = wires.swap(Zm2, Zm3, z=1)
    g2, g3 = Spreading(wires, Zm2, Wg2), Spreading(wires, Zm3, Wg3)
    exchange = [wires.swap(out_s, Hm.at[k], dp=1) for k in range(4)]
    sums = [Summing(wires, Hm.at[k], Lm.at[k], zr, k) for k in (0, 1)]
    moves.start("second", "E0", "S0", "T0", "midway", "gout", "goutT", "secondT")
    greet(d, z, MASKS)
    z3[0]()
    g2.step0()
    sec_s[...] = jnp.zeros_like(sec_s)
    geb[...] = jnp.zeros_like(geb)
    moves.wait("second", "midway")

    def forward(k, tick):
        b = k % 2
        moves.wait(f"E{k}", f"S{k}", f"T{k}")
        lane = lax.broadcasted_iota(jnp.int32, (D, 128), 1)
        last = tail_s[b]
        E[b, :, cut:] = jnp.where(lane < tail, last, jnp.zeros_like(last))
        moved = jnp.concatenate([last[:, tail:2 * tail], jnp.zeros((D, 128 - tail), BF)], axis=1)
        ST[b, :, cut:] = moved
        eb = bias_all[k, 0:1, 768:768 + cut + 128]

        @pl.loop(0, TOK // RT)
        def _(i):
            tick(i)
            rows = pl.ds(pl.multiple_of(i * RT, RT), RT)
            act, slope = gelu_parts(nn(second_s[rows, :], E[b]) + eb)
            act_s[b, rows, :] = act.astype(BF)
            slope_s[b, rows, :] = slope.astype(BF)
            mlp[rows, :] += nt(act_s[b, rows, :], ST[b])

    def grads(k, half):
        b = k % 2
        for t in range(2):
            q = 4 * t + 1 - half
            lhs = lambda ref: jnp.concatenate([ref[pl.ds(pl.multiple_of((d ^ p) * r, 16), r), :] for p in (q, q + 2)], axis=0)
            place = pl.ds(t * 2 * r, 2 * r)
            ve, vs = nn(lhs(secondT_s), gpre_s[...]), nn(lhs(goutT_s), act_s[b])
            last = jnp.concatenate([ve[:, cut:fw], vs[:, cut:fw], jnp.zeros((2 * r, 128 - 2 * tail), F32)], axis=1)
            to = out_s if half == 0 else Hm.at[k]
            for lo, v in ((0, ve[:, :cut]), (cut, vs[:, :cut]), (2 * cut, last)):
                n = v.shape[1]
                if half:
                    v = v + to[place, lo:lo + n].astype(F32)
                to[place, lo:lo + n] = v.astype(BF)

    def backward(k, tick):
        b = k % 2

        @pl.loop(0, TOK // RT)
        def _(i):
            tick(i)
            rows = pl.ds(pl.multiple_of(i * RT, RT), RT)
            gp = nn(gout_s[rows, :], ST[b]) * slope_s[b, rows, :].astype(F32)
            geb[k] += jnp.sum(gp, axis=0, keepdims=True)
            gpre_s[rows, :] = gp.astype(BF)

        grads(k, 0)
        exchange[k][0]()

        @pl.loop(0, TOK // RT)
        def _(i):
            tick(i + 3)
            rows = pl.ds(pl.multiple_of(i * RT, RT), RT)
            sec_s[rows, :] += nt(gpre_s[rows, :], E[b])

        exchange[k][1]()
        grads(k, 1)

    def ticks(table):
        def tick(i):
            for n, actions in table.items():
                def run():
                    for a in actions:
                        a()
                pl.when(i == n)(run)
        return tick

    none = ticks({})
    moves.start("E1", "S1", "T1")
    forward(0, none)
    moves.wait("gout", "goutT", "secondT")
    backward(0, ticks({0: [g2.step1], 2: [z3[1], g3.step0], 3: [g2.step2]}))
    g2.finish()
    moves.start("E2", "S2", "T2")
    sums[0].step1()
    forward(1, ticks({2: [g3.step1]}))
    backward(1, ticks({0: [g3.step2], 2: [sums[0].step2], 4: [sums[0].step3]}))
    g3.finish()
    moves.start("E3", "S3", "T3")
    sums[1].step1()
    forward(2, none)
    forward(3, ticks({1: [sums[1].step2]}))

    @pl.loop(0, TOK // RT)
    def _(i):
        rows = pl.ds(pl.multiple_of(i * RT, RT), RT)
        mine_s[rows, :] = ((mlp[rows, :] + shrink_b[...]) * live[...]).astype(BF)
        pl.when(i == 0)(lambda: share.start(0, 0))

    own_out[0]()
    moves.start("mine")
    backward(2, ticks({0: [sums[1].step3], 4: [lambda: share.on(0, 1)]}))
    moves.start("h2")
    backward(3, ticks({2: [lambda: share.on(0, 2)]}))
    moves.start("h3", "sec")
    sums[1].step4()
    part_sum[...] = Hm[0, :r, :].astype(F32) + zr[...].astype(F32)
    share.wait(0, 2)
    own_out[1]()
    moves.wait("h2", "h3", "sec", "mine")


def middle(number, fw, live, shrink_b, bias_all, second, secondT, gout, goutT, midway, Wm0, Wm1, Zm2):
    D = second.shape[1]
    cut = fw // 128 * 128
    wide = cut + 128
    cm = 2 * cut + 128
    r = D // 8
    n0 = OUT_CHUNKS[0][0]
    vm = pltpu.VMEM
    dma = pltpu.SemaphoreType.DMA
    got = pl.pallas_call(
        functools.partial(middle_kernel, fw),
        out_shape=(shape((TOK, D), BF), shape((TOK, D), F32), shape((3 * n0, D), BF), shape((4 * r, cm), BF), shape((4 * r, cm), BF), shape((4, 1, wide), F32), shape((r, cm), F32),
                   shape((D, cm), BF), shape((D, cm), BF), shape((r, cm), BF)),
        in_specs=[VM] * 3 + [HB] * 8,
        out_specs=(HB,) * 5 + (VM,) * 2 + (HB,) * 3,
        scratch_shapes=[vm((TOK, D), BF), vm((D, TOK), BF), vm((TOK, D), BF), vm((D, TOK), BF), vm((TOK, D), F32), vm((TOK, D), F32), vm((TOK, D), BF), vm((2, D, 128), BF),
                        vm((2, D, wide), BF), vm((2, D, wide), BF), vm((2, TOK, wide), BF), vm((2, TOK, wide), BF), vm((TOK, wide), BF), vm((4 * r, cm), BF),
                        vm((4, 4 * r, cm), BF), vm((2, 3 * r, cm), BF), vm((r, cm), BF), dma((32,)), dma((72,)), dma((72,))],
        compiler_params=pltpu.CompilerParams(vmem_limit_bytes=63 * 2**20, collective_id=number, has_side_effects=True),
        cost_estimate=pl.CostEstimate(flops=4 * 2 * 9 * TOK * D * fw, bytes_accessed=60 * 2**20, transcendentals=4 * TOK * fw),
        name="middle",
    )(live, shrink_b, bias_all, second, secondT, gout, goutT, midway, Wm0, Wm1, Zm2)
    return got[:7]


class General:
    def __init__(self, groups, attn_own, mlp_own):
        self.groups = groups
        self.attn, self.mlp = self.spread(attn_own), self.spread(mlp_own)

    def vectors(self, own):
        every = lax.all_gather(own, "tensor")
        return [every[i] for i in range(self.groups)]

    def spread(self, own):
        d, count = lax.axis_index("dp"), lax.axis_size("dp")
        rows = own.shape[0] // count
        piece = lax.dynamic_slice_in_dim(own, d * rows, rows, 0)
        piece = lax.all_gather(piece, "tensor")
        whole = lax.all_gather(piece, "dp", axis=1, tiled=True)
        return [whole[i] for i in range(self.groups)]

    def reduce(self, parts):
        part = lax.psum_scatter(jnp.stack(parts), "dp", scatter_dimension=1, tiled=True)
        return lax.psum_scatter(part, "tensor", scatter_dimension=0, tiled=True)[0].astype(F32)

    def collect(self, grad_attn, grad_mlp):
        return self.reduce(grad_attn), self.reduce(grad_mlp)

    def by_index(self, items):
        return jnp.stack(items)

    def share(self, mine):
        every = lax.all_gather(mine, "tensor")
        middle = 1 + lax.axis_index("dp") % 2
        return jnp.stack([every[0], every[self.groups - 1], lax.dynamic_index_in_dim(every, middle, 0, keepdims=False)])


def shards(images, counts, cotangent, query_w, query_b, key_w, value_w, value_b, out_w, out_b, norm1_gain, norm1_shift,
           norm2_gain, norm2_shift, expand_w, expand_b, shrink_w, shrink_b):
    slots, length, width = images.shape
    groups = lax.axis_size("tensor")
    d, z = lax.axis_index("dp"), lax.axis_index("tensor")
    cw, fw = query_w.shape[1], expand_w.shape[1]
    heads = cw // HD
    cut = fw // 128 * 128
    slot, used = slot_table(d, groups)
    live = jnp.where(used & (slot < counts[0]), 1.0, 0.0).astype(F32)
    pad = lambda a: jnp.pad(a, ((0, TOK - length), (0, 0)))

    x_low = pad(lax.dynamic_index_in_dim(images, slot, 0, keepdims=False))
    gout = pad(lax.dynamic_index_in_dim(cotangent, slot, 0, keepdims=False)) * live.astype(BF)
    gout_t = gout.T
    shrink_t = shrink_w.T
    if (groups, lax.axis_size("dp")) == (4, 8):
        one = lambda a: a[None]
        blank = lambda n: jnp.zeros((n,), F32)
        bias_own = jnp.concatenate([query_b, blank(384 - cw), value_b, blank(384 - cw), expand_b, blank(1280 - fw)])
        tail_own = jnp.concatenate([expand_w[:, cut:], shrink_t[:, cut:], jnp.zeros((width, 128 - 2 * (fw - cut)), BF)], axis=1)
        qkvs, atts, lses, (first_t, second, second_t, midway), attn_ws, mlp_ws, tops, bias_all = front(
            0, one(norm1_gain), one(norm1_shift), one(norm2_gain), one(norm2_shift), one(out_b), jnp.broadcast_to(bias_own, (8, 2048)),
            x_low, query_w, key_w, value_w, out_w, expand_w, shrink_t, tail_own, length)
        mine, sec, out_low, h2, h3, geb, part_sum = middle(1, fw, live[None, None], one(shrink_b), bias_all, second, second_t, gout, gout_t, midway, *mlp_ws)
        out_high, in_all, sum_attn, sum_mlp, vec = back(
            2, one(norm1_gain), one(norm2_gain), live[None, None], geb, jnp.where(live > 0.0, tops[:, :, 0], -1e30)[:, None],
            gout, midway, sec, first_t, x_low, mine, part_sum, h2, h3, qkvs, atts, lses, attn_ws, length)
        outputs = jnp.concatenate([out_low.reshape(3, -1, width), out_high.reshape(3, -1, width)], axis=1)[:, :length]
        input_grads = in_all.reshape(3, TOK, width)[:, :length].astype(F32)
        own = lax.dynamic_index_in_dim(vec, z, 0, keepdims=False)
        grad_query_b, grad_value_b, grad_expand_b, logit_top = own[:cw], own[384:384 + cw], own[768:768 + fw], own[1920:1920 + heads]
        tail = [vec[4 + i, :width] for i in range(6)]
    else:
        attn_own = jnp.concatenate([query_w, key_w, value_w, out_w.T], axis=1)
        mlp_own = jnp.concatenate([expand_w[:, :cut], shrink_t[:, :cut], expand_w[:, cut:], shrink_t[:, cut:]], axis=1)
        net = General(groups, attn_own, mlp_own)
        biases = net.vectors(jnp.concatenate([query_b, value_b, expand_b]))

        x = x_low.astype(F32)
        normed1, inverse1 = normalize(x)
        first = (normed1 * norm1_gain + norm1_shift).astype(BF)
        first_t = first.T
        acc = x + out_b
        kept, tops = [], []
        for k in range(groups):
            b = biases[k]
            qkv, att, lse, top, acc = attn_fwd(first, net.attn[k], b[None, :cw], b[None, cw:2 * cw], acc, length)
            kept.append((qkv, att, lse))
            tops.append(top[:, 0])
        midway = acc
        normed2, inverse2 = normalize(midway)
        second = (normed2 * norm2_gain + norm2_shift).astype(BF)
        second_t = second.T
        mlp = midway + shrink_b
        sec = jnp.zeros((TOK, width), F32)
        grad_mlp, geb = [], []
        for k in range(groups):
            grad, g_b, mlp, sec = mlp_call(second, second_t, gout, gout_t, net.mlp[k], biases[k][None, 2 * cw:], mlp, sec)
            grad_mlp.append(grad)
            geb.append(g_b[0, :fw])
        back2, gn2g, gn2s = norm_back(sec, normed2, inverse2, norm2_gain)
        gout32 = gout.astype(F32)
        gmid = gout32 + back2
        gmid_low = gmid.astype(BF)
        gmid_t = gmid_low.T
        acc = jnp.zeros((TOK, width), F32)
        grad_attn, gqb, gvb = [None] * groups, [None] * groups, [None] * groups
        for k in reversed(range(groups)):
            grad, g_q, g_v, acc = attn_bwd(gmid_low, gmid_t, first_t, net.attn[k], *kept[k], acc, length)
            grad_attn[k], gqb[k], gvb[k] = grad, g_q[0], g_v[0]
        back1, gn1g, gn1s = norm_back(acc, normed1, inverse1, norm1_gain)
        input_grad = ((gmid + back1) * live)[:length].astype(BF)

        outputs = net.share((mlp[:length] * live).astype(BF))
        input_grads = net.share(input_grad).astype(F32)
        sum_attn, sum_mlp = net.collect(grad_attn, grad_mlp)
        flat = lambda items: net.by_index(items).reshape(-1)
        vector = jnp.concatenate([flat(gqb), flat(gvb), flat(geb), jnp.sum(gmid, axis=0), jnp.sum(gout32, axis=0), gn1g, gn1s, gn2g, gn2s])
        vector = lax.psum(vector, ("dp", "tensor"))
        part = lambda start, size: lax.dynamic_slice_in_dim(vector, start, size, 0)
        whole, hidden = cw * groups, fw * groups
        tail = [vector[2 * whole + hidden + i * width:][:width] for i in range(6)]
        logit_top = lax.pmax(jnp.where(live > 0.0, net.by_index(tops), -1e30), ("dp", "tensor"))
        logit_top = lax.dynamic_index_in_dim(logit_top, z, 0, keepdims=False)
        grad_query_b, grad_value_b, grad_expand_b = part(z * cw, cw), part(whole + z * cw, cw), part(2 * whole + z * fw, fw)
    factor = jnp.sqrt(clip_limit / jnp.maximum(logit_top, clip_limit))
    column_factor = jnp.repeat(factor, HD)
    clipped_query = (query_w.astype(F32) * column_factor).astype(BF)
    clipped_key = (key_w.astype(F32) * column_factor).astype(BF)
    unpack = lambda a, i: jnp.concatenate([a[:, i * cut:(i + 1) * cut], a[:, 2 * cut + i * (fw - cut):][:, :fw - cut]], axis=1)
    return (outputs, input_grads, sum_attn[:, :cw], grad_query_b, sum_attn[:, cw:2 * cw], sum_attn[:, 2 * cw:3 * cw], grad_value_b,
            sum_attn[:, 3 * cw:].T, tail[0], tail[2], tail[3], tail[4], tail[5], unpack(sum_mlp, 0), grad_expand_b, unpack(sum_mlp, 1).T,
            tail[1], clipped_query, clipped_key)


def solution(mesh):
    columns, rows, vector = P(None, "tensor"), P("tensor", None), P("tensor")
    whole = P("dp", None, None)
    return jax.shard_map(
        shards, mesh=mesh,
        in_specs=(whole, P("dp"), whole, columns, vector, columns, columns, vector, rows, P(), P(), P(), P(), P(), columns, vector, rows, P()),
        out_specs=(whole, whole, P("dp", "tensor"), vector, P("dp", "tensor"), P("dp", "tensor"), vector, P("tensor", "dp"), P(), P(), P(), P(), P(),
                   P("dp", "tensor"), vector, P("tensor", "dp"), P(), columns, columns),
        check_vma=False)
```

time: 695 us -> 538 us (0.77)
  local copies, waits for them, and re-layouts: 101 us -> 37.6 us
  Pallas kernels: 537 us -> 476 us
  other arithmetic: 40.4 us -> 17.6 us
    pallas_call x8 -> x2, Pallas kernels: 280 us -> 235 us  [the longest x1 138 us: middle(): pl.pallas_call(functools.partial(middle_kernel, fw), out_shape=(shape((TO...]
    pallas_call x1, Pallas kernels: 257 us -> 242 us  [back(): pl.pallas_call(functools.partial(back_kernel, length, heads), out_shape=(...]
    concatenate x4 -> x2, local copies, waits for them, and re-layouts: 15.5 us -> 0.88 us  [the longest x1 0.8 us: shards(): jnp.concatenate([query_b, blank(384 - cw), value_b, blank(384 - cw), expa...]
    unnamed x98 -> x19, local copies, waits for them, and re-layouts: 30.1 us -> 15.6 us
    slice x13 -> x0, local copies, waits for them, and re-layouts: 13 us -> none  [the longest x1 3.45 us: shards(): shrink_t[:, :cut]]
    another operation x7 -> x0, other arithmetic: 6.97 us -> none
  transfers between devices with their start and end apart: 3 -> 0, of which waited for: 0 -> 0; matrix products, arithmetic and copies ran while one was open for 10% -> 0% of each run, Pallas kernels for 11% -> 0%
where the time goes in v4:
time: 538 us; the launch traced here: 533 us
  Pallas kernels  476 us (88%)
  local copies, waits for them, and re-layouts  37.6 us (7%)
  other arithmetic  17.6 us (3%)
    pallas_call x1, Pallas kernels, back(): pl.pallas_call(functools.partial(back_kernel, length, heads), out_shape=(...  242 us
    pallas_call x1, Pallas kernels, middle(): pl.pallas_call(functools.partial(middle_kernel, fw), out_shape=(shape((TO...  138 us
    pallas_call x1, Pallas kernels, front(): pl.pallas_call(functools.partial(front_kernel, length, heads), out_shape=...  96.9 us
    unnamed x19, local copies, waits for them, and re-layouts  15.6 us

profile of v4, /device:TPU:1, one launch (start us, length us, event | category | flops | bytes accessed | tf_op | source)
XLA Modules:
  0.0 533.3 jit_solution(9890388407076511262)
XLA Ops:
  0.7 0.0 copy-start.3
  1.4 0.1 pad.17.clone
  1.5 1.3 broadcast_in_dim.43.gain1
  2.8 1.3 broadcast_in_dim.45.gain2
  4.1 1.3 broadcast_in_dim.47.out_b
  5.4 1.3 broadcast_in_dim.44.shift1
  6.7 1.3 broadcast_in_dim.46.shift2
  8.0 1.3 broadcast_in_dim.42.shrink_b
  9.3 0.8 concatenate.15
  10.1 0.6 broadcast_in_dim.49.bias_own
  10.7 2.4 copy.49.vw
  13.1 2.3 copy.47.qw
  15.4 0.0 copy-done.3
  15.4 1.3 copy.48.kw
  16.7 4.1 copy.50.ew
  20.8 0.0 copy-start.1
  20.8 5.5 %copy.45 = bf16[1076,1152]{0,1:T(8,128)(2,1)} copy(bf16[1076,1152]{1,0:T(8,128)(2,1)} %param.34) | data formatting | bytes 4958208 | tf_op args[16]
  26.3 0.0 copy-done.1
  26.3 1.0 slice.110
  27.3 0.9 maximum_maximum_fusion.te
  28.2 2.2 dynamic-slice_bitcast_fusion
  30.4 1.3 pad.7.x
  31.7 1.6 fusion.1
  33.3 2.3 copy.51.goutT
  35.6 96.9 %front.1 = (bf16[12,768,72]{2,1,0:T(8,128)(2,1)}, bf16[12,768,72]{2,1,0:T(8,128)(2,1)}, bf16[12,768,72]{2,1,0:T(8,128)(2,1)}, bf16[12,768,72]{2,1,0:T(8,128)(2,1...) custom-call(f32[1,1152]{1,0:T(1,128)} %broadcast_in_dim.43.gain1, ...), custom_call_target="tpu_custom_call" | custom-call | flops 24461180928 | bytes 62914560 | tf_op jit(solution)/shard_map/front/pallas_call | solution.py:882
  132.5 1.4 select_reduce_fusion
  133.8 137.7 %middle.1 = (bf16[768,1152]{1,0:T(8,128)(2,1)}, f32[768,1152]{1,0:T(8,128)}, bf16[768,1152]{1,0:T(8,128)(2,1)}, bf16[576,2176]{1,0:T(8,128)(2,1)}, bf16[576,2176...) custom-call(f32[1,1]{1,0:T(1,128)} %bitcast.1.live, ...), custom_call_target="tpu_custom_call" | custom-call | flops 68542267392 | bytes 62914560 | tf_op jit(solution)/shard_map/middle/pallas_call | solution.py:1046
  271.6 241.7 %back.1 = (bf16[1536,1152]{1,0:T(8,128)(2,1)}, bf16[2304,1152]{1,0:T(8,128)(2,1)}, f32[144,1152]{1,0:T(8,128)}, f32[144,2176]{1,0:T(8,128)}, f32[16,2048]{1,0:T(8,128)}) custom-call(f32[1,1152]{1,0:T(1,128)} %broadcast_in_dim.43.gain1, f32[1,1152]{1,0:T(1,128)} %broadcast_in_dim.45.gain2, f32[1,1]{1,0:T(1,128)} %bitcast.1.live, ...), custom_call_target="tpu_custom_call" | custom-call | flops 57076088832 | bytes 62914560 | tf_op jit(solution)/shard_map/back/pallas_call | solution.py:645
  513.3 0.8 sqrt_bitcast_fusion
  514.0 5.3 pad_maximum_fusion
  519.3 0.1 broadcast_in_dim.52
  519.4 0.1 mul.24
  519.5 1.4 dynamic-slice_reduce_fusion.1
  520.9 1.5 dynamic-slice_reduce_fusion
  522.3 1.6 slice_reduce_fusion
  524.0 0.0 copy-done.5
  524.0 0.1 fusion.3
  524.0 0.1 fusion.2
  524.2 0.0 copy-start.2
  524.2 0.0 copy-start.4
  524.2 0.9 maximum_bitcast_fusion
  525.1 0.9 pad_maximum_fusion.1
  526.0 0.0 copy-done.6
  526.0 1.1 slice_bitcast_fusion
  527.1 0.0 copy-done.2
  527.1 1.3 multiply_convert_fusion
  528.4 0.0 copy-done
  528.4 4.6 slice_convert_fusion
  (8 shorter events, 0.0 us)
Async XLA Ops:
  0.7 14.8 %copy-start.3 = (bf16[1152,288]{0,1:T(8,128)(2,1)S(1)}, bf16[1152,288]{0,1:T(8,128)(2,1)}, u32[]{:S(2)}) copy-start(bf16[1152,288]{0,1:T(8,128)(2,1)} %param.23) | copy-start | bytes 1990660
  20.8 5.5 %copy-start.1 = (bf16[1152,1076]{1,0:T(8,128)(2,1)}, bf16[1152,1076]{1,0:T(8,128)(2,1)S(1)}, u32[]{:S(2)}) copy-start(bf16[1152,1076]{1,0:T(8,128)(2,1)S(1)} %copy.50.ew) | copy-start | bytes 7437316
  514.0 9.9 %copy-start.5 = (f32[144,2176]{1,0:T(8,128)S(1)}, f32[144,2176]{1,0:T(8,128)}, u32[]{:S(2)}) copy-start(f32[144,2176]{1,0:T(8,128)} %get-tuple-element.92) | copy-start | bytes 3760132
  524.0 2.0 copy-start.6
  524.2 2.9 copy-start.2
  524.2 2.9 copy-start.4
  525.1 3.3 copy-start

commit v5 on v4

--- a/solution.py
+++ b/solution.py
@@ -319,8 +319,8 @@
 
 
 class Summing:
-    def __init__(self, wires, H, land, zr, k):
-        self.H, self.k = H, k
+    def __init__(self, wires, H, land):
+        self.H = H
         self.rows = r = H.shape[0] // 4
         self.one, self.two = one, two = cut_rows(r)
         ax, by = land.at[pl.ds(0, 2 * one), :], land.at[pl.ds(2 * one, 2 * two), :]
@@ -331,7 +331,6 @@
         self.c1 = [wires.swap(h(r, one), at(land, 0, one), dp=2), wires.swap(h(3 * r, one), at(land, one, one), dp=2),
                    wires.swap(h(2 * r + one, two), at(land, 2 * one, two), dp=4), wires.swap(h(3 * r + one, two), at(land, 2 * one + two, two), dp=4)]
         self.c2 = [wires.swap(h(2 * r, one), ay, dp=4), wires.swap(h(r + one, two), bx, dp=2)]
-        self.c3 = [wires.swap(h(0, r), zr, z=k)] if k else []
 
     def add(self, lo, n, *froms):
         total = self.H[lo:lo + n, :].astype(F32)
@@ -358,12 +357,47 @@
             w()
         self.add(0, one, 0, 2 * r)
         self.add(one, two, 2 * one, 2 * r + one)
-        for s, _ in self.c3:
+
+
+ENDS = ((0, None), (3, None))
+INNER = ((1, None), (2, None))
+
+
+class LineSum:
+    def __init__(self, wires, parts, land):
+        self.parts, self.land = parts, land
+        self.inner = (wires.z == 1) | (wires.z == 2)
+        self.a = {k: wires.swap(parts[k], land.at[k - 1], z=1, sends=ENDS) for k in (1, 2, 3)}
+        self.b = [wires.swap(parts[3], land.at[3], z=3, sends=INNER), wires.swap(parts[2], land.at[4], z=3, sends=INNER)]
+        self.g = wires.swap(parts[1], land.at[0], z=1, sends=INNER)
+
+    def alpha(self, k):
+        self.a[k][0]()
+
+    def add(self, k, i):
+        @pl.when(self.inner)
+        def _():
+            self.parts[k][...] = (self.parts[k][...].astype(F32) + self.land[i].astype(F32)).astype(BF)
+
+    def beta(self):
+        self.a[2][1]()
+        self.a[3][1]()
+        self.add(3, 1)
+        self.add(2, 2)
+        for s, _ in self.b:
             s()
 
-    def step4(self):
-        for _, w in self.c3:
+    def gamma(self):
+        for _, w in self.b:
             w()
+        self.a[1][1]()
+        self.add(1, 4)
+        self.g[0]()
+
+    def total(self, own):
+        self.g[1]()
+        other = jnp.where(self.inner, self.land[3].astype(F32), 0.0)
+        return own + self.land[0].astype(F32) + other
 
 
 class Sharing:
@@ -400,10 +434,10 @@
 COPIES = 180
 
 
-def back_kernel(length, heads, gain1, gain2, live, geb, tops, gout, midway, sec, firstT, x, mine, whole0, h2, h3, *rest):
+def back_kernel(length, heads, gain1, gain2, live, geb, tops, gout, midway, sec, firstT, x, mine, whole0, h1, h2, h3, *rest):
     Ws, qkvs, atts, lses, rest = rest[:4], rest[4:8], rest[8:12], rest[12:16], rest[16:]
-    (O_out, O_in, sum_a, sum_m, vec, g_s, gm_s, acc, gT, fT, x_s, W_s, Wo, qkv_s, att_s, lse_s, ga_s, d_s, dk_s, dv_s, out_s,
-     Ha, La, Hm, Lm, za, zm, vr, w0_s, l_sem, s_sem, r_sem) = rest
+    (O_out, O_in, sum_a, sum_m, vec, g_s, gm_s, acc, gT, fT, x_s, W_s, qkv_s, att_s, lse_s, ga_s, d_s, dk_s, dv_s, out_s,
+     Ha, La, Hm, Lm, za, zm, vr, w0_s, w1_s, l_sem, s_sem, r_sem) = rest
     cw = heads * HD
     D = g_s.shape[1]
     wires = Wires(s_sem, r_sem)
@@ -423,13 +457,14 @@
     load("h2", h2, Hm.at[0])
     load("h3", h3, Hm.at[1])
     load("w0", whole0, w0_s)
+    load("w1", h1, w1_s)
     for i, k in enumerate(order):
         b = i % 2
         load(f"W{i}", Ws[k], W_s.at[b])
         load(f"qkv{i}", qkvs[k], qkv_s.at[b])
         load(f"att{i}", atts[k], att_s.at[b])
         load(f"lse{i}", lses[k], lse_s.at[b])
-    for key in ("midway", "sec", "gout", "h2", "h3", "w0", "firstT", "W0", "qkv0", "att0", "lse0", "x"):
+    for key in ("midway", "sec", "gout", "h2", "h3", "w1", "w0", "firstT", "W0", "qkv0", "att0", "lse0", "x"):
         loads[key].start()
     slot = jnp.where(z == 0, 0, jnp.where(z == 3, 1, 2))
     own_place = pl.ds(pl.multiple_of(slot * TOK, 256), TOK)
@@ -440,31 +475,33 @@
     own_out, own_in = wires.local(mine.at[pl.ds(out_base, out_rows), :], O_out.at[out_place, :], used), wires.local(g_s, O_in.at[own_place, :], used)
     share_out = Sharing(wires, mine, O_out, OUT_CHUNKS, out_base)
     share_in = Sharing(wires, g_s, O_in, IN_CHUNKS)
-    sums = {"m2": Summing(wires, Hm.at[0], Lm.at[0], zm.at[0], 2), "m3": Summing(wires, Hm.at[1], Lm.at[1], zm.at[1], 3)}
+    sums = {"m2": Summing(wires, Hm.at[0], Lm.at[0]), "m3": Summing(wires, Hm.at[1], Lm.at[1])}
     for k in range(4):
-        sums[f"b{k}"] = Summing(wires, Ha.at[k], La.at[k], za.at[max(k - 1, 0)], k)
+        sums[f"b{k}"] = Summing(wires, Ha.at[k], La.at[k])
+    r = sum_a.shape[0]
+    top = pl.ds(0, r)
+    line_m = LineSum(wires, [None, w1_s, Hm.at[0, top, :], Hm.at[1, top, :]], zm)
+    line_b = LineSum(wires, [Ha.at[k, top, :] for k in range(4)], za)
     exchange = {k: wires.swap(out_s, Ha.at[k], dp=1) for k in range(4)}
     spread = [wires.swap(vec, vr.at[i], dp=dp, z=t) for i, (dp, t) in enumerate(((1, 0), (2, 0), (4, 0), (0, 1), (0, 2)))]
     greet(d, z, MASKS)
 
     todo = {
         -3: [lambda: share_out.start(0, 0), own_out[0]],
-        -2: [lambda: loads["h2"].wait(), sums["m2"].step1],
+        -2: [lambda: loads["h2"].wait(), sums["m2"].step1, lambda: loads["w1"].wait(), lambda: line_m.alpha(1)],
         0: [lambda: loads["h3"].wait(), lambda: loads["w0"].wait()],
-        2: [lambda: share_out.on(0, 1), lambda: share_out.start(1, 0)],
-        3: [sums["m2"].step2, sums["m3"].step1],
-        5: [sums["m2"].step3],
-        8: [sums["b3"].step1, lambda: share_out.on(0, 2), lambda: share_out.on(1, 1)],
-        12: [sums["m3"].step2],
-        13: [sums["b3"].step2],
-        15: [sums["m3"].step3, sums["b3"].step3],
-        18: [sums["b2"].step1, lambda: share_out.on(1, 2)],
-        23: [sums["b2"].step2],
-        25: [sums["b2"].step3],
-        28: [sums["b1"].step1],
-        33: [sums["b1"].step2],
-        35: [sums["b1"].step3],
-        38: [sums["b0"].step1],
+        5: [sums["m2"].step2, sums["m3"].step1],
+        8: [lambda: share_out.on(0, 1), lambda: share_out.start(1, 0)],
+        10: [sums["m2"].step3, lambda: line_m.alpha(2)],
+        15: [sums["m3"].step2],
+        18: [lambda: share_out.on(0, 2), lambda: share_out.on(1, 1), sums["b3"].step2],
+        20: [sums["m3"].step3, lambda: line_m.alpha(3)],
+        22: [sums["b3"].step3, lambda: line_b.alpha(3)],
+        25: [line_m.beta],
+        28: [lambda: share_out.on(1, 2), sums["b2"].step2],
+        33: [sums["b2"].step3, lambda: line_b.alpha(2)],
+        35: [sums["b1"].step2],
+        38: [sums["b1"].step3, lambda: line_b.alpha(1), line_m.gamma],
     }
 
     def tick(t):
@@ -503,26 +540,43 @@
         g_s[rows, :] = gm.astype(BF)
         gT[:, rows] = gm.T.astype(BF)
 
+    def write(dst, lo, hi, add):
+        def put(where, val):
+            if add:
+                val = val + dst[where, lo:hi].astype(F32)
+            dst[where, lo:hi] = val.astype(BF)
+        return put
+
+    def keep(i):
+        k, b = order[i], i % 2
+        exchange[k][1]()
+        block_rows(fT, d_s.at[b], 1, write(Ha.at[k], 0, 3 * cw, True))
+        block_rows(gT, att_s.at[b], 1, write(Ha.at[k], 3 * cw, 4 * cw, True))
+
     loads["firstT"].wait()
     acc[...] = jnp.zeros_like(acc)
     for i, k in enumerate(order):
         base, b = 10 * i, i % 2
-        W, qkv, att, lse, H = W_s.at[b], qkv_s.at[b], att_s.at[b], lse_s.at[b], Ha.at[k]
+        W, qkv, att, lse, dd_s = W_s.at[b], qkv_s.at[b], att_s.at[b], lse_s.at[b], d_s.at[b]
         for key in ("W", "qkv", "att", "lse"):
             loads[f"{key}{i}"].wait()
         if i < 3:
-            for key in ("W", "qkv", "att", "lse"):
+            for key in ("W", "qkv", "lse"):
                 loads[f"{key}{i + 1}"].start()
         tick(base)
-        Wo[...] = W[:, 3 * cw:]
 
         @pl.loop(0, TOK // RT)
         def _(t):
             rows = pl.ds(pl.multiple_of(t * RT, RT), RT)
-            g = nn(g_s[rows, :], Wo[...]).astype(BF)
+            g = nt(g_s[rows, :], W[3 * cw:, :]).astype(BF)
             for h in range(heads):
                 ga_s[h, rows, :] = g[:, h * HD:(h + 1) * HD]
 
+        if i:
+            keep(i - 1)
+            sums[f"b{order[i - 1]}"].step1()
+        if i < 3:
+            loads[f"att{i + 1}"].start()
         tick(base + 1)
         dk_s[...] = jnp.zeros_like(dk_s)
         dv_s[...] = jnp.zeros_like(dv_s)
@@ -548,24 +602,17 @@
                 dv_s[h] += tn(p.astype(BF), g)
             dq = jnp.concatenate(dqs, axis=1)
             put_row(place, 0, jnp.sum(dq, axis=0, keepdims=True))
-            d_s[rows, :cw] = dq.astype(BF)
-
-        d_s[:, cw:2 * cw] = jnp.concatenate([dk_s[h] * SC for h in range(heads)], axis=1).astype(BF)
+            dd_s[rows, :cw] = dq.astype(BF)
+
+        dd_s[:, cw:2 * cw] = jnp.concatenate([dk_s[h] * SC for h in range(heads)], axis=1).astype(BF)
         dv = jnp.concatenate([dv_s[h] for h in range(heads)], axis=1)
         put_row(place, 384, jnp.sum(dv, axis=0, keepdims=True))
-        d_s[:, 2 * cw:] = dv.astype(BF)
+        dd_s[:, 2 * cw:] = dv.astype(BF)
         put_row(place, 768, geb[k])
         put_row(place, 1920, tops[k])
         tick(base + 5)
 
-        def write(dst, lo, hi, add):
-            def put(where, val):
-                if add:
-                    val = val + dst[where, lo:hi].astype(F32)
-                dst[where, lo:hi] = val.astype(BF)
-            return put
-
-        block_rows(fT, d_s, 0, write(out_s, 0, 3 * cw, False))
+        block_rows(fT, dd_s, 0, write(out_s, 0, 3 * cw, False))
         block_rows(gT, att, 0, write(out_s, 3 * cw, 4 * cw, False))
         exchange[k][0]()
         tick(base + 6)
@@ -573,12 +620,9 @@
         @pl.loop(0, TOK // RT)
         def _(t):
             rows = pl.ds(pl.multiple_of(t * RT, RT), RT)
-            acc[rows, :] += nt(d_s[rows, :], W[:, :3 * cw])
+            acc[rows, :] += nn(dd_s[rows, :], W[:3 * cw, :])
 
         tick(base + 7)
-        exchange[k][1]()
-        block_rows(fT, d_s, 1, write(H, 0, 3 * cw, True))
-        block_rows(gT, att, 1, write(H, 3 * cw, 4 * cw, True))
         tick(base + 8)
 
     loads["x"].wait()
@@ -601,7 +645,10 @@
                 share_in.start(2 * t + 1, 0)
 
     own_in[0]()
-    after = {0: [spread[0][0], sums["b0"].step2], 1: [], 2: [sums["b0"].step3]}
+    spread[0][0]()
+    keep(3)
+    sums["b0"].step1()
+    after = {0: [line_b.beta], 1: [sums["b0"].step2], 2: [sums["b0"].step3], 3: [line_b.gamma]}
     row = lax.broadcasted_iota(jnp.int32, vec.shape, 1)
 
     def fold(i):
@@ -625,18 +672,15 @@
         share_out.wait(c, 2)
     own_out[1]()
     own_in[1]()
-    for s in ("m2", "m3", "b3", "b2", "b1"):
-        sums[s].step4()
-    r = sum_a.shape[0]
-    sum_a[...] = Ha[0, :r, :].astype(F32) + za[0].astype(F32) + za[1].astype(F32) + za[2].astype(F32)
-    sum_m[...] = w0_s[...] + zm[0].astype(F32) + zm[1].astype(F32)
+    sum_m[...] = line_m.total(w0_s[...].astype(F32))
+    sum_a[...] = line_b.total(Ha[0, :r, :].astype(F32))
     for c in range(n):
         share_in.wait(c, 2)
 
 
-def back(number, gain1, gain2, live, geb, tops, gout, midway, sec, firstT, x, mine, whole0, h2, h3, qkvs, atts, lses, Ws, length):
+def back(number, gain1, gain2, live, geb, tops, gout, midway, sec, firstT, x, mine, whole0, h1, h2, h3, qkvs, atts, lses, Ws, length):
     D = gout.shape[1]
-    cw = Ws[0].shape[1] // 4
+    cw = Ws[0].shape[0] // 4
     cm = h2.shape[1]
     heads = cw // HD
     r = D // 8
@@ -645,18 +689,18 @@
     return pl.pallas_call(
         functools.partial(back_kernel, length, heads),
         out_shape=(shape((3 * (TOK - OUT_CHUNKS[0][0]), D), BF), shape((3 * TOK, D), BF), shape((r, 4 * cw), F32), shape((r, cm), F32), shape((16, 2048), F32)),
-        in_specs=[VM] * 5 + [HB] * 25,
+        in_specs=[VM] * 5 + [HB] * 26,
         out_specs=(HB, HB, VM, VM, VM),
         scratch_shapes=[vm((TOK, D), BF), vm((TOK, D), F32), vm((TOK, D), F32), vm((D, TOK), BF), vm((D, TOK), BF), vm((TOK, D), BF),
-                        vm((2, D, 4 * cw), BF), vm((D, cw), BF), vm((2, 3 * heads, TOK, HD), BF), vm((2, TOK, cw), BF), vm((2, TOK, 128), F32),
-                        vm((heads, TOK, HD), BF), vm((TOK, 3 * cw), BF), vm((heads, TOK, HD), F32), vm((heads, TOK, HD), F32), vm((4 * r, 4 * cw), BF),
+                        vm((2, 4 * cw, D), BF), vm((2, 3 * heads, TOK, HD), BF), vm((2, TOK, cw), BF), vm((2, TOK, 128), F32),
+                        vm((heads, TOK, HD), BF), vm((2, TOK, 3 * cw), BF), vm((heads, TOK, HD), F32), vm((heads, TOK, HD), F32), vm((4 * r, 4 * cw), BF),
                         vm((4, 4 * r, 4 * cw), BF), vm((4, 3 * r, 4 * cw), BF), vm((2, 4 * r, cm), BF), vm((2, 3 * r, cm), BF),
-                        vm((3, r, 4 * cw), BF), vm((2, r, cm), BF), vm((5, 16, 2048), F32), vm((r, cm), F32),
+                        vm((5, r, 4 * cw), BF), vm((5, r, cm), BF), vm((5, 16, 2048), F32), vm((r, cm), BF), vm((r, cm), BF),
                         dma((32,)), dma((COPIES,)), dma((COPIES,))],
         compiler_params=pltpu.CompilerParams(vmem_limit_bytes=63 * 2**20, collective_id=number, has_side_effects=True),
         cost_estimate=pl.CostEstimate(flops=4 * 2 * TOK * (D * cw * 8 + heads * 5 * TOK * HD * 6), bytes_accessed=60 * 2**20, transcendentals=4 * heads * TOK * TOK),
         name="back",
-    )(gain1, gain2, live, geb, tops, gout, midway, sec, firstT, x, mine, whole0, h2, h3, *Ws, *qkvs, *atts, *lses)
+    )(gain1, gain2, live, geb, tops, gout, midway, sec, firstT, x, mine, whole0, h1, h2, h3, *Ws, *qkvs, *atts, *lses)
 
 
 class Spreading:
@@ -676,19 +720,26 @@
         for s, _ in self.s0:
             s()
 
+    def landed(self):
+        for _, w in self.s0 + [self.own]:
+            w()
+
+    def go_on(self):
+        for s, _ in self.s1 + self.s1c:
+            s()
+
     def step1(self):
         for _, w in self.s0:
             w()
-        for s, _ in self.s1 + self.s1c:
-            s()
+        self.go_on()
 
     def step2(self):
         for _, w in self.s1:
             w()
         self.s2[0]()
 
-    def finish(self):
-        for _, w in self.s1c + [self.own, self.s2]:
+    def finish(self, own=True):
+        for _, w in self.s1c + [self.s2] + [self.own] * own:
             w()
 
 
@@ -708,25 +759,22 @@
             self.made[k].wait()
 
 
-def front_kernel(length, heads, gain1, shift1, gain2, shift2, out_b, bias_own, x, qw, kw, vw, ow, ew, st, te, *rest):
-    (qkv0, qkv1, qkv2, qkv3, att0, att1, att2, att3, lse0, lse1, lse2, lse3, firstT, second, secondT, midway, Wa0, Wa1, Wa2, Wa3, Wm0, Wm1, Zm2,
-     tops, bias_all, x_s, raw, ow_s, first_s, T_s, second_s, acc, W, Wm, Za, Zm1, qkv_s, att_s, lse_s, bias, l_sem, s_sem, r_sem) = rest
+def front_kernel(length, heads, gain1, shift1, gain2, shift2, out_b, bias_own, x, qw, kw, vw, ow, mw, *rest):
+    (qkv0, qkv1, qkv2, qkv3, att0, att1, att2, att3, lse0, lse1, lse2, lse3, firstT, second, secondT, midway, Wa0, Wa1, Wa2, Wa3, Wm1, Zm2,
+     tops, bias_all, x_s, first_s, T_s, second_s, acc, W, Za, Zm1, qkv_s, att_s, lse_s, bias, l_sem, s_sem, r_sem) = rest
     cw = heads * HD
     D = x_s.shape[1]
-    cut = (Wm.shape[1] - 128) // 2
     wires, moves = Wires(s_sem, r_sem), Moves(l_sem)
     d, z = wires.d, wires.z
-    rows = D // 8
-    own_rows = pl.ds(pl.multiple_of(d * rows, 16), rows)
-    for i, ref in enumerate((qw, kw, vw)):
-        moves.add(f"w{i}", ref, raw.at[i])
-    moves.add("ow", ow, ow_s.at[pl.ds(0, cw), :])
+
+    def own_rows(ref):
+        n = ref.shape[0] // 8
+        return pl.ds(pl.multiple_of(d * n, 16), n)
+
+    for i, ref in enumerate((qw, kw, vw, ow)):
+        moves.add(f"w{i}", ref, W.at[0, pl.ds(i * cw, cw), :])
     moves.add("x", x, x_s)
-    moves.add("m0", ew.at[:, pl.ds(0, cut)], Wm.at[:, pl.ds(0, cut)])
-    moves.add("m1", st.at[:, pl.ds(0, cut)], Wm.at[:, pl.ds(cut, cut)])
-    moves.add("m2", te, Wm.at[:, pl.ds(2 * cut, 128)])
     moves.add("oW0", W.at[0], Wa0)
-    moves.add("oWm", Wm, Wm0)
     for k, (a, b, c) in enumerate(((qkv0, att0, lse0), (qkv1, att1, lse1), (qkv2, att2, lse2), (qkv3, att3, lse3))):
         moves.add(f"qkv{k}", qkv_s.at[k], a)
         moves.add(f"att{k}", att_s.at[k], b)
@@ -737,30 +785,22 @@
     moves.add("second", second_s, second)
     moves.add("secondT", T_s, secondT)
     moves.add("midway", acc, midway)
-    moves.start("w0", "w1", "w2", "ow", "x", "m0", "m1", "m2")
+    moves.start("w0", "w1", "w2", "w3", "x")
 
     zb = [wires.swap(bias.at[0], bias.at[k], z=k) for k in (1, 2, 3)]
-    za = [wires.swap(W.at[0, own_rows, :], Za.at[0], z=1), wires.swap(W.at[0, own_rows, :], Za.at[1], z=2), wires.swap(Za.at[1], Za.at[2], z=1)]
-    zm = [wires.swap(Wm.at[own_rows, :], Zm1, z=1), wires.swap(Wm.at[own_rows, :], Zm2, z=2)]
+    a_piece, m_piece = W.at[0, own_rows(W.at[0]), :], mw.at[own_rows(mw), :]
+    za = [wires.swap(a_piece, Za.at[0], z=1), wires.swap(a_piece, Za.at[1], z=2), wires.swap(Za.at[1], Za.at[2], z=1)]
+    zm = [wires.swap(m_piece, Zm1, z=1), wires.swap(m_piece, Zm2, z=2)]
     ga = {k: Spreading(wires, Za.at[k - 1], W.at[k]) for k in (1, 2, 3)}
     gm = Spreading(wires, Zm1, Wm1)
     greet(d, z, MASKS)
     bias[0] = bias_own[...]
     for s, _ in zb:
         s()
-    moves.wait("w0", "w1", "w2", "ow")
-
-    @pl.loop(0, D // 384)
-    def _(i):
-        part = pl.ds(pl.multiple_of(i * 384, 128), 384)
-        turned = ow_s[:, part].astype(F32).T[:, :cw].astype(BF)
-        W[0, part, :] = jnp.concatenate([raw[0, part, :], raw[1, part, :], raw[2, part, :], turned], axis=1)
-
+    moves.wait("w0", "w1", "w2", "w3")
     za[0][0]()
     za[1][0]()
     moves.start("oW0")
-    moves.wait("m0", "m1", "m2")
-    moves.start("oWm")
     moves.wait("x")
 
     @pl.loop(0, TOK // RT)
@@ -783,19 +823,15 @@
         za[2][0]()
 
     todo = {
-        0: [za[0][1], ga[1].step0, zm[0][0]],
-        2: [],
-        3: [ga[1].step1],
-        4: [z_a3, ga[2].step0, ga[1].step2],
-        10: [],
-        11: [ga[2].step1, zm[1][0]],
-        12: [za[2][1], ga[3].step0],
-        13: [ga[2].step2],
-        20: [zm[0][1], gm.step0],
-        21: [ga[3].step1],
+        0: [zm[0][0]],
+        1: [za[0][1], ga[1].step0],
+        5: [z_a3, ga[2].step0, ga[1].step1, ga[1].step2],
+        10: [za[2][1], ga[3].step0],
+        11: [zm[1][0]],
+        13: [ga[2].step1],
+        15: [ga[2].step2],
+        20: [ga[3].step1, zm[0][1], gm.step0],
         23: [ga[3].step2],
-        31: [gm.step1],
-        34: [gm.step2],
     }
 
     def tick(t):
@@ -814,7 +850,7 @@
         @pl.loop(0, TOK // RT)
         def _(i):
             part = pl.ds(pl.multiple_of(i * RT, RT), RT)
-            t = nn(first_s[part, :], Wk[:, :3 * cw])
+            t = nt(first_s[part, :], Wk[:3 * cw, :])
             q = (t[:, :cw] + qb).astype(BF)
             kk = t[:, cw:2 * cw].astype(BF)
             v = (t[:, 2 * cw:] + vb).astype(BF)
@@ -847,9 +883,10 @@
                 tops[k, h:h + 1, :] = jnp.maximum(tops[k, h:h + 1, :], jnp.max(jnp.where(rid < length, m, -1e30)) * SC)
             a = jnp.concatenate(res, axis=1)
             att[part, :] = a
-            acc[part, :] += nt(a, Wk[:, 3 * cw:])
+            acc[part, :] += nn(a, Wk[3 * cw:, :])
 
         moves.start(f"att{k}", f"lse{k}")
+        tick(base + 5)
 
     moves.start("midway")
     moves.wait("firstT")
@@ -863,57 +900,55 @@
         T_s[:, part] = f.T.astype(BF)
 
     moves.start("second", "secondT")
-    gm.finish()
+    gm.landed()
     zm[1][1]()
     for k in range(4):
         moves.wait(f"qkv{k}", f"att{k}", f"lse{k}", f"oW{k}")
-    moves.wait("oWm", "second", "secondT", "midway")
-
-
-def front(number, gain1, shift1, gain2, shift2, out_b, bias_own, x, qw, kw, vw, ow, ew, st, te, length):
-    D, cw = qw.shape
+    moves.wait("second", "secondT", "midway")
+
+
+def front(number, gain1, shift1, gain2, shift2, out_b, bias_own, x, qw, kw, vw, ow, mw, length):
+    cw, D = qw.shape
     heads = cw // HD
-    cut = ew.shape[1] // 128 * 128
-    cm = 2 * cut + 128
-    r = D // 8
+    cm = mw.shape[0]
     vm = pltpu.VMEM
     dma = pltpu.SemaphoreType.DMA
     four = lambda s: (s,) * 4
     got = pl.pallas_call(
         functools.partial(front_kernel, length, heads),
         out_shape=(*four(shape((3 * heads, TOK, HD), BF)), *four(shape((TOK, cw), BF)), *four(shape((TOK, 128), F32)),
-                   shape((D, TOK), BF), shape((TOK, D), BF), shape((D, TOK), BF), shape((TOK, D), F32), *four(shape((D, 4 * cw), BF)),
-                   shape((D, cm), BF), shape((D, cm), BF), shape((r, cm), BF), shape((4, heads, 128), F32), shape((4, 8, 2048), F32)),
-        in_specs=[VM] * 6 + [HB] * 8,
-        out_specs=(HB,) * 23 + (VM,) * 2,
-        scratch_shapes=[vm((TOK, D), BF), vm((3, D, cw), BF), vm((384, D), BF), vm((TOK, D), BF), vm((D, TOK), BF), vm((TOK, D), BF), vm((TOK, D), F32),
-                        vm((4, D, 4 * cw), BF), vm((D, cm), BF), vm((3, r, 4 * cw), BF), vm((r, cm), BF), vm((4, 3 * heads, TOK, HD), BF),
+                   shape((D, TOK), BF), shape((TOK, D), BF), shape((D, TOK), BF), shape((TOK, D), F32), *four(shape((4 * cw, D), BF)),
+                   shape((cm, D), BF), shape((cm // 8, D), BF), shape((4, heads, 128), F32), shape((4, 8, 2048), F32)),
+        in_specs=[VM] * 6 + [HB] * 6,
+        out_specs=(HB,) * 22 + (VM,) * 2,
+        scratch_shapes=[vm((TOK, D), BF), vm((TOK, D), BF), vm((D, TOK), BF), vm((TOK, D), BF), vm((TOK, D), F32),
+                        vm((4, 4 * cw, D), BF), vm((3, cw // 2, D), BF), vm((cm // 8, D), BF), vm((4, 3 * heads, TOK, HD), BF),
                         vm((4, TOK, cw), BF), vm((4, TOK, 128), F32), vm((4, 8, 2048), F32), dma((32,)), dma((64,)), dma((64,))],
         compiler_params=pltpu.CompilerParams(vmem_limit_bytes=62 * 2**20, collective_id=number, has_side_effects=True),
         cost_estimate=pl.CostEstimate(flops=4 * 2 * TOK * (D * cw * 4 + heads * 2 * TOK * HD * 6), bytes_accessed=60 * 2**20, transcendentals=4 * heads * TOK * TOK),
         name="front",
-    )(gain1, shift1, gain2, shift2, out_b, bias_own, x, qw, kw, vw, ow, ew, st, te)
-    return got[:4], got[4:8], got[8:12], got[12:16], got[16:20], got[20:23], got[23], got[24]
+    )(gain1, shift1, gain2, shift2, out_b, bias_own, x, qw, kw, vw, ow, mw)
+    return got[:4], got[4:8], got[8:12], got[12:16], got[16:20], got[20:22], got[22], got[23]
 
 
 def middle_kernel(fw, live, shrink_b, bias_all, second, secondT, gout, goutT, midway, Wm0, Wm1, Zm2, *rest):
-    (mine, sec, O0, H2, H3, geb, part_sum, Wg2, Wg3, Zm3, second_s, secondT_s, gout_s, goutT_s, mlp, sec_s, mine_s, tail_s, E, ST, act_s, slope_s, gpre_s, out_s,
-     Hm, Lm, zr, l_sem, s_sem, r_sem) = rest
+    (mine, sec, O0, H1, H2, H3, geb, part_sum, Wg2, Wg3, Zm3, Wg1, second_s, secondT_s, gout_s, goutT_s, mlp, sec_s, mine_s, W, act_s, slope_s, gpre_s, out_s,
+     Hm, Lm, l_sem, s_sem, r_sem) = rest
     D = second_s.shape[1]
+    hid = W.shape[1] // 2
     cut = fw // 128 * 128
     tail = fw - cut
     r = D // 8
     wires, moves = Wires(s_sem, r_sem), Moves(l_sem)
     d, z = wires.d, wires.z
-    Ws = (Wm0, Wm1, Wg2, Wg3)
+    Ws = (Wm0, Wg1, Wg2, Wg3)
     for key, a, b in (("second", second, second_s), ("secondT", secondT, secondT_s), ("gout", gout, gout_s), ("goutT", goutT, goutT_s), ("midway", midway, mlp)):
         moves.add(key, a, b)
     for k in range(4):
-        moves.add(f"E{k}", Ws[k].at[:, pl.ds(0, cut)], E.at[k % 2, :, pl.ds(0, cut)])
-        moves.add(f"S{k}", Ws[k].at[:, pl.ds(cut, cut)], ST.at[k % 2, :, pl.ds(0, cut)])
-        moves.add(f"T{k}", Ws[k].at[:, pl.ds(2 * cut, 128)], tail_s.at[k % 2])
+        moves.add(f"W{k}", Ws[k], W.at[k % 2])
     moves.add("mine", mine_s, mine)
     moves.add("sec", sec_s, sec)
+    moves.add("h1", Hm.at[1, pl.ds(0, r), :], H1)
     moves.add("h2", Hm.at[2], H2)
     moves.add("h3", Hm.at[3], H3)
     slot = jnp.where(z == 0, 0, jnp.where(z == 3, 1, 2))
@@ -922,35 +957,30 @@
     own_out = wires.local(mine_s.at[pl.ds(0, n0), :], O0.at[pl.ds(pl.multiple_of(slot * n0, 256), n0), :], used)
     share = Sharing(wires, mine_s, O0, ((0, n0),))
     z3 = wires.swap(Zm2, Zm3, z=1)
-    g2, g3 = Spreading(wires, Zm2, Wg2), Spreading(wires, Zm3, Wg3)
-    exchange = [wires.swap(out_s, Hm.at[k], dp=1) for k in range(4)]
-    sums = [Summing(wires, Hm.at[k], Lm.at[k], zr, k) for k in (0, 1)]
-    moves.start("second", "E0", "S0", "T0", "midway", "gout", "goutT", "secondT")
+    g1, g2, g3 = Spreading(wires, Zm2, Wg1), Spreading(wires, Zm2, Wg2), Spreading(wires, Zm3, Wg3)
+    exchange = [wires.swap(out_s.at[k % 2], Hm.at[k], dp=1) for k in range(4)]
+    sums = [Summing(wires, Hm.at[k], Lm.at[k]) for k in (0, 1)]
+    moves.start("second", "W0", "midway", "gout", "goutT", "secondT")
     greet(d, z, MASKS)
+    g1.go_on()
     z3[0]()
-    g2.step0()
     sec_s[...] = jnp.zeros_like(sec_s)
     geb[...] = jnp.zeros_like(geb)
     moves.wait("second", "midway")
 
     def forward(k, tick):
         b = k % 2
-        moves.wait(f"E{k}", f"S{k}", f"T{k}")
-        lane = lax.broadcasted_iota(jnp.int32, (D, 128), 1)
-        last = tail_s[b]
-        E[b, :, cut:] = jnp.where(lane < tail, last, jnp.zeros_like(last))
-        moved = jnp.concatenate([last[:, tail:2 * tail], jnp.zeros((D, 128 - tail), BF)], axis=1)
-        ST[b, :, cut:] = moved
-        eb = bias_all[k, 0:1, 768:768 + cut + 128]
+        moves.wait(f"W{k}")
+        eb = bias_all[k, 0:1, 768:768 + hid]
 
         @pl.loop(0, TOK // RT)
         def _(i):
             tick(i)
             rows = pl.ds(pl.multiple_of(i * RT, RT), RT)
-            act, slope = gelu_parts(nn(second_s[rows, :], E[b]) + eb)
+            act, slope = gelu_parts(nt(second_s[rows, :], W[b, :hid, :]) + eb)
             act_s[b, rows, :] = act.astype(BF)
             slope_s[b, rows, :] = slope.astype(BF)
-            mlp[rows, :] += nt(act_s[b, rows, :], ST[b])
+            mlp[rows, :] += nn(act_s[b, rows, :], W[b, hid:, :])
 
     def grads(k, half):
         b = k % 2
@@ -958,25 +988,25 @@
             q = 4 * t + 1 - half
             lhs = lambda ref: jnp.concatenate([ref[pl.ds(pl.multiple_of((d ^ p) * r, 16), r), :] for p in (q, q + 2)], axis=0)
             place = pl.ds(t * 2 * r, 2 * r)
-            ve, vs = nn(lhs(secondT_s), gpre_s[...]), nn(lhs(goutT_s), act_s[b])
+            ve, vs = nn(lhs(secondT_s), gpre_s[b]), nn(lhs(goutT_s), act_s[b])
             last = jnp.concatenate([ve[:, cut:fw], vs[:, cut:fw], jnp.zeros((2 * r, 128 - 2 * tail), F32)], axis=1)
-            to = out_s if half == 0 else Hm.at[k]
+            to = out_s.at[b] if half == 0 else Hm.at[k]
             for lo, v in ((0, ve[:, :cut]), (cut, vs[:, :cut]), (2 * cut, last)):
                 n = v.shape[1]
                 if half:
                     v = v + to[place, lo:lo + n].astype(F32)
                 to[place, lo:lo + n] = v.astype(BF)
 
-    def backward(k, tick):
+    def back_a(k, tick):
         b = k % 2
 
         @pl.loop(0, TOK // RT)
         def _(i):
             tick(i)
             rows = pl.ds(pl.multiple_of(i * RT, RT), RT)
-            gp = nn(gout_s[rows, :], ST[b]) * slope_s[b, rows, :].astype(F32)
+            gp = nt(gout_s[rows, :], W[b, hid:, :]) * slope_s[b, rows, :].astype(F32)
             geb[k] += jnp.sum(gp, axis=0, keepdims=True)
-            gpre_s[rows, :] = gp.astype(BF)
+            gpre_s[b, rows, :] = gp.astype(BF)
 
         grads(k, 0)
         exchange[k][0]()
@@ -985,8 +1015,9 @@
         def _(i):
             tick(i + 3)
             rows = pl.ds(pl.multiple_of(i * RT, RT), RT)
-            sec_s[rows, :] += nt(gpre_s[rows, :], E[b])
-
+            sec_s[rows, :] += nn(gpre_s[b, rows, :], W[b, :hid, :])
+
+    def back_b(k):
         exchange[k][1]()
         grads(k, 1)
 
@@ -1000,20 +1031,22 @@
         return tick
 
     none = ticks({})
-    moves.start("E1", "S1", "T1")
-    forward(0, none)
+    forward(0, ticks({2: [g2.step0]}))
     moves.wait("gout", "goutT", "secondT")
-    backward(0, ticks({0: [g2.step1], 2: [z3[1], g3.step0], 3: [g2.step2]}))
+    back_a(0, ticks({2: [g1.step2]}))
+    g1.finish(False)
+    moves.start("W1")
+    forward(1, ticks({1: [g2.step1], 2: [z3[1], g3.step0]}))
+    back_b(0)
+    back_a(1, ticks({1: [g2.step2], 4: [g3.step1]}))
     g2.finish()
-    moves.start("E2", "S2", "T2")
+    moves.start("W2")
+    forward(2, ticks({2: [g3.step2]}))
+    back_b(1)
+    g3.finish()
+    moves.start("W3")
     sums[0].step1()
-    forward(1, ticks({2: [g3.step1]}))
-    backward(1, ticks({0: [g3.step2], 2: [sums[0].step2], 4: [sums[0].step3]}))
-    g3.finish()
-    moves.start("E3", "S3", "T3")
-    sums[1].step1()
-    forward(2, none)
-    forward(3, ticks({1: [sums[1].step2]}))
+    forward(3, none)
 
     @pl.loop(0, TOK // RT)
     def _(i):
@@ -1023,40 +1056,46 @@
 
     own_out[0]()
     moves.start("mine")
-    backward(2, ticks({0: [sums[1].step3], 4: [lambda: share.on(0, 1)]}))
+    sums[1].step1()
+    back_a(2, ticks({4: [lambda: share.on(0, 1), sums[0].step2]}))
+    back_a(3, ticks({4: [sums[0].step3, lambda: share.on(0, 2)]}))
+    sums[1].step2()
+    moves.start("sec")
+    back_b(2)
     moves.start("h2")
-    backward(3, ticks({2: [lambda: share.on(0, 2)]}))
-    moves.start("h3", "sec")
-    sums[1].step4()
-    part_sum[...] = Hm[0, :r, :].astype(F32) + zr[...].astype(F32)
+    back_b(3)
+    moves.start("h3")
+    sums[1].step3()
+    moves.start("h1")
+    part_sum[...] = Hm[0, :r, :]
     share.wait(0, 2)
     own_out[1]()
-    moves.wait("h2", "h3", "sec", "mine")
+    moves.wait("h1", "h2", "h3", "sec", "mine")
 
 
 def middle(number, fw, live, shrink_b, bias_all, second, secondT, gout, goutT, midway, Wm0, Wm1, Zm2):
     D = second.shape[1]
-    cut = fw // 128 * 128
-    wide = cut + 128
-    cm = 2 * cut + 128
+    cm, hid = Wm0.shape[0], Wm0.shape[0] // 2
+    cg = fw // 128 * 256 + 128
     r = D // 8
     n0 = OUT_CHUNKS[0][0]
     vm = pltpu.VMEM
     dma = pltpu.SemaphoreType.DMA
     got = pl.pallas_call(
         functools.partial(middle_kernel, fw),
-        out_shape=(shape((TOK, D), BF), shape((TOK, D), F32), shape((3 * n0, D), BF), shape((4 * r, cm), BF), shape((4 * r, cm), BF), shape((4, 1, wide), F32), shape((r, cm), F32),
-                   shape((D, cm), BF), shape((D, cm), BF), shape((r, cm), BF)),
+        out_shape=(shape((TOK, D), BF), shape((TOK, D), F32), shape((3 * n0, D), BF), shape((r, cg), BF), shape((4 * r, cg), BF), shape((4 * r, cg), BF), shape((4, 1, hid), F32), shape((r, cg), BF),
+                   shape((cm, D), BF), shape((cm, D), BF), shape((cm // 8, D), BF), shape((cm, D), BF)),
         in_specs=[VM] * 3 + [HB] * 8,
-        out_specs=(HB,) * 5 + (VM,) * 2 + (HB,) * 3,
-        scratch_shapes=[vm((TOK, D), BF), vm((D, TOK), BF), vm((TOK, D), BF), vm((D, TOK), BF), vm((TOK, D), F32), vm((TOK, D), F32), vm((TOK, D), BF), vm((2, D, 128), BF),
-                        vm((2, D, wide), BF), vm((2, D, wide), BF), vm((2, TOK, wide), BF), vm((2, TOK, wide), BF), vm((TOK, wide), BF), vm((4 * r, cm), BF),
-                        vm((4, 4 * r, cm), BF), vm((2, 3 * r, cm), BF), vm((r, cm), BF), dma((32,)), dma((72,)), dma((72,))],
+        out_specs=(HB,) * 6 + (VM,) * 2 + (HB,) * 4,
+        input_output_aliases={9: 11},
+        scratch_shapes=[vm((TOK, D), BF), vm((D, TOK), BF), vm((TOK, D), BF), vm((D, TOK), BF), vm((TOK, D), F32), vm((TOK, D), F32), vm((TOK, D), BF), vm((2, cm, D), BF),
+                        vm((2, TOK, hid), BF), vm((2, TOK, hid), BF), vm((2, TOK, hid), BF), vm((2, 4 * r, cg), BF),
+                        vm((4, 4 * r, cg), BF), vm((2, 3 * r, cg), BF), dma((32,)), dma((72,)), dma((72,))],
         compiler_params=pltpu.CompilerParams(vmem_limit_bytes=63 * 2**20, collective_id=number, has_side_effects=True),
         cost_estimate=pl.CostEstimate(flops=4 * 2 * 9 * TOK * D * fw, bytes_accessed=60 * 2**20, transcendentals=4 * TOK * fw),
         name="middle",
     )(live, shrink_b, bias_all, second, secondT, gout, goutT, midway, Wm0, Wm1, Zm2)
-    return got[:7]
+    return got[:8]
 
 
 class General:
@@ -1107,19 +1146,19 @@
     x_low = pad(lax.dynamic_index_in_dim(images, slot, 0, keepdims=False))
     gout = pad(lax.dynamic_index_in_dim(cotangent, slot, 0, keepdims=False)) * live.astype(BF)
     gout_t = gout.T
-    shrink_t = shrink_w.T
     if (groups, lax.axis_size("dp")) == (4, 8):
         one = lambda a: a[None]
         blank = lambda n: jnp.zeros((n,), F32)
         bias_own = jnp.concatenate([query_b, blank(384 - cw), value_b, blank(384 - cw), expand_b, blank(1280 - fw)])
-        tail_own = jnp.concatenate([expand_w[:, cut:], shrink_t[:, cut:], jnp.zeros((width, 128 - 2 * (fw - cut)), BF)], axis=1)
+        deep = -fw % 16
+        mlp_own = jnp.pad(jnp.stack([expand_w.T, shrink_w]), ((0, 0), (0, deep), (0, 0))).reshape(2 * (fw + deep), width)
         qkvs, atts, lses, (first_t, second, second_t, midway), attn_ws, mlp_ws, tops, bias_all = front(
             0, one(norm1_gain), one(norm1_shift), one(norm2_gain), one(norm2_shift), one(out_b), jnp.broadcast_to(bias_own, (8, 2048)),
-            x_low, query_w, key_w, value_w, out_w, expand_w, shrink_t, tail_own, length)
-        mine, sec, out_low, h2, h3, geb, part_sum = middle(1, fw, live[None, None], one(shrink_b), bias_all, second, second_t, gout, gout_t, midway, *mlp_ws)
+            x_low, query_w.T, key_w.T, value_w.T, out_w, mlp_own, length)
+        mine, sec, out_low, h1, h2, h3, geb, part_sum = middle(1, fw, live[None, None], one(shrink_b), bias_all, second, second_t, gout, gout_t, midway, mlp_own, *mlp_ws)
         out_high, in_all, sum_attn, sum_mlp, vec = back(
             2, one(norm1_gain), one(norm2_gain), live[None, None], geb, jnp.where(live > 0.0, tops[:, :, 0], -1e30)[:, None],
-            gout, midway, sec, first_t, x_low, mine, part_sum, h2, h3, qkvs, atts, lses, attn_ws, length)
+            gout, midway, sec, first_t, x_low, mine, part_sum, h1, h2, h3, qkvs, atts, lses, attn_ws, length)
         outputs = jnp.concatenate([out_low.reshape(3, -1, width), out_high.reshape(3, -1, width)], axis=1)[:, :length]
         input_grads = in_all.reshape(3, TOK, width)[:, :length].astype(F32)
         own = lax.dynamic_index_in_dim(vec, z, 0, keepdims=False)
@@ -1127,6 +1166,7 @@
         tail = [vec[4 + i, :width] for i in range(6)]
     else:
         attn_own = jnp.concatenate([query_w, key_w, value_w, out_w.T], axis=1)
+        shrink_t = shrink_w.T
         mlp_own = jnp.concatenate([expand_w[:, :cut], shrink_t[:, :cut], expand_w[:, cut:], shrink_t[:, cut:]], axis=1)
         net = General(groups, attn_own, mlp_own)
         biases = net.vectors(jnp.concatenate([query_b, value_b, expand_b]))

time: 538 us -> 455 us (0.85)
  Pallas kernels: 476 us -> 405 us
  local copies, waits for them, and re-layouts: 37.6 us -> 21 us
    pallas_call x1, Pallas kernels: 242 us -> 205 us  [back(): pl.pallas_call(functools.partial(back_kernel, length, heads), out_shape=(...]
    pallas_call x1, Pallas kernels: 138 us -> 112 us  [middle(): pl.pallas_call(functools.partial(middle_kernel, fw), out_shape=(shape((TO...]
    unnamed x19 -> x10, local copies, waits for them, and re-layouts: 15.6 us -> 0.02 us
    pallas_call x1, Pallas kernels: 96.9 us -> 87.6 us  [front(): pl.pallas_call(functools.partial(front_kernel, length, heads), out_shape=...]
where the time goes in v5:
time: 455 us; the launch traced here: 450 us
  Pallas kernels  405 us (89%)
  other arithmetic  21.9 us (5%)
  local copies, waits for them, and re-layouts  21 us (5%)
    pallas_call x1, Pallas kernels, back(): pl.pallas_call(functools.partial(back_kernel, length, heads), out_shape=(...  205 us
    pallas_call x1, Pallas kernels, middle(): pl.pallas_call(functools.partial(middle_kernel, fw), out_shape=(shape((TO...  112 us
    pallas_call x1, Pallas kernels, front(): pl.pallas_call(functools.partial(front_kernel, length, heads), out_shape=...  87.6 us

profile of v5, /device:TPU:1, one launch (start us, length us, event | category | flops | bytes accessed | tf_op | source)
XLA Modules:
  0.0 449.9 jit_solution(15499490228990234112)
XLA Ops:
  1.3 1.3 broadcast_in_dim.40.gain1
  2.6 1.3 broadcast_in_dim.42.gain2
  3.9 1.3 broadcast_in_dim.44.out_b
  5.2 1.3 broadcast_in_dim.41.shift1
  6.5 1.3 broadcast_in_dim.43.shift2
  7.8 1.3 broadcast_in_dim.39.shrink_b
  9.1 0.8 concatenate.12
  9.9 0.6 broadcast_in_dim.46.bias_own
  10.5 2.2 dynamic-slice_bitcast_fusion
  12.8 1.3 pad.11.x
  14.1 1.6 fusion.4
  15.7 2.3 copy.40.goutT
  18.0 5.1 %fusion.2 = bf16[2,1088,1152]{2,1,0:T(8,128)(2,1)} fusion(bf16[1,1076,1152]{2,1,0:T(8,128)(2,1)} %bitcast.33, bf16[1,1076,1152]{2,1,0:T(8,128)(2,1)} %bitcast.34), kind=kLoop, calls=%fused_computation.5 | loop fusion | flops 17547264 | bytes 9971712 | tf_op jit(solution)/shard_map/stack | solution.py:1154
  23.1 87.6 %front.1 = (bf16[12,768,72]{2,1,0:T(8,128)(2,1)}, bf16[12,768,72]{2,1,0:T(8,128)(2,1)}, bf16[12,768,72]{2,1,0:T(8,128)(2,1)}, bf16[12,768,72]{2,1,0:T(8,128)(2,1...) custom-call(f32[1,1152]{1,0:T(1,128)} %broadcast_in_dim.40.gain1, ...), custom_call_target="tpu_custom_call" | custom-call | flops 24461180928 | bytes 62914560 | tf_op jit(solution)/shard_map/front/pallas_call | solution.py:917
  110.7 1.4 select_reduce_fusion
  112.0 112.4 %middle.1 = (bf16[768,1152]{1,0:T(8,128)(2,1)}, f32[768,1152]{1,0:T(8,128)}, bf16[768,1152]{1,0:T(8,128)(2,1)}, bf16[144,2176]{1,0:T(8,128)(2,1)}, bf16[576,2176...) custom-call(f32[1,1]{1,0:T(1,128)} %bitcast.1.live, ...), custom_call_target="tpu_custom_call", output_to_operand_aliasing={{11}: (9, {})} | custom-call | flops 68542267392 | bytes 62914560 | tf_op jit(solution)/shard_map/middle/pallas_call | solution.py:1084
  224.4 205.5 %back.1 = (bf16[1536,1152]{1,0:T(8,128)(2,1)}, bf16[2304,1152]{1,0:T(8,128)(2,1)}, f32[144,1152]{1,0:T(8,128)}, f32[144,2176]{1,0:T(8,128)}, f32[16,2048]{1,0:T(8,128)}) custom-call(f32[1,1152]{1,0:T(1,128)} %broadcast_in_dim.40.gain1, f32[1,1152]{1,0:T(1,128)} %broadcast_in_dim.42.gain2, f32[1,1]{1,0:T(1,128)} %bitcast.1.live, ...), custom_call_target="tpu_custom_call" | custom-call | flops 57076088832 | bytes 62914560 | tf_op jit(solution)/shard_map/back/pallas_call | solution.py:689
  429.9 0.8 sqrt_bitcast_fusion
  430.7 0.0 copy-start.1
  430.7 5.3 %pad_maximum_fusion = bf16[3,729,1152]{2,1,0:T(8,128)(2,1)} fusion(bf16[3,512,1152]{2,1,0:T(8,128)(2,1)} %bitcast.32, bf16[3,256,1152]{2,1,0:T(8,128)(2,1)} %bitcast.35), kind=kLoop, calls=%fused_computation.4 | loop fusion | flops 10077696 | bytes 10347264 | tf_op jit(solution)/shard_map/concatenate | solution.py:1162
  436.0 0.1 broadcast_in_dim.48
  436.0 0.1 mul.24
  436.1 1.4 dynamic-slice_reduce_fusion.1
  437.5 1.5 dynamic-slice_reduce_fusion
  439.0 1.6 slice_reduce_fusion
  440.6 0.0 copy-done.1
  440.6 0.0 copy-start.2
  440.6 0.1 fusion.6
  440.7 0.1 fusion.5
  440.8 0.0 copy-start.3
  440.8 0.0 copy-start.4
  440.8 0.9 maximum_bitcast_fusion
  441.7 0.0 copy-start
  441.7 0.9 pad_maximum_fusion.1
  442.6 0.0 copy-done.2
  442.6 1.1 slice_bitcast_fusion
  443.7 0.0 copy-done.3
  443.7 0.0 copy-done.4
  443.7 1.3 multiply_convert_fusion
  445.0 0.0 copy-done
  445.1 4.6 %slice_convert_fusion = f32[3,729,1152]{2,1,0:T(8,128)} fusion(bf16[3,768,1152]{2,1,0:T(8,128)(2,1)S(1)} %bitcast.31), kind=kLoop, calls=%fused_computation.3 | loop fusion | flops 2519424 | bytes 15116544 | tf_op jit(solution)/shard_map/convert_element_type | solution.py:1163
  (2 shorter events, 0.0 us)
Async XLA Ops:
  430.7 9.9 %copy-start.1 = (f32[144,2176]{1,0:T(8,128)S(1)}, f32[144,2176]{1,0:T(8,128)}, u32[]{:S(2)}) copy-start(f32[144,2176]{1,0:T(8,128)} %get-tuple-element.92) | copy-start | bytes 3760132
  440.6 2.0 copy-start.2
  440.8 2.9 copy-start.3
  440.8 2.9 copy-start.4
  441.7 3.3 copy-start

commit v6 on v5

--- a/solution.py
+++ b/solution.py
@@ -428,13 +428,17 @@
         self.start(chunk, stage)
 
 
-OUT_CHUNKS = ((256, 256), (512, 224))
+OUT_CHUNKS = ((0, 256), (256, 256), (512, 224))
 IN_CHUNKS = ((0, 128), (128, 128), (256, 128), (384, 128), (512, 128), (640, 96))
 MASKS = [(1, 0), (2, 0), (4, 0), (0, 1), (0, 2), (0, 3)]
 COPIES = 180
 
 
-def back_kernel(length, heads, gain1, gain2, live, geb, tops, gout, midway, sec, firstT, x, mine, whole0, h1, h2, h3, *rest):
+LATE = 2
+
+
+def back_kernel(length, heads, vectors, live, geb, tops, gout, midway, sec, firstT, x, mine, whole0, h1, h2, h3, O_low, *rest):
+    gain1, gain2 = vectors[0:1, :], vectors[2:3, :]
     Ws, qkvs, atts, lses, rest = rest[:4], rest[4:8], rest[8:12], rest[12:16], rest[16:]
     (O_out, O_in, sum_a, sum_m, vec, g_s, gm_s, acc, gT, fT, x_s, W_s, qkv_s, att_s, lse_s, ga_s, d_s, dk_s, dv_s, out_s,
      Ha, La, Hm, Lm, za, zm, vr, w0_s, w1_s, l_sem, s_sem, r_sem) = rest
@@ -468,12 +472,9 @@
         loads[key].start()
     slot = jnp.where(z == 0, 0, jnp.where(z == 3, 1, 2))
     own_place = pl.ds(pl.multiple_of(slot * TOK, 256), TOK)
-    out_rows = O_out.shape[0] // 3
-    out_base = TOK - out_rows
-    out_place = pl.ds(pl.multiple_of(slot * out_rows, 256), out_rows)
     used = (z == 0) | (z == 3) | (z == 1 + d % 2)
-    own_out, own_in = wires.local(mine.at[pl.ds(out_base, out_rows), :], O_out.at[out_place, :], used), wires.local(g_s, O_in.at[own_place, :], used)
-    share_out = Sharing(wires, mine, O_out, OUT_CHUNKS, out_base)
+    own_in = wires.local(g_s, O_in.at[own_place, :], used)
+    share_out = Sharing(wires, mine, O_out, OUT_CHUNKS)
     share_in = Sharing(wires, g_s, O_in, IN_CHUNKS)
     sums = {"m2": Summing(wires, Hm.at[0], Lm.at[0]), "m3": Summing(wires, Hm.at[1], Lm.at[1])}
     for k in range(4):
@@ -487,21 +488,20 @@
     greet(d, z, MASKS)
 
     todo = {
-        -3: [lambda: share_out.start(0, 0), own_out[0]],
+        -3: [lambda: share_out.start(0, 1), lambda: share_out.start(1, 1), lambda: share_out.start(2, 0)],
         -2: [lambda: loads["h2"].wait(), sums["m2"].step1, lambda: loads["w1"].wait(), lambda: line_m.alpha(1)],
         0: [lambda: loads["h3"].wait(), lambda: loads["w0"].wait()],
         5: [sums["m2"].step2, sums["m3"].step1],
-        8: [lambda: share_out.on(0, 1), lambda: share_out.start(1, 0)],
+        8: [lambda: share_out.on(0, 2), lambda: share_out.on(2, 1)],
         10: [sums["m2"].step3, lambda: line_m.alpha(2)],
         15: [sums["m3"].step2],
-        18: [lambda: share_out.on(0, 2), lambda: share_out.on(1, 1), sums["b3"].step2],
+        18: [lambda: share_out.on(1, 2), sums["b3"].step2],
         20: [sums["m3"].step3, lambda: line_m.alpha(3)],
         22: [sums["b3"].step3, lambda: line_b.alpha(3)],
         25: [line_m.beta],
-        28: [lambda: share_out.on(1, 2), sums["b2"].step2],
+        28: [lambda: share_out.on(2, 2), sums["b2"].step2],
         33: [sums["b2"].step3, lambda: line_b.alpha(2)],
-        35: [sums["b1"].step2],
-        38: [sums["b1"].step3, lambda: line_b.alpha(1), line_m.gamma],
+        38: [line_m.gamma],
     }
 
     def tick(t):
@@ -528,7 +528,7 @@
         normed, inverse = normalize(acc[rows, :])
         e = gm_s[rows, :]
         go = g_s[rows, :].astype(F32)
-        scaled = e * gain2[...]
+        scaled = e * gain2
         mean1 = jnp.mean(scaled, axis=-1, keepdims=True)
         mean2 = jnp.mean(scaled * normed, axis=-1, keepdims=True)
         gm = go + inverse * (scaled - mean1 - normed * mean2)
@@ -546,6 +546,12 @@
                 val = val + dst[where, lo:hi].astype(F32)
             dst[where, lo:hi] = val.astype(BF)
         return put
+
+    def give(i):
+        k, b = order[i], i % 2
+        block_rows(fT, d_s.at[b], 0, write(out_s, 0, 3 * cw, False))
+        block_rows(gT, att_s.at[b], 0, write(out_s, 3 * cw, 4 * cw, False))
+        exchange[k][0]()
 
     def keep(i):
         k, b = order[i], i % 2
@@ -572,7 +578,7 @@
             for h in range(heads):
                 ga_s[h, rows, :] = g[:, h * HD:(h + 1) * HD]
 
-        if i:
+        if 1 <= i <= LATE:
             keep(i - 1)
             sums[f"b{order[i - 1]}"].step1()
         if i < 3:
@@ -598,23 +604,22 @@
                 dd = jnp.sum(g.astype(F32) * att[rows, h * HD:(h + 1) * HD].astype(F32), axis=1, keepdims=True)
                 ds = (p * (dp - dd)).astype(BF)
                 dqs.append(nn(ds, kk) * SC)
-                dk_s[h] += tn(ds, q)
-                dv_s[h] += tn(p.astype(BF), g)
+                dk_s[h * HD:(h + 1) * HD, :] += tn(q, ds)
+                dv_s[h * HD:(h + 1) * HD, :] += tn(g, p.astype(BF))
             dq = jnp.concatenate(dqs, axis=1)
             put_row(place, 0, jnp.sum(dq, axis=0, keepdims=True))
             dd_s[rows, :cw] = dq.astype(BF)
 
-        dd_s[:, cw:2 * cw] = jnp.concatenate([dk_s[h] * SC for h in range(heads)], axis=1).astype(BF)
-        dv = jnp.concatenate([dv_s[h] for h in range(heads)], axis=1)
+        dd_s[:, cw:2 * cw] = (dk_s[...].T[:, :cw] * SC).astype(BF)
+        dv = dv_s[...].T[:, :cw]
         put_row(place, 384, jnp.sum(dv, axis=0, keepdims=True))
         dd_s[:, 2 * cw:] = dv.astype(BF)
         put_row(place, 768, geb[k])
         put_row(place, 1920, tops[k])
         tick(base + 5)
 
-        block_rows(fT, dd_s, 0, write(out_s, 0, 3 * cw, False))
-        block_rows(gT, att, 0, write(out_s, 3 * cw, 4 * cw, False))
-        exchange[k][0]()
+        if i < LATE:
+            give(i)
         tick(base + 6)
 
         @pl.loop(0, TOK // RT)
@@ -632,7 +637,7 @@
         rows = pl.ds(pl.multiple_of(i * RT, RT), RT)
         normed, inverse = normalize(x_s[rows, :].astype(F32))
         e = acc[rows, :]
-        scaled = e * gain1[...]
+        scaled = e * gain1
         mean1 = jnp.mean(scaled, axis=-1, keepdims=True)
         mean2 = jnp.mean(scaled * normed, axis=-1, keepdims=True)
         total_of(6, e * normed)
@@ -646,9 +651,15 @@
 
     own_in[0]()
     spread[0][0]()
-    keep(3)
-    sums["b0"].step1()
-    after = {0: [line_b.beta], 1: [sums["b0"].step2], 2: [sums["b0"].step3], 3: [line_b.gamma]}
+    give(2)
+    after = {
+        0: [line_b.beta, lambda: keep(2), sums["b1"].step1, lambda: give(3)],
+        1: [lambda: keep(3), sums["b0"].step1],
+        2: [sums["b1"].step2],
+        3: [sums["b1"].step3, lambda: line_b.alpha(1), sums["b0"].step2],
+        4: [sums["b0"].step3],
+        5: [line_b.gamma],
+    }
     row = lax.broadcasted_iota(jnp.int32, vec.shape, 1)
 
     def fold(i):
@@ -670,7 +681,6 @@
             fold(t - 1)
     for c in range(len(OUT_CHUNKS)):
         share_out.wait(c, 2)
-    own_out[1]()
     own_in[1]()
     sum_m[...] = line_m.total(w0_s[...].astype(F32))
     sum_a[...] = line_b.total(Ha[0, :r, :].astype(F32))
@@ -678,7 +688,7 @@
         share_in.wait(c, 2)
 
 
-def back(number, gain1, gain2, live, geb, tops, gout, midway, sec, firstT, x, mine, whole0, h1, h2, h3, qkvs, atts, lses, Ws, length):
+def back(number, vectors, live, geb, tops, gout, midway, sec, firstT, x, mine, whole0, h1, h2, h3, O_low, qkvs, atts, lses, Ws, length):
     D = gout.shape[1]
     cw = Ws[0].shape[0] // 4
     cm = h2.shape[1]
@@ -688,19 +698,20 @@
     dma = pltpu.SemaphoreType.DMA
     return pl.pallas_call(
         functools.partial(back_kernel, length, heads),
-        out_shape=(shape((3 * (TOK - OUT_CHUNKS[0][0]), D), BF), shape((3 * TOK, D), BF), shape((r, 4 * cw), F32), shape((r, cm), F32), shape((16, 2048), F32)),
-        in_specs=[VM] * 5 + [HB] * 26,
+        out_shape=(shape((3 * TOK, D), BF), shape((3 * TOK, D), BF), shape((r, 4 * cw), F32), shape((r, cm), F32), shape((16, 2048), F32)),
+        in_specs=[VM] * 4 + [HB] * 27,
         out_specs=(HB, HB, VM, VM, VM),
+        input_output_aliases={14: 0},
         scratch_shapes=[vm((TOK, D), BF), vm((TOK, D), F32), vm((TOK, D), F32), vm((D, TOK), BF), vm((D, TOK), BF), vm((TOK, D), BF),
                         vm((2, 4 * cw, D), BF), vm((2, 3 * heads, TOK, HD), BF), vm((2, TOK, cw), BF), vm((2, TOK, 128), F32),
-                        vm((heads, TOK, HD), BF), vm((2, TOK, 3 * cw), BF), vm((heads, TOK, HD), F32), vm((heads, TOK, HD), F32), vm((4 * r, 4 * cw), BF),
+                        vm((heads, TOK, HD), BF), vm((2, TOK, 3 * cw), BF), vm((-(-cw // 128) * 128, TOK), F32), vm((-(-cw // 128) * 128, TOK), F32), vm((4 * r, 4 * cw), BF),
                         vm((4, 4 * r, 4 * cw), BF), vm((4, 3 * r, 4 * cw), BF), vm((2, 4 * r, cm), BF), vm((2, 3 * r, cm), BF),
                         vm((5, r, 4 * cw), BF), vm((5, r, cm), BF), vm((5, 16, 2048), F32), vm((r, cm), BF), vm((r, cm), BF),
                         dma((32,)), dma((COPIES,)), dma((COPIES,))],
         compiler_params=pltpu.CompilerParams(vmem_limit_bytes=63 * 2**20, collective_id=number, has_side_effects=True),
         cost_estimate=pl.CostEstimate(flops=4 * 2 * TOK * (D * cw * 8 + heads * 5 * TOK * HD * 6), bytes_accessed=60 * 2**20, transcendentals=4 * heads * TOK * TOK),
         name="back",
-    )(gain1, gain2, live, geb, tops, gout, midway, sec, firstT, x, mine, whole0, h1, h2, h3, *Ws, *qkvs, *atts, *lses)
+    )(vectors, live, geb, tops, gout, midway, sec, firstT, x, mine, whole0, h1, h2, h3, O_low, *Ws, *qkvs, *atts, *lses)
 
 
 class Spreading:
@@ -759,9 +770,9 @@
             self.made[k].wait()
 
 
-def front_kernel(length, heads, gain1, shift1, gain2, shift2, out_b, bias_own, x, qw, kw, vw, ow, mw, *rest):
-    (qkv0, qkv1, qkv2, qkv3, att0, att1, att2, att3, lse0, lse1, lse2, lse3, firstT, second, secondT, midway, Wa0, Wa1, Wa2, Wa3, Wm1, Zm2,
-     tops, bias_all, x_s, first_s, T_s, second_s, acc, W, Za, Zm1, qkv_s, att_s, lse_s, bias, l_sem, s_sem, r_sem) = rest
+def front_kernel(length, heads, vectors, live, bias_own, x, cot, qw, kw, vw, ow, mw, *rest):
+    (qkv0, qkv1, qkv2, qkv3, att0, att1, att2, att3, lse0, lse1, lse2, lse3, firstT, second, secondT, midway, Wa0, Wa1, Wa2, Wa3, Wm1, Zm2, gout, goutT,
+     tops, bias_all, gout_s, goutT_s, x_s, first_s, T_s, second_s, acc, W, Za, Zm1, qkv_s, att_s, lse_s, bias, l_sem, s_sem, r_sem) = rest
     cw = heads * HD
     D = x_s.shape[1]
     wires, moves = Wires(s_sem, r_sem), Moves(l_sem)
@@ -774,6 +785,10 @@
     for i, ref in enumerate((qw, kw, vw, ow)):
         moves.add(f"w{i}", ref, W.at[0, pl.ds(i * cw, cw), :])
     moves.add("x", x, x_s)
+    moves.add("cot", cot, gout_s)
+    moves.add("gout", gout_s, gout)
+    moves.add("goutT", goutT_s, goutT)
+    gain1, shift1, gain2, shift2, out_b = [vectors[n:n + 1, :] for n in range(5)]
     moves.add("oW0", W.at[0], Wa0)
     for k, (a, b, c) in enumerate(((qkv0, att0, lse0), (qkv1, att1, lse1), (qkv2, att2, lse2), (qkv3, att3, lse3))):
         moves.add(f"qkv{k}", qkv_s.at[k], a)
@@ -785,7 +800,7 @@
     moves.add("second", second_s, second)
     moves.add("secondT", T_s, secondT)
     moves.add("midway", acc, midway)
-    moves.start("w0", "w1", "w2", "w3", "x")
+    moves.start("w0", "w1", "w2", "w3", "x", "cot")
 
     zb = [wires.swap(bias.at[0], bias.at[k], z=k) for k in (1, 2, 3)]
     a_piece, m_piece = W.at[0, own_rows(W.at[0]), :], mw.at[own_rows(mw), :]
@@ -808,16 +823,28 @@
         part = pl.ds(pl.multiple_of(i * RT, RT), RT)
         xt = x_s[part, :].astype(F32)
         normed, _ = normalize(xt)
-        f = normed * gain1[...] + shift1[...]
+        f = normed * gain1 + shift1
         first_s[part, :] = f.astype(BF)
         T_s[:, part] = f.T.astype(BF)
-        acc[part, :] = xt + out_b[...]
+        acc[part, :] = xt + out_b
 
     moves.start("firstT")
     for _, w in zb:
         w()
     bias_all[...] = bias[...]
 
+    def turn_gout():
+        moves.wait("cot")
+
+        @pl.loop(0, TOK // RT)
+        def _(i):
+            part = pl.ds(pl.multiple_of(i * RT, RT), RT)
+            g = gout_s[part, :].astype(F32) * live[...]
+            gout_s[part, :] = g.astype(BF)
+            goutT_s[:, part] = g.T.astype(BF)
+
+        moves.start("gout", "goutT")
+
     def z_a3():
         za[1][1]()
         za[2][0]()
@@ -825,13 +852,14 @@
     todo = {
         0: [zm[0][0]],
         1: [za[0][1], ga[1].step0],
-        5: [z_a3, ga[2].step0, ga[1].step1, ga[1].step2],
+        5: [z_a3, ga[2].step0, turn_gout, ga[1].step1, ga[1].step2],
         10: [za[2][1], ga[3].step0],
         11: [zm[1][0]],
         13: [ga[2].step1],
         15: [ga[2].step2],
         20: [ga[3].step1, zm[0][1], gm.step0],
         23: [ga[3].step2],
+        30: [],
     }
 
     def tick(t):
@@ -895,7 +923,7 @@
     def _(i):
         part = pl.ds(pl.multiple_of(i * RT, RT), RT)
         normed, _ = normalize(acc[part, :])
-        f = normed * gain2[...] + shift2[...]
+        f = normed * gain2 + shift2
         second_s[part, :] = f.astype(BF)
         T_s[:, part] = f.T.astype(BF)
 
@@ -904,10 +932,10 @@
     zm[1][1]()
     for k in range(4):
         moves.wait(f"qkv{k}", f"att{k}", f"lse{k}", f"oW{k}")
-    moves.wait("second", "secondT", "midway")
-
-
-def front(number, gain1, shift1, gain2, shift2, out_b, bias_own, x, qw, kw, vw, ow, mw, length):
+    moves.wait("second", "secondT", "midway", "gout", "goutT")
+
+
+def front(number, vectors, live, bias_own, x, cot, qw, kw, vw, ow, mw, length):
     cw, D = qw.shape
     heads = cw // HD
     cm = mw.shape[0]
@@ -918,20 +946,20 @@
         functools.partial(front_kernel, length, heads),
         out_shape=(*four(shape((3 * heads, TOK, HD), BF)), *four(shape((TOK, cw), BF)), *four(shape((TOK, 128), F32)),
                    shape((D, TOK), BF), shape((TOK, D), BF), shape((D, TOK), BF), shape((TOK, D), F32), *four(shape((4 * cw, D), BF)),
-                   shape((cm, D), BF), shape((cm // 8, D), BF), shape((4, heads, 128), F32), shape((4, 8, 2048), F32)),
-        in_specs=[VM] * 6 + [HB] * 6,
-        out_specs=(HB,) * 22 + (VM,) * 2,
-        scratch_shapes=[vm((TOK, D), BF), vm((TOK, D), BF), vm((D, TOK), BF), vm((TOK, D), BF), vm((TOK, D), F32),
+                   shape((cm, D), BF), shape((cm // 8, D), BF), shape((TOK, D), BF), shape((D, TOK), BF), shape((4, heads, 128), F32), shape((4, 8, 2048), F32)),
+        in_specs=[VM] * 3 + [HB] * 7,
+        out_specs=(HB,) * 24 + (VM,) * 2,
+        scratch_shapes=[vm((TOK, D), BF), vm((D, TOK), BF), vm((TOK, D), BF), vm((TOK, D), BF), vm((D, TOK), BF), vm((TOK, D), BF), vm((TOK, D), F32),
                         vm((4, 4 * cw, D), BF), vm((3, cw // 2, D), BF), vm((cm // 8, D), BF), vm((4, 3 * heads, TOK, HD), BF),
                         vm((4, TOK, cw), BF), vm((4, TOK, 128), F32), vm((4, 8, 2048), F32), dma((32,)), dma((64,)), dma((64,))],
         compiler_params=pltpu.CompilerParams(vmem_limit_bytes=62 * 2**20, collective_id=number, has_side_effects=True),
         cost_estimate=pl.CostEstimate(flops=4 * 2 * TOK * (D * cw * 4 + heads * 2 * TOK * HD * 6), bytes_accessed=60 * 2**20, transcendentals=4 * heads * TOK * TOK),
         name="front",
-    )(gain1, shift1, gain2, shift2, out_b, bias_own, x, qw, kw, vw, ow, mw)
-    return got[:4], got[4:8], got[8:12], got[12:16], got[16:20], got[20:22], got[22], got[23]
-
-
-def middle_kernel(fw, live, shrink_b, bias_all, second, secondT, gout, goutT, midway, Wm0, Wm1, Zm2, *rest):
+    )(vectors, live, bias_own, x, cot, qw, kw, vw, ow, mw)
+    return got[:4], got[4:8], got[8:12], got[12:16], got[16:20], got[20:22], got[22:24], got[24], got[25]
+
+
+def middle_kernel(fw, live, vectors, bias_all, second, secondT, gout, goutT, midway, Wm0, Wm1, Zm2, *rest):
     (mine, sec, O0, H1, H2, H3, geb, part_sum, Wg2, Wg3, Zm3, Wg1, second_s, secondT_s, gout_s, goutT_s, mlp, sec_s, mine_s, W, act_s, slope_s, gpre_s, out_s,
      Hm, Lm, l_sem, s_sem, r_sem) = rest
     D = second_s.shape[1]
@@ -953,9 +981,8 @@
     moves.add("h3", Hm.at[3], H3)
     slot = jnp.where(z == 0, 0, jnp.where(z == 3, 1, 2))
     used = (z == 0) | (z == 3) | (z == 1 + d % 2)
-    n0 = O0.shape[0] // 3
-    own_out = wires.local(mine_s.at[pl.ds(0, n0), :], O0.at[pl.ds(pl.multiple_of(slot * n0, 256), n0), :], used)
-    share = Sharing(wires, mine_s, O0, ((0, n0),))
+    own_out = wires.local(mine_s, O0.at[pl.ds(pl.multiple_of(slot * TOK, 256), TOK), :], used)
+    share = Sharing(wires, mine_s, O0, OUT_CHUNKS)
     z3 = wires.swap(Zm2, Zm3, z=1)
     g1, g2, g3 = Spreading(wires, Zm2, Wg1), Spreading(wires, Zm2, Wg2), Spreading(wires, Zm3, Wg3)
     exchange = [wires.swap(out_s.at[k % 2], Hm.at[k], dp=1) for k in range(4)]
@@ -1051,14 +1078,15 @@
     @pl.loop(0, TOK // RT)
     def _(i):
         rows = pl.ds(pl.multiple_of(i * RT, RT), RT)
-        mine_s[rows, :] = ((mlp[rows, :] + shrink_b[...]) * live[...]).astype(BF)
+        mine_s[rows, :] = ((mlp[rows, :] + vectors[5:6, :]) * live[...]).astype(BF)
         pl.when(i == 0)(lambda: share.start(0, 0))
+        pl.when(i == 1)(lambda: share.start(1, 0))
 
     own_out[0]()
     moves.start("mine")
     sums[1].step1()
-    back_a(2, ticks({4: [lambda: share.on(0, 1), sums[0].step2]}))
-    back_a(3, ticks({4: [sums[0].step3, lambda: share.on(0, 2)]}))
+    back_a(2, ticks({4: [sums[0].step2]}))
+    back_a(3, ticks({4: [sums[0].step3]}))
     sums[1].step2()
     moves.start("sec")
     back_b(2)
@@ -1068,22 +1096,22 @@
     sums[1].step3()
     moves.start("h1")
     part_sum[...] = Hm[0, :r, :]
-    share.wait(0, 2)
+    share.wait(0, 0)
+    share.wait(1, 0)
     own_out[1]()
     moves.wait("h1", "h2", "h3", "sec", "mine")
 
 
-def middle(number, fw, live, shrink_b, bias_all, second, secondT, gout, goutT, midway, Wm0, Wm1, Zm2):
+def middle(number, fw, live, vectors, bias_all, second, secondT, gout, goutT, midway, Wm0, Wm1, Zm2):
     D = second.shape[1]
     cm, hid = Wm0.shape[0], Wm0.shape[0] // 2
     cg = fw // 128 * 256 + 128
     r = D // 8
-    n0 = OUT_CHUNKS[0][0]
     vm = pltpu.VMEM
     dma = pltpu.SemaphoreType.DMA
     got = pl.pallas_call(
         functools.partial(middle_kernel, fw),
-        out_shape=(shape((TOK, D), BF), shape((TOK, D), F32), shape((3 * n0, D), BF), shape((r, cg), BF), shape((4 * r, cg), BF), shape((4 * r, cg), BF), shape((4, 1, hid), F32), shape((r, cg), BF),
+        out_shape=(shape((TOK, D), BF), shape((TOK, D), F32), shape((3 * TOK, D), BF), shape((r, cg), BF), shape((4 * r, cg), BF), shape((4 * r, cg), BF), shape((4, 1, hid), F32), shape((r, cg), BF),
                    shape((cm, D), BF), shape((cm, D), BF), shape((cm // 8, D), BF), shape((cm, D), BF)),
         in_specs=[VM] * 3 + [HB] * 8,
         out_specs=(HB,) * 6 + (VM,) * 2 + (HB,) * 4,
@@ -1094,7 +1122,7 @@
         compiler_params=pltpu.CompilerParams(vmem_limit_bytes=63 * 2**20, collective_id=number, has_side_effects=True),
         cost_estimate=pl.CostEstimate(flops=4 * 2 * 9 * TOK * D * fw, bytes_accessed=60 * 2**20, transcendentals=4 * TOK * fw),
         name="middle",
-    )(live, shrink_b, bias_all, second, secondT, gout, goutT, midway, Wm0, Wm1, Zm2)
+    )(live, vectors, bias_all, second, secondT, gout, goutT, midway, Wm0, Wm1, Zm2)
     return got[:8]
 
 
@@ -1144,27 +1172,27 @@
     pad = lambda a: jnp.pad(a, ((0, TOK - length), (0, 0)))
 
     x_low = pad(lax.dynamic_index_in_dim(images, slot, 0, keepdims=False))
-    gout = pad(lax.dynamic_index_in_dim(cotangent, slot, 0, keepdims=False)) * live.astype(BF)
-    gout_t = gout.T
+    cot_low = pad(lax.dynamic_index_in_dim(cotangent, slot, 0, keepdims=False))
     if (groups, lax.axis_size("dp")) == (4, 8):
-        one = lambda a: a[None]
         blank = lambda n: jnp.zeros((n,), F32)
         bias_own = jnp.concatenate([query_b, blank(384 - cw), value_b, blank(384 - cw), expand_b, blank(1280 - fw)])
         deep = -fw % 16
         mlp_own = jnp.pad(jnp.stack([expand_w.T, shrink_w]), ((0, 0), (0, deep), (0, 0))).reshape(2 * (fw + deep), width)
-        qkvs, atts, lses, (first_t, second, second_t, midway), attn_ws, mlp_ws, tops, bias_all = front(
-            0, one(norm1_gain), one(norm1_shift), one(norm2_gain), one(norm2_shift), one(out_b), jnp.broadcast_to(bias_own, (8, 2048)),
-            x_low, query_w.T, key_w.T, value_w.T, out_w, mlp_own, length)
-        mine, sec, out_low, h1, h2, h3, geb, part_sum = middle(1, fw, live[None, None], one(shrink_b), bias_all, second, second_t, gout, gout_t, midway, mlp_own, *mlp_ws)
-        out_high, in_all, sum_attn, sum_mlp, vec = back(
-            2, one(norm1_gain), one(norm2_gain), live[None, None], geb, jnp.where(live > 0.0, tops[:, :, 0], -1e30)[:, None],
-            gout, midway, sec, first_t, x_low, mine, part_sum, h1, h2, h3, qkvs, atts, lses, attn_ws, length)
-        outputs = jnp.concatenate([out_low.reshape(3, -1, width), out_high.reshape(3, -1, width)], axis=1)[:, :length]
+        vectors = jnp.stack([norm1_gain, norm1_shift, norm2_gain, norm2_shift, out_b, shrink_b, shrink_b, shrink_b])
+        qkvs, atts, lses, (first_t, second, second_t, midway), attn_ws, mlp_ws, (gout, gout_t), tops, bias_all = front(
+            0, vectors, live[None, None], jnp.broadcast_to(bias_own, (8, 2048)), x_low, cot_low, query_w.T, key_w.T, value_w.T, out_w, mlp_own, length)
+        mine, sec, out_low, h1, h2, h3, geb, part_sum = middle(1, fw, live[None, None], vectors, bias_all, second, second_t, gout, gout_t, midway, mlp_own, *mlp_ws)
+        out_all, in_all, sum_attn, sum_mlp, vec = back(
+            2, vectors, live[None, None], geb, jnp.where(live > 0.0, tops[:, :, 0], -1e30)[:, None],
+            gout, midway, sec, first_t, x_low, mine, part_sum, h1, h2, h3, out_low, qkvs, atts, lses, attn_ws, length)
+        outputs = out_all.reshape(3, TOK, width)[:, :length]
         input_grads = in_all.reshape(3, TOK, width)[:, :length].astype(F32)
         own = lax.dynamic_index_in_dim(vec, z, 0, keepdims=False)
         grad_query_b, grad_value_b, grad_expand_b, logit_top = own[:cw], own[384:384 + cw], own[768:768 + fw], own[1920:1920 + heads]
         tail = [vec[4 + i, :width] for i in range(6)]
     else:
+        gout = cot_low * live.astype(BF)
+        gout_t = gout.T
         attn_own = jnp.concatenate([query_w, key_w, value_w, out_w.T], axis=1)
         shrink_t = shrink_w.T
         mlp_own = jnp.concatenate([expand_w[:, :cut], shrink_t[:, :cut], expand_w[:, cut:], shrink_t[:, cut:]], axis=1)

time: 455 us -> 446 us (0.980)
  other arithmetic: 21.9 us -> 12.6 us
    broadcast_in_dim x6 -> x0, local copies, waits for them, and re-layouts: 7.75 us -> none  [shards(): one = lambda a: a[None]]
    concatenate x1 -> x0, other arithmetic: 5.28 us -> none  [shards(): jnp.concatenate([out_low.reshape(3, -1, width), out_high.reshape(3, -1, w...]
    slice x0 -> x1, local copies, waits for them, and re-layouts: none -> 5.25 us  [shards(): outputs = out_all.reshape(3, TOK, width)[:, :length]]
    another operation x1 -> x8, local copies, waits for them, and re-layouts: 0.01 us -> 4.88 us  [the longest x7 4.87 us: shards(): jnp.stack([norm1_gain, norm1_shift, norm2_gain, norm2_shift, out_b, shrin...]
where the time goes in v6:
time: 446 us; the launch traced here: 441 us
  Pallas kernels  403 us (90%)
  local copies, waits for them, and re-layouts  23.5 us (5%)
  other arithmetic  12.6 us (3%)
    pallas_call x1, Pallas kernels, back(): pl.pallas_call(functools.partial(back_kernel, length, heads), out_shape=(...  205 us
    pallas_call x1, Pallas kernels, middle(): pl.pallas_call(functools.partial(middle_kernel, fw), out_shape=(shape((TO...  110 us
    pallas_call x1, Pallas kernels, front(): pl.pallas_call(functools.partial(front_kernel, length, heads), out_shape=...  87.5 us

profile of v6, /device:TPU:1, one launch (start us, length us, event | category | flops | bytes accessed | tf_op | source)
XLA Modules:
  0.0 440.9 jit_solution(11607034950520653292)
XLA Ops:
  1.3 0.7 stack.36
  2.0 0.7 stack.32
  2.7 0.7 stack.33
  3.4 0.7 stack.34
  4.1 0.7 stack.35
  4.8 0.7 stack.37
  5.5 0.8 concatenate.9
  6.4 0.7 stack.38.vectors
  7.0 0.6 broadcast_in_dim.21.bias_own
  7.7 2.2 dynamic-slice_bitcast_fusion
  9.9 0.0 copy-start.1
  9.9 0.0 copy-start.2
  9.9 1.4 pad.12.cot
  11.3 1.3 pad.11.x
  12.6 0.0 copy-done.1
  12.6 1.0 copy-done.2
  13.6 2.7 fusion.2
  16.3 87.5 %front.1 = (bf16[12,768,72]{2,1,0:T(8,128)(2,1)}, bf16[12,768,72]{2,1,0:T(8,128)(2,1)}, bf16[12,768,72]{2,1,0:T(8,128)(2,1)}, bf16[12,768,72]{2,1,0:T(8,128)(2,1...) custom-call(f32[8,1152]{1,0:T(8,128)} %stack.38.vectors, ...), custom_call_target="tpu_custom_call" | custom-call | flops 24461180928 | bytes 62914560 | tf_op jit(solution)/shard_map/front/pallas_call | solution.py:945
  103.8 1.4 select_reduce_fusion
  105.2 110.5 %middle.1 = (bf16[768,1152]{1,0:T(8,128)(2,1)}, f32[768,1152]{1,0:T(8,128)}, bf16[2304,1152]{1,0:T(8,128)(2,1)}, bf16[144,2176]{1,0:T(8,128)(2,1)}, bf16[576,217...) custom-call(f32[1,1]{1,0:T(1,128)} %bitcast.1.live, ...), custom_call_target="tpu_custom_call", output_to_operand_aliasing={{11}: (9, {})} | custom-call | flops 68542267392 | bytes 62914560 | tf_op jit(solution)/shard_map/middle/pallas_call | solution.py:1112
  215.6 205.3 %back.1 = (bf16[2304,1152]{1,0:T(8,128)(2,1)}, bf16[2304,1152]{1,0:T(8,128)(2,1)}, f32[144,1152]{1,0:T(8,128)}, f32[144,2176]{1,0:T(8,128)}, f32[16,2048]{1,0:T(8,128)}) custom-call(f32[8,1152]{1,0:T(8,128)} %stack.38.vectors, f32[1,1]{1,0:T(1,128)} %bitcast.1.live, f32[4,1,1088]{2,1,0:T(1,128)} %get-tuple-element.66.geb, ...), custom_call_target="tpu_custom_call", output_to_operand_aliasing={{0}: (14, {})} | custom-call | flops 57076088832 | bytes 62914560 | tf_op jit(solution)/shard_map/back/pallas_call | solution.py:699
  420.9 0.8 sqrt_bitcast_fusion
  421.7 0.0 copy-start.3
  421.7 5.2 %slice.101 = bf16[3,729,1152]{2,1,0:T(8,128)(2,1)} slice(bf16[3,768,1152]{2,1,0:T(8,128)(2,1)} %bitcast.28), slice={[0:3], [0:729], [0:1152]} | slice | bytes 10077696 | tf_op jit(solution)/shard_map/slice | solution.py:1188
  426.9 0.1 broadcast_in_dim.23
  427.0 0.1 mul.16
  427.1 1.4 dynamic-slice_reduce_fusion.1
  428.5 1.5 dynamic-slice_reduce_fusion
  430.0 1.6 slice_reduce_fusion
  431.6 0.0 copy-done.3
  431.6 0.0 copy-start.4
  431.6 0.1 fusion.5
  431.7 0.1 fusion.4
  431.8 0.0 copy-start.5
  431.8 0.0 copy-start.6
  431.8 0.9 maximum_bitcast_fusion
  432.7 0.0 copy-start
  432.7 0.9 pad_maximum_fusion
  433.6 0.0 copy-done.4
  433.6 1.1 slice_bitcast_fusion
  434.7 0.0 copy-done.5
  434.7 0.0 copy-done.6
  434.7 1.3 multiply_convert_fusion
  436.1 0.0 copy-done
  436.1 4.6 %slice_convert_fusion = f32[3,729,1152]{2,1,0:T(8,128)} fusion(bf16[3,768,1152]{2,1,0:T(8,128)(2,1)S(1)} %bitcast.29), kind=kLoop, calls=%fused_computation.3 | loop fusion | flops 2519424 | bytes 15116544 | tf_op jit(solution)/shard_map/convert_element_type | solution.py:1189
  (2 shorter events, 0.0 us)
Async XLA Ops:
  9.9 2.7 copy-start.1
  9.9 3.7 copy-start.2
  421.7 9.9 %copy-start.3 = (f32[144,2176]{1,0:T(8,128)S(1)}, f32[144,2176]{1,0:T(8,128)}, u32[]{:S(2)}) copy-start(f32[144,2176]{1,0:T(8,128)} %get-tuple-element.96) | copy-start | bytes 3760132
  431.6 2.0 copy-start.4
  431.8 2.9 copy-start.5
  431.8 2.9 copy-start.6
  432.7 3.3 copy-start

commit v7 on v6

--- a/solution.py
+++ b/solution.py
@@ -854,9 +854,9 @@
         1: [za[0][1], ga[1].step0],
         5: [z_a3, ga[2].step0, turn_gout, ga[1].step1, ga[1].step2],
         10: [za[2][1], ga[3].step0],
-        11: [zm[1][0]],
+        11: [],
         13: [ga[2].step1],
-        15: [ga[2].step2],
+        15: [ga[2].step2, zm[1][0]],
         20: [ga[3].step1, zm[0][1], gm.step0],
         23: [ga[3].step2],
         30: [],
@@ -1085,12 +1085,14 @@
     own_out[0]()
     moves.start("mine")
     sums[1].step1()
-    back_a(2, ticks({4: [sums[0].step2]}))
-    back_a(3, ticks({4: [sums[0].step3]}))
-    sums[1].step2()
+    back_a(2, none)
+    sums[0].step2()
+    back_a(3, none)
     moves.start("sec")
     back_b(2)
     moves.start("h2")
+    sums[0].step3()
+    sums[1].step2()
     back_b(3)
     moves.start("h3")
     sums[1].step3()

time: 446 us -> 443 us (level)
  no operation moved by 1% of the time
where the time goes in v7:
time: 443 us; the launch traced here: 438 us
  Pallas kernels  400 us (90%)
  local copies, waits for them, and re-layouts  23.5 us (5%)
  other arithmetic  12.6 us (3%)
    pallas_call x1, Pallas kernels, back(): pl.pallas_call(functools.partial(back_kernel, length, heads), out_shape=(...  206 us
    pallas_call x1, Pallas kernels, middle(): pl.pallas_call(functools.partial(middle_kernel, fw), out_shape=(shape((TO...  107 us
    pallas_call x1, Pallas kernels, front(): pl.pallas_call(functools.partial(front_kernel, length, heads), out_shape=...  87.5 us

profile of v7, /device:TPU:1, one launch (start us, length us, event | category | flops | bytes accessed | tf_op | source)
XLA Modules:
  0.0 438.1 jit_solution(10138930077080210100)
XLA Ops:
  1.3 0.7 stack.36
  2.0 0.7 stack.32
  2.7 0.7 stack.33
  3.4 0.7 stack.34
  4.1 0.7 stack.35
  4.8 0.7 stack.37
  5.5 0.8 concatenate.9
  6.4 0.7 stack.38.vectors
  7.0 0.6 broadcast_in_dim.21.bias_own
  7.7 2.2 dynamic-slice_bitcast_fusion
  9.9 0.0 copy-start.1
  9.9 0.0 copy-start.2
  9.9 1.4 pad.12.cot
  11.3 1.3 pad.11.x
  12.6 0.0 copy-done.1
  12.6 1.0 copy-done.2
  13.6 2.7 fusion.2
  16.3 87.5 %front.1 = (bf16[12,768,72]{2,1,0:T(8,128)(2,1)}, bf16[12,768,72]{2,1,0:T(8,128)(2,1)}, bf16[12,768,72]{2,1,0:T(8,128)(2,1)}, bf16[12,768,72]{2,1,0:T(8,128)(2,1...) custom-call(f32[8,1152]{1,0:T(8,128)} %stack.38.vectors, ...), custom_call_target="tpu_custom_call" | custom-call | flops 24461180928 | bytes 62914560 | tf_op jit(solution)/shard_map/front/pallas_call | solution.py:945
  103.8 1.4 select_reduce_fusion
  105.2 106.9 %middle.1 = (bf16[768,1152]{1,0:T(8,128)(2,1)}, f32[768,1152]{1,0:T(8,128)}, bf16[2304,1152]{1,0:T(8,128)(2,1)}, bf16[144,2176]{1,0:T(8,128)(2,1)}, bf16[576,217...) custom-call(f32[1,1]{1,0:T(1,128)} %bitcast.1.live, ...), custom_call_target="tpu_custom_call", output_to_operand_aliasing={{11}: (9, {})} | custom-call | flops 68542267392 | bytes 62914560 | tf_op jit(solution)/shard_map/middle/pallas_call | solution.py:1114
  212.0 206.1 %back.1 = (bf16[2304,1152]{1,0:T(8,128)(2,1)}, bf16[2304,1152]{1,0:T(8,128)(2,1)}, f32[144,1152]{1,0:T(8,128)}, f32[144,2176]{1,0:T(8,128)}, f32[16,2048]{1,0:T(8,128)}) custom-call(f32[8,1152]{1,0:T(8,128)} %stack.38.vectors, f32[1,1]{1,0:T(1,128)} %bitcast.1.live, f32[4,1,1088]{2,1,0:T(1,128)} %get-tuple-element.66.geb, ...), custom_call_target="tpu_custom_call", output_to_operand_aliasing={{0}: (14, {})} | custom-call | flops 57076088832 | bytes 62914560 | tf_op jit(solution)/shard_map/back/pallas_call | solution.py:699
  418.2 0.8 sqrt_bitcast_fusion
  418.9 0.0 copy-start.3
  418.9 5.2 %slice.101 = bf16[3,729,1152]{2,1,0:T(8,128)(2,1)} slice(bf16[3,768,1152]{2,1,0:T(8,128)(2,1)} %bitcast.28), slice={[0:3], [0:729], [0:1152]} | slice | bytes 10077696 | tf_op jit(solution)/shard_map/slice | solution.py:1190
  424.2 0.1 broadcast_in_dim.23
  424.3 0.1 mul.16
  424.3 1.4 dynamic-slice_reduce_fusion.1
  425.7 1.5 dynamic-slice_reduce_fusion
  427.2 1.6 slice_reduce_fusion
  428.8 0.0 copy-done.3
  428.8 0.0 copy-start.4
  428.8 0.1 fusion.5
  428.9 0.1 fusion.4
  429.1 0.0 copy-start.5
  429.1 0.0 copy-start.6
  429.1 0.9 maximum_bitcast_fusion
  430.0 0.0 copy-start
  430.0 0.9 pad_maximum_fusion
  430.9 0.0 copy-done.4
  430.9 1.1 slice_bitcast_fusion
  431.9 0.0 copy-done.5
  431.9 0.0 copy-done.6
  431.9 1.3 multiply_convert_fusion
  433.3 0.0 copy-done
  433.3 4.6 %slice_convert_fusion = f32[3,729,1152]{2,1,0:T(8,128)} fusion(bf16[3,768,1152]{2,1,0:T(8,128)(2,1)S(1)} %bitcast.29), kind=kLoop, calls=%fused_computation.3 | loop fusion | flops 2519424 | bytes 15116544 | tf_op jit(solution)/shard_map/convert_element_type | solution.py:1191
  (2 shorter events, 0.0 us)
Async XLA Ops:
  9.9 2.7 copy-start.1
  9.9 3.7 copy-start.2
  418.9 9.9 %copy-start.3 = (f32[144,2176]{1,0:T(8,128)S(1)}, f32[144,2176]{1,0:T(8,128)}, u32[]{:S(2)}) copy-start(f32[144,2176]{1,0:T(8,128)} %get-tuple-element.96) | copy-start | bytes 3760132
  428.8 2.0 copy-start.4
  429.1 2.9 copy-start.5
  429.1 2.9 copy-start.6
  430.0 3.3 copy-start
